TPU v7x, 32 devices: a whole 2x2x4 slice. The times are simulated.
32 devices in a mesh: dp: 4 (over z), slab: 4 (over x, core), chan: 2 (over y).
Axes of the slice: x: 2, y: 2, z: 4, core: 2. Of those that a mesh axis runs over, the one named last changes fastest.
Arguments:
- volumes: bfloat16 [4, 8, 32, 16, 256], P('dp', 'slab', None, None, 'chan'), may hold values from -6 to 6
- weight: bfloat16 [3, 3, 3, 256, 256], P(None, None, None, 'chan'), may hold values from -0.078125 to 0.078125
- bias: bfloat16 [256], P('chan'), may hold values from -3 to 3
- cotangent: bfloat16 [4, 8, 32, 16, 256], P('dp', 'slab', None, None, 'chan'), may hold values from -6 to 6
Outputs:
- activations: bfloat16 [4, 8, 32, 16, 256], P('dp', 'slab', None, None, 'chan')
- input_grad: bfloat16 [4, 8, 32, 16, 256], P('dp', 'slab', None, None, 'chan')
- weight_grad: float32 [3, 3, 3, 256, 256], P(None, None, None, 'chan')
- bias_grad: float32 [256], P('chan')
All inputs are finite; a program needn't handle non-finite values.
Results may differ from a plain program's by a relative error of at most 0.0049.
Values may be sent and summed in bfloat16 or wider, within the bound.
No kernel may reach another device: no remote copies, remote signals or barrier semaphores. Data moves between devices by JAX's collectives and lax.ppermute only.
A program may use at most 64 MiB of HBM per device.

v0:
```python
import jax
import jax.numpy as jnp
from jax import lax
from jax.sharding import PartitionSpec as P


def with_halo(value, sides, width):
    for axis, dim in sides:
        count, length = (lax.axis_size(axis), value.shape[dim])
        up = [(i, (i + 1) % count) for i in range(count - 1)]
        down = [(j, i) for i, j in up]
        last = lax.slice_in_dim(value, length - width, length, axis=dim)
        first = lax.slice_in_dim(value, 0, width, axis=dim)
        before = lax.ppermute(last, axis, up)
        after = lax.ppermute(first, axis, down)
        value = jnp.concatenate([before, value, after], axis=dim)
    return value


def plane_patches(field, depth, flipped, planes, rows_x, rows_y):
    pieces = []
    for shift_x in range(3):
        for shift_y in range(3):
            start_x = 2 - shift_x if flipped else shift_x
            start_y = 2 - shift_y if flipped else shift_y
            pieces.append(
                field[
                    :,
                    depth : depth + planes,
                    start_x : start_x + rows_x,
                    start_y : start_y + rows_y,
                    :,
                ]
            )
    block = jnp.concatenate(pieces, axis=4)
    return block.reshape(-1, block.shape[4])


def pad_sides(field):
    return jnp.pad(field, ((0, 0), (0, 0), (1, 1), (1, 1), (0, 0)))


def per_device(volumes, weight, bias, cotangent):
    samples, planes, rows_x, rows_y, local_in = volumes.shape
    outputs = weight.shape[4]
    local_out = bias.shape[0]
    cells = samples * planes * rows_x * rows_y
    with_planes = with_halo(volumes, (("slab", 1),), 1)
    padded = pad_sides(with_planes)
    partial_value = jnp.zeros((cells, outputs), jnp.float32)
    for depth in range(3):
        block = plane_patches(padded, depth, False, planes, rows_x, rows_y)
        partial_value = partial_value + jnp.dot(
            block, weight[depth].reshape(-1, outputs), preferred_element_type=jnp.float32
        )
    summed = lax.psum_scatter(partial_value, "chan", scatter_dimension=1, tiled=True)
    pre = summed + bias.astype(jnp.float32)
    logistic = jax.nn.sigmoid(pre)
    activations = (
        (pre * logistic).astype(jnp.bfloat16).reshape(samples, planes, rows_x, rows_y, local_out)
    )
    upstream = cotangent.reshape(cells, local_out).astype(jnp.float32)
    grad_pre = (upstream * logistic * (1.0 + pre * (1.0 - logistic))).astype(jnp.bfloat16)
    bias_term = jnp.sum(grad_pre.astype(jnp.float32), axis=0)
    grad_full = lax.all_gather(
        grad_pre.reshape(samples, planes, rows_x, rows_y, local_out), "chan", axis=4, tiled=True
    )
    grad_flat = grad_full.reshape(cells, outputs)
    total_cells = cells * lax.axis_size("dp") * lax.axis_size("slab")
    factor = float(total_cells) ** (-0.5)

    def depth_term(depth):
        block = plane_patches(padded, depth, False, planes, rows_x, rows_y)
        term = lax.dot_general(
            block, grad_flat, (((0,), (0,)), ((), ())), preferred_element_type=jnp.float32
        )
        return term.reshape(3, 3, local_in, outputs)

    grad_padded = pad_sides(with_halo(grad_full, (("slab", 1),), 1))
    accum = jnp.zeros((cells, local_in), jnp.float32)
    for input_depth in range(3):
        block = plane_patches(grad_padded, 2 - input_depth, True, planes, rows_x, rows_y)
        flipped = jnp.transpose(weight[input_depth], (0, 1, 3, 2)).reshape(-1, local_in)
        accum = accum + jnp.dot(block, flipped, preferred_element_type=jnp.float32)
    input_grad = accum.astype(jnp.bfloat16).reshape(samples, planes, rows_x, rows_y, local_in)
    stacked = jnp.stack([depth_term(depth) for depth in range(3)], axis=0)
    kernel_sum, bias_sum = lax.psum((stacked, bias_term), ("dp", "slab"))
    weight_grad = kernel_sum * factor
    bias_grad = bias_sum * factor
    return (activations, input_grad, weight_grad, bias_grad)


def solution(mesh):
    placed = (
        P("dp", "slab", None, None, "chan"),
        P(None, None, None, "chan", None),
        P("chan"),
        P("dp", "slab", None, None, "chan"),
    )
    return jax.shard_map(
        per_device,
        mesh=mesh,
        in_specs=placed,
        out_specs=(
            P("dp", "slab", None, None, "chan"),
            P("dp", "slab", None, None, "chan"),
            P(None, None, None, "chan", None),
            P("chan"),
        ),
        check_vma=False,
    )
```

profile of v0, /device:TPU:1, one launch (start us, length us, event | category | flops | bytes accessed | tf_op | source)
XLA Modules:
  0.0 185.7 jit_solution(17833604500887666795)
XLA Ops:
  7.2 1.0 fusion.21
  8.2 4.5 %collective-permute-start = (bf16[1,1,32,16,128]{4,3,2,1,0:T(8,128)(2,1)S(1)}, bf16[1,1,32,16,128]{4,3,2,1,0:T(8,128)(2,1)S(1)}, u32[]{:S(2)}, u32[]{:S(2)}) collective-permute-start(bf16[1,1,32,16,128]{4,3,2,1,0:T(8,128)(2,1)S(1)} %get-tuple-element.69), channel_id=1, source_target_pairs={{0,2},{2,4},{4,6},{1,3},{3,5},{5,7},{8,10},{10,12},{12,14},{9,11},... | collective-permute-start | bytes 393224 | tf_op jit(solution)/shard_map/ppermute | solution.py:14
  12.7 2.1 %collective-permute-start.1 = (bf16[1,1,32,16,128]{4,3,2,1,0:T(8,128)(2,1)S(1)}, bf16[1,1,32,16,128]{4,3,2,1,0:T(8,128)(2,1)S(1)}, u32[]{:S(2)}, u32[]{:S(2)}) collective-permute-start(bf16[1,1,32,16,128]{4,3,2,1,0:T(8,128)(2,1)S(1)} %get-tuple-element.70), channel_id=1, source_target_pairs={{2,0},{4,2},{6,4},{3,1},{5,3},{7,5},{10,8},{12,10},{14,12},{11,9},... | collective-permute-start | bytes 393224 | tf_op jit(solution)/shard_map/ppermute | solution.py:15
  14.8 2.8 %slice_bitcast_fusion = (bf16[3,3,256,128]{2,3,1,0:T(8,128)(2,1)}, bf16[3,3,256,128]{2,3,1,0:T(8,128)(2,1)}, bf16[3,3,256,128]{2,3,1,0:T(8,128)(2,1)S(1)}, bf16[...) fusion(bf16[3,3,3,128,256]{4,3,2,1,0:T(8,128)(2,1)} %param.5), kind=kLoop, calls=%fused_computation.99 | loop fusion | bytes 5308416 | tf_op jit(solution)/shard_map/transpose | solution.py:83
  17.6 1.6 collective-permute-done.1
  25.1 1.9 %convolution_add_fusion = f32[1024,256]{1,0:T(8,128)} fusion(f32[1024,256]{1,0:T(8,128)S(1)} %convolution_add_fusion.1, bf16[1024,1152]{1,0:T(8,128)(2,1)S(1)} %bitcast.72, bf16[1152,256]{1,0:T(8,128)(2,1)S(1)} %bitcast.86), kind=kOutput, calls=%fused_computation.24 | convolution fusion | flops 604241920 | bytes 5046272 | tf_op jit(solution)/shard_map/dot_general | solution.py:53
  27.0 1.4 copy.19
  28.4 2.2 %copy.17 = bf16[3,3,256,128]{3,2,1,0:T(8,128)(2,1)} copy(bf16[3,3,256,128]{2,3,1,0:T(8,128)(2,1)} %get-tuple-element.7) | data formatting | bytes 1179648 | tf_op jit(solution)/shard_map/transpose | solution.py:83
  30.5 1.1 copy.18
  31.6 2.5 %copy.22 = bf16[1024,1152]{0,1:T(8,128)(2,1)} copy(bf16[1024,1152]{1,0:T(8,128)(2,1)S(1)} %bitcast.73) | data formatting | bytes 4718592 | tf_op jit(solution)/shard_map/reshape | solution.py:36
  34.1 4.4 %copy.21 = bf16[1024,1152]{0,1:T(8,128)(2,1)} copy(bf16[1024,1152]{1,0:T(8,128)(2,1)} %bitcast.75) | data formatting | bytes 4718592 | tf_op jit(solution)/shard_map/reshape | solution.py:36
  38.5 2.5 %copy.20 = bf16[1024,1152]{0,1:T(8,128)(2,1)} copy(bf16[1024,1152]{1,0:T(8,128)(2,1)S(1)} %bitcast.83) | data formatting | bytes 4718592 | tf_op jit(solution)/shard_map/reshape | solution.py:36
  41.1 6.2 %reduce-scatter.2.cloned.1.call-done = f32[1024,128]{1,0:T(8,128)} async-done(((f32[1024,256]{1,0:T(8,128)}), f32[1024,128]{1,0:T(8,128)}) %reduce-scatter.2.cloned.1.call-update) | async-done | bytes 524304 | tf_op jit(solution)/shard_map/reduce_scatter | solution.py:56
  47.2 2.1 %convert_reduce_fusion = (f32[128]{0:T(128)S(1)}, bf16[1024,128]{1,0:T(8,128)(2,1)S(1)}, bf16[1024,128]{1,0:T(8,128)(2,1)}) fusion(f32[1024,128]{1,0:T(8,128)} %reduce-scatter.2.cloned.1.call-done, f32[128]{0:T(128)S(1)} %convert_element_type.25, bf16[1,2,32,16,128]{4,3,2,1,0:T(8,128)(2,1)} %param.7), kind=kLoop, calls=%fused_computation.65 | loop fusion | flops 1965952 | bytes 1311744 | tf_op jit(solution)/shard_map/reduce_sum | solution.py:64
  49.3 8.0 %all_gather.3 = bf16[1,2,32,16,256]{4,3,2,1,0:T(8,128)(2,1)S(1)} all-gather(bf16[1,2,32,16,128]{4,3,2,1,0:T(8,128)(2,1)S(1)} %bitcast.89), channel_id=1, replica_groups=mesh['dp'=4,'slab'=4,'chan'=2] {'chan'}, dimensions={4}, use_global_device_ids=true | all-gather | bytes 786432 | tf_op jit(solution)/shard_map/all_gather | solution.py:65
  61.4 4.4 %collective-permute-start.2 = (bf16[1,1,32,16,256]{4,3,2,1,0:T(8,128)(2,1)}, bf16[1,1,32,16,256]{4,3,2,1,0:T(8,128)(2,1)S(1)}, u32[]{:S(2)}, u32[]{:S(2)}) collective-permute-start(bf16[1,1,32,16,256]{4,3,2,1,0:T(8,128)(2,1)} %get-tuple-element.64), channel_id=1, source_target_pairs={{0,2},{2,4},{4,6},{1,3},{3,5},{5,7},{8,10},{10,12},{12,14},{9,11},... | collective-permute-start | bytes 786440 | tf_op jit(solution)/shard_map/ppermute | solution.py:14
  65.8 1.9 %collective-permute-start.3 = (bf16[1,1,32,16,256]{4,3,2,1,0:T(8,128)(2,1)}, bf16[1,1,32,16,256]{4,3,2,1,0:T(8,128)(2,1)S(1)}, u32[]{:S(2)}, u32[]{:S(2)}) collective-permute-start(bf16[1,1,32,16,256]{4,3,2,1,0:T(8,128)(2,1)} %get-tuple-element.65), channel_id=1, source_target_pairs={{2,0},{4,2},{6,4},{3,1},{5,3},{7,5},{10,8},{12,10},{14,12},{11,9},... | collective-permute-start | bytes 786440 | tf_op jit(solution)/shard_map/ppermute | solution.py:15
  67.7 2.0 %pad_maximum_fusion = f32[3,3,3,128,256]{4,3,2,1,0:T(8,128)} fusion(f32[1,3,3,128,256]{4,3,2,1,0:T(8,128)S(1)} %convolution_bitcast_fusion, f32[1,3,3,128,256]{4,3,2,1,0:T(8,128)S(1)} %convolution_bitcast_fusion.1, f32[1,3,3,128,256]{4,3,2,1,0:T(8,128)S(1)} %convolution_bitcast_fusion.2), kind=kLoop, calls=%fused_computation.4 | loop fusion | flops 1769472 | bytes 7077888 | tf_op jit(solution)/shard_map/stack | solution.py:86
  69.8 30.4 %psum.15 = f32[128]{0:T(128)S(1)} all-reduce(f32[128]{0:T(128)S(1)} %get-tuple-element.4), channel_id=1, replica_groups=mesh['dp'=4,'slab'=4,'chan'=2] {'dp','slab'}, use_global_device_ids=true, to_apply=%region_3.4 | all-reduce | flops 128 | bytes 1024 | tf_op jit(solution)/shard_map/psum | solution.py:87
  105.4 1.4 fusion.23
  106.8 1.4 convolution_add_fusion.3
  108.2 2.1 %fusion.9 = bf16[1024,128]{1,0:T(8,128)(2,1)} fusion(f32[1024,128]{1,0:T(8,128)S(1)} %convolution_add_fusion.3, bf16[1024,2304]{1,0:T(8,128)(2,1)S(1)} %bitcast.79, bf16[2304,128]{1,0:T(8,128)(2,1)S(1)} %bitcast.84), kind=kOutput, calls=%fused_computation.28 | convolution fusion | flops 604241920 | bytes 6094848 | tf_op jit(solution)/shard_map/dot_general | solution.py:84
  110.3 64.4 %all-reduce.4.cloned.1.call-done = f32[3,3,3,128,256]{4,3,2,1,0:T(8,128)} async-done(((f32[3,3,3,128,256]{4,3,2,1,0:T(8,128)}), f32[3,3,3,128,256]{4,3,2,1,0:T(8,128)}) %all-reduce.4.cloned.1.call-update) | async-done | bytes 3538960 | tf_op jit(solution)/shard_map/psum | solution.py:87
  174.7 4.2 %broadcast_multiply_fusion = f32[3,3,3,128,256]{4,3,2,1,0:T(8,128)} fusion(f32[3,3,3,128,256]{4,3,2,1,0:T(8,128)} %all-reduce.4.cloned.1.call-done), kind=kLoop, calls=%fused_computation.12 | loop fusion | flops 884736 | bytes 7077888 | tf_op jit(solution)/shard_map/mul | solution.py:88
  (55 shorter events, 15.2 us)
Async XLA Ops:
  7.2 40.1 %reduce-scatter.2.cloned.1.call-start = ((), (), s32[]{:S(2)}) async-start(), calls=%async_computation.1 | async-start | bytes 1572864 | tf_op jit(solution)/shard_map/reduce_scatter | solution.py:56
  8.2 9.4 %collective-permute-start = (bf16[1,1,32,16,128]{4,3,2,1,0:T(8,128)(2,1)S(1)}, bf16[1,1,32,16,128]{4,3,2,1,0:T(8,128)(2,1)S(1)}, u32[]{:S(2)}, u32[]{:S(2)}) collective-permute-start(bf16[1,1,32,16,128]{4,3,2,1,0:T(8,128)(2,1)S(1)} %get-tuple-element.69), channel_id=1, source_target_pairs={{0,2},{2,4},{4,6},{1,3},{3,5},{5,7},{8,10},{10,12},{12,14},{9,11},... | collective-permute-start | bytes 393224 | tf_op jit(solution)/shard_map/ppermute | solution.py:14
  12.7 6.4 %copy-start.7 = (bf16[1,2,32,16,128]{4,3,2,1,0:T(8,128)(2,1)S(1)}, bf16[1,2,32,16,128]{4,3,2,1,0:T(8,128)(2,1)}, u32[]{:S(2)}) copy-start(bf16[1,2,32,16,128]{4,3,2,1,0:T(8,128)(2,1)} %param.4) | copy-start | bytes 786436
  12.7 6.4 %collective-permute-start.1 = (bf16[1,1,32,16,128]{4,3,2,1,0:T(8,128)(2,1)S(1)}, bf16[1,1,32,16,128]{4,3,2,1,0:T(8,128)(2,1)S(1)}, u32[]{:S(2)}, u32[]{:S(2)}) collective-permute-start(bf16[1,1,32,16,128]{4,3,2,1,0:T(8,128)(2,1)S(1)} %get-tuple-element.70), channel_id=1, source_target_pairs={{2,0},{4,2},{6,4},{3,1},{5,3},{7,5},{10,8},{12,10},{14,12},{11,9},... | collective-permute-start | bytes 393224 | tf_op jit(solution)/shard_map/ppermute | solution.py:15
  22.0 1.4 copy-start.4
  22.0 2.2 %copy-start = (bf16[1,2,32,16,1152]{4,3,2,1,0:T(8,128)(2,1)}, bf16[1,2,32,16,1152]{4,3,2,1,0:T(8,128)(2,1)S(1)}, u32[]{:S(2)}) copy-start(bf16[1,2,32,16,1152]{4,3,2,1,0:T(8,128)(2,1)S(1)} %get-tuple-element.37) | copy-start | bytes 7077892
  25.0 1.9 %copy-start.9 = (bf16[128]{0:T(256)(128)(2,1)S(1)}, bf16[128]{0:T(256)(128)(2,1)}, u32[]{:S(2)}) copy-start(bf16[128]{0:T(256)(128)(2,1)} %param.6) | copy-start | bytes 772
  26.9 147.8 %all-reduce.4.cloned.1.call-start = ((), (), s32[]{:S(2)}) async-start(), calls=%async_computation.2 | async-start | bytes 7077888 | tf_op jit(solution)/shard_map/psum | solution.py:87
  34.1 4.4 %copy-start.5 = (bf16[1,2,32,16,1152]{4,3,2,1,0:T(8,128)(2,1)S(1)}, bf16[1,2,32,16,1152]{4,3,2,1,0:T(8,128)(2,1)}, u32[]{:S(2)}) copy-start(bf16[1,2,32,16,1152]{4,3,2,1,0:T(8,128)(2,1)} %copy-done.4) | copy-start | bytes 7077892
  41.1 17.0 %copy-start.1 = (bf16[1024,1152]{0,1:T(8,128)(2,1)S(1)}, bf16[1024,1152]{0,1:T(8,128)(2,1)}, u32[]{:S(2)}) copy-start(bf16[1024,1152]{0,1:T(8,128)(2,1)} %copy.22) | copy-start | bytes 7077892
  57.3 1.9 copy-start.2
  58.9 1.7 copy-start.3
  61.4 39.3 %collective-permute-start.2 = (bf16[1,1,32,16,256]{4,3,2,1,0:T(8,128)(2,1)}, bf16[1,1,32,16,256]{4,3,2,1,0:T(8,128)(2,1)S(1)}, u32[]{:S(2)}, u32[]{:S(2)}) collective-permute-start(bf16[1,1,32,16,256]{4,3,2,1,0:T(8,128)(2,1)} %get-tuple-element.64), channel_id=1, source_target_pairs={{0,2},{2,4},{4,6},{1,3},{3,5},{5,7},{8,10},{10,12},{12,14},{9,11},... | collective-permute-start | bytes 786440 | tf_op jit(solution)/shard_map/ppermute | solution.py:14
  65.8 34.9 %collective-permute-start.3 = (bf16[1,1,32,16,256]{4,3,2,1,0:T(8,128)(2,1)}, bf16[1,1,32,16,256]{4,3,2,1,0:T(8,128)(2,1)S(1)}, u32[]{:S(2)}, u32[]{:S(2)}) collective-permute-start(bf16[1,1,32,16,256]{4,3,2,1,0:T(8,128)(2,1)} %get-tuple-element.65), channel_id=1, source_target_pairs={{2,0},{4,2},{6,4},{3,1},{5,3},{7,5},{10,8},{12,10},{14,12},{11,9},... | collective-permute-start | bytes 786440 | tf_op jit(solution)/shard_map/ppermute | solution.py:15
  104.3 1.1 copy-start.8
  105.4 1.4 copy-start.6
Sparse Core Ops, SparseCore 0:
  27.1 20.1 reduce-scatter.1
  69.9 104.7 all-reduce.3
where the time goes:
time: 188 us; the launch traced here: 186 us
  waiting for transfers between devices  72.2 us (38%)
  blocking collectives  38.3 us (20%)
  local copies, waits for them, and re-layouts  26.8 us (14%)
  between operations  14.4 us (8%)
  starting transfers between devices  13 us (7%)
  matrix products  10.8 us (6%)
  other arithmetic  10.3 us (5%)
    psum x1, waiting for transfers between devices, per_device(): kernel_sum, bias_sum = lax.psum((stacked, bias_term), ('dp', 'slab'))  64.4 us
    psum x1, blocking collectives, per_device(): kernel_sum, bias_sum = lax.psum((stacked, bias_term), ('dp', 'slab'))  30.4 us
    reshape x3, local copies, waits for them, and re-layouts, plane_patches(): return block.reshape(-1, block.shape[4])  9.43 us
    ppermute x2, starting transfers between devices, with_halo(): before = lax.ppermute(last, axis, up)  8.91 us
    all_gather x1, blocking collectives, per_device(): lax.all_gather(grad_pre.reshape(samples, planes, rows_x, rows_y, local_ou...  7.96 us
    unnamed x34, local copies, waits for them, and re-layouts  7.74 us
    transpose x4, local copies, waits for them, and re-layouts, per_device(): jnp.transpose(weight[input_depth], (0, 1, 3, 2)).reshape(-1, local_in)  7.4 us
    reduce_scatter x1, waiting for transfers between devices, per_device(): lax.psum_scatter(partial_value, 'chan', scatter_dimension=1, tiled=True)  6.16 us
  transfers between devices with their start and end apart: 6, of which 3 were waited for; matrix products, arithmetic and copies ran while one was open for 15% of the time, Pallas kernels for 0%

commit v1 on v0

v1 whole, which is shorter than its diff:
```python
import functools

import jax
import jax.numpy as jnp
from jax import lax
from jax.experimental import pallas as pl
from jax.experimental.pallas import tpu as pltpu
from jax.sharding import PartitionSpec as P

BF = jnp.bfloat16
F32 = jnp.float32
MIB = 1 << 20


def swap(value, axis, bit):
    return lax.ppermute(value, axis, [(i, i ^ bit) for i in range(lax.axis_size(axis))])


def vmem_call(body, outs, scratch, flops, *args, limit=40):
    shapes = [jax.ShapeDtypeStruct(s, d) for s, d in outs]
    moved = sum(a.size * a.dtype.itemsize for a in args)
    return pl.pallas_call(
        body,
        out_shape=shapes,
        in_specs=[pl.BlockSpec(memory_space=pltpu.SMEM)]
        + [pl.BlockSpec(memory_space=pltpu.VMEM)] * (len(args) - 1),
        out_specs=[pl.BlockSpec(memory_space=pltpu.VMEM)] * len(shapes),
        scratch_shapes=scratch,
        compiler_params=pltpu.CompilerParams(vmem_limit_bytes=limit * MIB),
        cost_estimate=pl.CostEstimate(flops=flops, bytes_accessed=moved, transcendentals=0),
    )(*args)


def shift_y(value, step, ny):
    rows = value.shape[0]
    y = lax.broadcasted_iota(jnp.int32, value.shape, 0) % ny
    rolled = pltpu.roll(value, (-step) % rows, 0)
    return jnp.where(y == (0 if step < 0 else ny - 1), 0.0, rolled)


def put_plane(buf, at, value, ny, flip):
    cells, lanes = value.shape
    wide = value.astype(F32)
    edge = jnp.zeros((ny, 3 * lanes), BF)
    buf[at, 0:ny, :] = edge
    buf[at, ny + cells : 2 * ny + cells, :] = edge
    for c in range(3):
        step = (1 - c) if flip else (c - 1)
        moved = value if step == 0 else shift_y(wide, step, ny).astype(BF)
        buf[at, ny : ny + cells, c * lanes : (c + 1) * lanes] = moved


def forward_body(ny, pos, vol, near, far, w, own, send, buf):
    planes, cells, _ = vol.shape
    odd, y = pos[0], pos[1]
    for p in range(planes):
        put_plane(buf, p + 1, vol[p], ny, False)
    put_plane(buf, jnp.where(odd == 0, planes + 1, 0), near[...], ny, False)
    put_plane(buf, jnp.where(odd == 0, 0, planes + 1), far[...], ny, False)
    half = own.shape[1]
    for z in range(planes):
        acc = jnp.zeros((cells, 2 * half), F32)
        for a in range(3):
            lhs = jnp.concatenate([buf[z + a, b * ny : b * ny + cells, :] for b in range(3)], axis=1)
            acc = acc + jnp.dot(lhs, w[a], preferred_element_type=F32)
        own[z * cells : (z + 1) * cells, :] = jnp.where(y == 0, acc[:, :half], acc[:, half:])
        send[z * cells : (z + 1) * cells, :] = jnp.where(y == 0, acc[:, half:], acc[:, :half]).astype(BF)


def gate_body(pos, own, recv, bias, cot, act, grad):
    pre = own[...] + recv[...].astype(F32) + bias[...].astype(F32)
    s = 1.0 / (1.0 + jnp.exp(-pre))
    act[...] = (pre * s).astype(BF)
    grad[...] = (cot[...].astype(F32) * s * (1.0 + pre * (1.0 - s))).astype(BF)


def volume_body(pos, v0, v1, v2, ends, vt):
    planes, cells, lanes = v0.shape
    mine, k = pos[2], pos[3]
    keep = lanes // 2
    total = 4 * planes

    def put(at, value):
        turned = value.astype(F32).T
        turned = jnp.where(k == 0, turned[:keep], turned[keep:]).astype(BF)
        for a in range(3):
            vt[at + 2 - a, a * keep : (a + 1) * keep, :] = turned

    put(-1 + 1, ends[0])
    put(total + 1, ends[1])
    for p in range(planes):
        put(mine * planes + p + 1, v0[p])
        put((mine ^ 2) * planes + p + 1, v1[p])
        put((mine ^ 1) * planes + p + 1, v2[p])
        put((mine ^ 3) * planes + p + 1, v2[planes + p])


def kernel_body(ny, pos, vt, g0, g1, g2, keep1, send1, total, buf, acc):
    planes, cells = g0.shape[0], g0.shape[1]
    mine, bit0 = pos[2], pos[4]
    bsum = jnp.zeros((1, g0.shape[2]), F32)
    for p in range(planes):
        for at, value in (
            (mine * planes + p, g0[p]),
            ((mine ^ 2) * planes + p, g1[p]),
            ((mine ^ 1) * planes + p, g2[p]),
            ((mine ^ 3) * planes + p, g2[planes + p]),
        ):
            put_plane(buf, at, value, ny, True)
            bsum = bsum + jnp.sum(value.astype(F32), axis=0, keepdims=True)
    total[...] = jnp.broadcast_to(bsum, total.shape)
    rows = acc.shape[0]
    for b in range(3):
        summed = jnp.zeros(acc.shape, F32)
        for z in range(4 * planes):
            rhs = buf[z, (2 - b) * ny : (2 - b) * ny + cells, :]
            summed = summed + jnp.dot(vt[z + 2], rhs, preferred_element_type=F32)
        acc[...] = summed
        part = rows // 6
        for a in range(3):
            at = (3 * b + a) * part
            keep1[at : at + part, :] = acc[pl.ds((2 * a + bit0) * part, part), :]
            send1[at : at + part, :] = acc[pl.ds((2 * a + 1 - bit0) * part, part), :].astype(BF)
    send1[9 * part : 9 * part + 16, :] = split_rows(total)


def split_rows(total):
    value = jnp.broadcast_to(total[0:1, :], (16, total.shape[1]))
    high = value.astype(BF)
    rest = value - high.astype(F32)
    mid = rest.astype(BF)
    low = (rest - mid.astype(F32)).astype(BF)
    return jnp.concatenate([high, mid, low], axis=1)


def joined(rows):
    n = rows.shape[1] // 3
    wide = rows[0:8, :].astype(F32)
    return wide[:, :n] + wide[:, n : 2 * n] + wide[:, 2 * n :]


def second_body(pos, keep1, recv1, total1, keep2, send2, total2):
    bit1 = pos[5]
    part = keep2.shape[0] // 9
    total2[...] = total1[...] + joined(recv1[18 * part : 18 * part + 16, :])
    for n in range(9):
        lo = keep1[2 * n * part : (2 * n + 1) * part, :] + recv1[2 * n * part : (2 * n + 1) * part, :].astype(F32)
        hi = keep1[(2 * n + 1) * part : (2 * n + 2) * part, :] + recv1[
            (2 * n + 1) * part : (2 * n + 2) * part, :
        ].astype(F32)
        keep2[n * part : (n + 1) * part, :] = jnp.where(bit1 == 0, lo, hi)
        send2[n * part : (n + 1) * part, :] = jnp.where(bit1 == 0, hi, lo).astype(BF)
    send2[9 * part : 9 * part + 16, :] = split_rows(total2)


def last_body(factor, pos, keep2, recv2, total2, quarter, total3):
    rows = keep2.shape[0]
    total3[...] = (total2[...] + joined(recv2[rows : rows + 16, :])) * factor
    quarter[0:rows, :] = ((keep2[...] + recv2[0:rows, :].astype(F32)) * factor).astype(BF)
    quarter[rows : rows + 16, :] = split_rows(total3)


def spread_body(pos, d, dx, e, total3, out, bias_out):
    x, y, k, bit0, bit1 = pos[6], pos[1], pos[3], pos[4], pos[5]
    half = out.shape[4] // 2
    for piece, kk, xx in ((d, k, x), (dx, k, 1 - x), (e.at[0], 1 - k, x), (e.at[1], 1 - k, 1 - x)):
        for j in range(4):
            q = 2 * (bit0 ^ (j >> 1)) + (bit1 ^ (j & 1))
            row = pl.multiple_of(kk * 64 + q * 16, 16)
            lane = pl.multiple_of(xx * half, half)
            n = 3 * pl.program_id(1) + pl.program_id(0)
            for c in range(3):
                out[0, 0, c, pl.ds(row, 16), pl.ds(lane, half)] = piece[
                    j, pl.ds(pl.multiple_of(n * 16, 16), 16), c * half : (c + 1) * half
                ].astype(F32)
    other = joined(dx[0, dx.shape[1] - 16 : dx.shape[1], :])
    bias_out[...] = jnp.where(x == y, total3[...], other)


def input_body(ny, pos, g, go, near, far, wt, out, buf):
    planes, cells, half = g.shape
    odd, y = pos[0], pos[1]

    def whole(p):
        mine, other = g[p], go[p]
        first = jnp.where(y == 0, mine, other)
        second = jnp.where(y == 0, other, mine)
        return jnp.concatenate([first, second], axis=1)

    for p in range(planes):
        put_plane(buf, p + 1, whole(p), ny, True)
    put_plane(buf, jnp.where(odd == 0, planes + 1, 0), near[...], ny, True)
    put_plane(buf, jnp.where(odd == 0, 0, planes + 1), far[...], ny, True)
    lanes = 2 * half
    for z in range(planes):
        acc = jnp.zeros((cells, out.shape[1]), F32)
        for a in range(3):
            for b in range(3):
                for c in range(3):
                    lhs = buf[z + 2 - a, (2 - b) * ny : (2 - b) * ny + cells, c * lanes : (c + 1) * lanes]
                    acc = acc + lax.dot_general(
                        lhs, wt[(a * 3 + b) * 3 + c], (((1,), (1,)), ((), ())), preferred_element_type=F32
                    )
        out[z * cells : (z + 1) * cells, :] = acc.astype(BF)


def per_device(volumes, weight, bias, cotangent):
    samples, planes, nx, ny, local_in = volumes.shape
    outputs = weight.shape[4]
    local_out = bias.shape[0]
    plane = nx * ny
    cells = planes * plane
    slabs = lax.axis_size("slab")
    s, z, y = lax.axis_index("slab"), lax.axis_index("dp"), lax.axis_index("chan")
    odd, mine, x = s % 2, s % 4, (s // 2) % 2
    pos = jnp.stack([odd, y, mine, odd, z % 2, (z // 2) % 2, x]).astype(jnp.int32)
    factor = float(samples * cells * slabs * lax.axis_size("dp")) ** -0.5

    def pair_edges(field):
        first, final = field[0], field[planes - 1]
        near = swap(jnp.where(odd == 0, final, first), "slab", 1)
        pairs = [(i, i + 1) for i in range(1, slabs - 1, 2)]
        far = lax.ppermute(jnp.where(odd == 0, first, final), "slab", pairs + [(j, i) for i, j in pairs])
        return near, far

    vol = volumes.reshape(planes, plane, local_in)
    near, far = pair_edges(vol)
    own, send = vmem_call(
        functools.partial(forward_body, ny),
        [((cells, local_out), F32), ((cells, local_out), BF)],
        [pltpu.VMEM((planes + 2, plane + 2 * ny, 3 * local_in), BF)],
        2 * cells * 27 * local_in * outputs,
        pos, vol, near, far, weight.reshape(3, 9 * local_in, outputs),
    )
    recv = swap(send, "chan", 1)
    vol_x = swap(vol, "slab", 2)
    vol_c = swap(jnp.concatenate([vol, vol_x], axis=0), "slab", 1)
    ends = group_ends(vol, slabs)
    vt = vmem_call(
        volume_body,
        [((4 * planes + 4, 3 * local_in // 2, plane), BF)],
        [],
        0,
        pos, vol, vol_x, vol_c, ends,
    )[0]

    act, grad = vmem_call(
        gate_body,
        [((cells, local_out), BF), ((cells, local_out), BF)],
        [],
        0,
        pos, own, recv, bias.reshape(1, local_out), cotangent.reshape(cells, local_out),
    )
    grad = grad.reshape(planes, plane, local_out)
    grad_y = swap(grad, "chan", 1)
    mine_x = jnp.where(x == y, grad, grad_y)
    g_x = swap(jnp.where(x == y, grad_y, grad), "slab", 2)
    g_c = swap(jnp.concatenate([mine_x, g_x], axis=0), "slab", 1)
    rows, lanes = 3 * local_in // 2, 3 * local_out
    keep1, send1, total1 = vmem_call(
        functools.partial(kernel_body, ny),
        [((3 * rows // 2, lanes), F32), ((3 * rows // 2 + 16, lanes), BF), ((8, local_out), F32)],
        [pltpu.VMEM((4 * planes, plane + 2 * ny, lanes), BF), pltpu.VMEM((rows, lanes), F32)],
        2 * cells * 27 * local_in * outputs,
        pos, vt, mine_x, g_x, g_c,
    )
    bit = 4
    while bit < slabs:
        keep1 = keep1 + swap(keep1, "slab", bit)
        total1 = total1 + swap(total1, "slab", bit)
        wide = send1[: 3 * rows // 2].astype(F32)
        wide = wide + swap(wide, "slab", bit)
        high = total1.astype(BF)
        mid = (total1 - high.astype(F32)).astype(BF)
        low = (total1 - high.astype(F32) - mid.astype(F32)).astype(BF)
        tail = jnp.tile(jnp.concatenate([high, mid, low], axis=1), (2, 1))
        send1 = jnp.concatenate([wide.astype(BF), tail], axis=0)
        bit *= 2
    recv1 = swap(send1, "dp", 1)
    keep2, send2, total2 = vmem_call(
        second_body,
        [((3 * rows // 4, lanes), F32), ((3 * rows // 4 + 16, lanes), BF), ((8, local_out), F32)],
        [],
        0,
        pos, keep1, recv1, total1,
    )
    recv2 = swap(send2, "dp", 2)
    quarter, total3 = vmem_call(
        functools.partial(last_body, factor),
        [((3 * rows // 4 + 16, lanes), BF), ((8, local_out), F32)],
        [],
        0,
        pos, keep2, recv2, total2,
    )
    q2 = swap(quarter, "dp", 2)
    q1 = swap(quarter, "dp", 1)
    q3 = swap(q2, "dp", 1)
    d = jnp.stack([quarter, q2, q1, q3])
    dx = swap(d, "slab", 2)
    e = swap(jnp.stack([d, dx]), "slab", 1)
    weight_grad, bias_grad = spread(pos, d, dx, e, total3, local_in, outputs)

    g_whole = jnp.concatenate([jnp.where(y == 0, grad, grad_y), jnp.where(y == 0, grad_y, grad)], axis=2)
    g_near, g_far = pair_edges(g_whole)
    input_grad = vmem_call(
        functools.partial(input_body, ny),
        [((cells, local_in), BF)],
        [pltpu.VMEM((planes + 2, plane + 2 * ny, 3 * outputs), BF)],
        2 * cells * 27 * local_in * outputs,
        pos, grad, grad_y, g_near, g_far, weight.reshape(27, local_in, outputs),
    )[0]
    shape = (samples, planes, nx, ny)
    return act.reshape(shape + (local_out,)), input_grad.reshape(shape + (local_in,)), weight_grad, bias_grad[0]


def group_ends(vol, slabs):
    before, after = jnp.zeros_like(vol[0]), jnp.zeros_like(vol[0])
    for group in range(4 if slabs > 4 else 0):
        up = [(i - 1, i + group) for i in range(4, slabs, 4)]
        down = [(i + 4, i + group) for i in range(0, slabs - 4, 4)]
        before = before + lax.ppermute(vol[vol.shape[0] - 1], "slab", up)
        after = after + lax.ppermute(vol[0], "slab", down)
    return jnp.stack([before, after])


def spread(pos, d, dx, e, total3, local_in, outputs):
    whole = pl.BlockSpec(memory_space=pltpu.VMEM)
    return pl.pallas_call(
        spread_body,
        grid=(3, 3),
        out_shape=[
            jax.ShapeDtypeStruct((3, 3, 3, local_in, outputs), F32),
            jax.ShapeDtypeStruct(total3.shape, F32),
        ],
        in_specs=[pl.BlockSpec(memory_space=pltpu.SMEM), whole, whole, whole, whole],
        out_specs=[
            pl.BlockSpec((1, 1, 3, local_in, outputs), lambda i, j: (i, j, 0, 0, 0)),
            pl.BlockSpec(total3.shape, lambda i, j: (0, 0)),
        ],
        compiler_params=pltpu.CompilerParams(vmem_limit_bytes=20 * MIB),
    )(pos, d, dx, e, total3)


def solution(mesh):
    placed = (
        P("dp", "slab", None, None, "chan"),
        P(None, None, None, "chan", None),
        P("chan"),
        P("dp", "slab", None, None, "chan"),
    )
    return jax.shard_map(
        per_device,
        mesh=mesh,
        in_specs=placed,
        out_specs=(
            P("dp", "slab", None, None, "chan"),
            P("dp", "slab", None, None, "chan"),
            P(None, None, None, "chan", None),
            P("chan"),
        ),
        check_vma=False,
    )
```

time: 188 us -> 103 us (0.55); the launches traced: 186 us -> 103 us
  blocking collectives: 38.3 us -> 0 us
  waiting for transfers between devices: 72.2 us -> 39.1 us
  starting transfers between devices: 13 us -> 37.2 us
  local copies, waits for them, and re-layouts: 26.8 us -> 3.08 us
  Pallas kernels: 0 us -> 21 us
  between operations: 14.4 us -> 0.84 us
  matrix products: 10.8 us -> 0 us
  other arithmetic: 10.3 us -> 1.5 us
    psum x1 -> x0, waiting for transfers between devices: 64.4 us -> none  [per_device(): kernel_sum, bias_sum = lax.psum((stacked, bias_term), ('dp', 'slab'))]
    ppermute x4 -> x17, waiting for transfers between devices: 1.57 us -> 39.1 us  [the longest x15 32 us: swap(): lax.ppermute(value, axis, [(i, i ^ bit) for i in range(lax.axis_size(axis...]
    psum x1 -> x0, blocking collectives: 30.4 us -> none  [per_device(): kernel_sum, bias_sum = lax.psum((stacked, bias_term), ('dp', 'slab'))]
    ppermute x4 -> x17, starting transfers between devices: 12.9 us -> 37.2 us  [the longest x15 29.8 us: swap(): lax.ppermute(value, axis, [(i, i ^ bit) for i in range(lax.axis_size(axis...]
    pallas_call x0 -> x8, Pallas kernels: none -> 21 us  [the longest x7 16.4 us: vmem_call(): pl.pallas_call(body, out_shape=shapes, in_specs=[pl.BlockSpec(memory_spac...]
    dot_general x9 -> x0, matrix products: 10.8 us -> none  [the longest x3 4.9 us: per_device(): accum = accum + jnp.dot(block, flipped, preferred_element_type=jnp.float32)]
    reshape x3 -> x0, local copies, waits for them, and re-layouts: 9.43 us -> none  [plane_patches(): return block.reshape(-1, block.shape[4])]
    all_gather x1 -> x0, blocking collectives: 7.96 us -> none  [per_device(): lax.all_gather(grad_pre.reshape(samples, planes, rows_x, rows_y, local_ou...]
  transfers between devices with their start and end apart: 6 -> 17, of which waited for: 3 -> 12; matrix products, arithmetic and copies ran while one was open for 15% -> 0% of each run, Pallas kernels for 0% -> 6%
where the time goes in v1:
time: 103 us
  waiting for transfers between devices  39.1 us (38%)
  starting transfers between devices  37.2 us (36%)
  Pallas kernels  21 us (20%)
  local copies, waits for them, and re-layouts  3.08 us (3%)
  other arithmetic  1.5 us (1%)
    ppermute x15, waiting for transfers between devices, swap(): lax.ppermute(value, axis, [(i, i ^ bit) for i in range(lax.axis_size(axis...  32 us
    ppermute x15, starting transfers between devices, swap(): lax.ppermute(value, axis, [(i, i ^ bit) for i in range(lax.axis_size(axis...  29.8 us
    pallas_call x7, Pallas kernels, vmem_call(): pl.pallas_call(body, out_shape=shapes, in_specs=[pl.BlockSpec(memory_spac...  16.4 us
    ppermute x2, starting transfers between devices, pair_edges(): lax.ppermute(jnp.where(odd == 0, first, final), 'slab', pairs + [(j, i) f...  7.39 us
    ppermute x2, waiting for transfers between devices, pair_edges(): lax.ppermute(jnp.where(odd == 0, first, final), 'slab', pairs + [(j, i) f...  7.15 us
    pallas_call x1, Pallas kernels, spread(): pl.pallas_call(spread_body, grid=(3, 3), out_shape=[jax.ShapeDtypeStruct(...  4.55 us
    unnamed x12, local copies, waits for them, and re-layouts  2.44 us
  transfers between devices with their start and end apart: 17, of which 12 were waited for; matrix products, arithmetic and copies ran while one was open for 0% of the time, Pallas kernels for 6%

profile of v1, /device:TPU:1, one launch (start us, length us, event | category | flops | bytes accessed | tf_op | source)
XLA Modules:
  0.0 102.7 jit_solution(1332826918340378464)
XLA Ops:
  1.8 4.5 %collective-permute-start.1 = (bf16[512,128]{1,0:T(8,128)(2,1)S(1)}, bf16[512,128]{1,0:T(8,128)(2,1)S(1)}, u32[]{:S(2)}, u32[]{:S(2)}) collective-permute-start(bf16[512,128]{1,0:T(8,128)(2,1)S(1)} %bitcast.42), channel_id=1, source_target_pairs={{2,4},{4,2},{3,5},{5,3},{10,12},{12,10},{11,13},{13,11},{18,20},{2... | collective-permute-start | bytes 393224 | tf_op jit(solution)/shard_map/ppermute | solution.py:223
  6.4 2.5 %collective-permute-done.1.far = bf16[512,128]{1,0:T(8,128)(2,1)S(1)} collective-permute-done((bf16[512,128]{1,0:T(8,128)(2,1)S(1)}, bf16[512,128]{1,0:T(8,128)(2,1)S(1)}, u32[]{:S(2)}, u32[]{:S(2)}) %collective-permute-start.1) | collective-permute-done | bytes 131104 | tf_op jit(solution)/shard_map/ppermute | solution.py:223
  9.8 1.5 %copy-done.4 = bf16[3,3,3,128,256]{4,3,2,1,0:T(8,128)(2,1)S(1)} copy-done((bf16[3,3,3,128,256]{4,3,2,1,0:T(8,128)(2,1)S(1)}, bf16[3,3,3,128,256]{4,3,2,1,0:T(8,128)(2,1)}, u32[]{:S(2)}) %copy-start.4) | copy-done | bytes 1769496
  11.3 2.8 %shard_map.75 = (f32[1024,128]{1,0:T(8,128)S(1)}, bf16[1024,128]{1,0:T(8,128)(2,1)S(1)}) custom-call(s32[7]{0:T(128)S(1)} %stack.55.pos, bf16[2,512,128]{2,1,0:T(8,128)(2,1)S(1)} %bitcast.29, bf16[512,128]{1,0:T(8,128)(2,1)S(1)} %collective-permute-done.near, bf16[512,128]{1,0:T(8,128)(2,1)S(1)} %collective-permute-done.1.far, bf16[3,1152,256]{2,1,0:T(8,128)(2,1)S(1)} %bitcast.40), custom_call_target="tpu_custom_call" | custom-call | flops 1811939328 | bytes 2293788 | tf_op jit(solution)/shard_map/pallas_call | solution.py:22
  14.1 1.9 %collective-permute-start.2 = (bf16[1024,128]{1,0:T(8,128)(2,1)S(1)}, bf16[1024,128]{1,0:T(8,128)(2,1)S(1)}, u32[]{:S(2)}, u32[]{:S(2)}) collective-permute-start(bf16[1024,128]{1,0:T(8,128)(2,1)S(1)} %get-tuple-element.19), channel_id=1, source_target_pairs={{0,1},{1,0},{2,3},{3,2},{4,5},{5,4},{6,7},{7,6},{8,9},{9,8},{10,11... | collective-permute-start | bytes 786440 | tf_op jit(solution)/shard_map/ppermute | solution.py:16
  16.1 3.8 %collective-permute-done.2.recv = bf16[1024,128]{1,0:T(8,128)(2,1)S(1)} collective-permute-done((bf16[1024,128]{1,0:T(8,128)(2,1)S(1)}, bf16[1024,128]{1,0:T(8,128)(2,1)S(1)}, u32[]{:S(2)}, u32[]{:S(2)}) %collective-permute-start.2) | collective-permute-done | bytes 262176 | tf_op jit(solution)/shard_map/ppermute | solution.py:16
  19.8 1.4 %shard_map.76 = (bf16[1024,128]{1,0:T(8,128)(2,1)}, bf16[1024,128]{1,0:T(8,128)(2,1)S(1)}) custom-call(s32[7]{0:T(128)S(1)} %stack.55.pos, f32[1024,128]{1,0:T(8,128)S(1)} %get-tuple-element.18.own, bf16[1024,128]{1,0:T(8,128)(2,1)S(1)} %collective-permute-done.2.recv, bf16[1,128]{1,0:T(2,128)(2,1)S(1)} %bitcast.39, bf16[1024,128]{1,0:T(8,128)(2,1)S(1)} %bitcast.34), custom_call_target="tpu_custom_call" | custom-call | bytes 1048860 | tf_op jit(solution)/shard_map/pallas_call | solution.py:22
  21.3 1.5 %collective-permute-start.3 = (bf16[2,512,128]{2,1,0:T(8,128)(2,1)S(1)}, bf16[2,512,128]{2,1,0:T(8,128)(2,1)S(1)}, u32[]{:S(2)}, u32[]{:S(2)}) collective-permute-start(bf16[2,512,128]{2,1,0:T(8,128)(2,1)S(1)} %bitcast.35), channel_id=1, source_target_pairs={{0,1},{1,0},{2,3},{3,2},{4,5},{5,4},{6,7},{7,6},{8,9},{9,8},{10,11... | collective-permute-start | bytes 786440 | tf_op jit(solution)/shard_map/ppermute | solution.py:16
  22.7 3.8 %collective-permute-done.3.go = bf16[2,512,128]{2,1,0:T(8,128)(2,1)S(1)} collective-permute-done((bf16[2,512,128]{2,1,0:T(8,128)(2,1)S(1)}, bf16[2,512,128]{2,1,0:T(8,128)(2,1)S(1)}, u32[]{:S(2)}, u32[]{:S(2)}) %collective-permute-start.3) | collective-permute-done | bytes 262176 | tf_op jit(solution)/shard_map/ppermute | solution.py:16
  28.0 6.4 %collective-permute-start.7 = (bf16[4,512,128]{2,1,0:T(8,128)(2,1)S(1)}, bf16[4,512,128]{2,1,0:T(8,128)(2,1)S(1)}, u32[]{:S(2)}, u32[]{:S(2)}) collective-permute-start(bf16[4,512,128]{2,1,0:T(8,128)(2,1)S(1)} %pad_maximum_fusion.1), channel_id=1, source_target_pairs={{0,2},{2,0},{4,6},{6,4},{1,3},{3,1},{5,7},{7,5},{8,10},{10,8},{12,... | collective-permute-start | bytes 1572872 | tf_op jit(solution)/shard_map/ppermute | solution.py:16
  34.9 2.7 %collective-permute-start.9 = (bf16[4,512,128]{2,1,0:T(8,128)(2,1)S(1)}, bf16[4,512,128]{2,1,0:T(8,128)(2,1)S(1)}, u32[]{:S(2)}, u32[]{:S(2)}) collective-permute-start(bf16[4,512,128]{2,1,0:T(8,128)(2,1)S(1)} %pad_maximum_fusion.2), channel_id=1, source_target_pairs={{0,2},{2,0},{4,6},{6,4},{1,3},{3,1},{5,7},{7,5},{8,10},{10,8},{12,... | collective-permute-start | bytes 1572872 | tf_op jit(solution)/shard_map/ppermute | solution.py:16
  39.2 4.6 %shard_map.79 = (f32[288,384]{1,0:T(8,128)S(1)}, bf16[304,384]{1,0:T(8,128)(2,1)S(1)}, f32[8,128]{1,0:T(8,128)S(1)}) custom-call(s32[7]{0:T(128)S(1)} %stack.55.pos, bf16[12,192,512]{2,1,0:T(8,128)(2,1)S(1)} %shard_map.78.vt, bf16[2,512,128]{2,1,0:T(8,128)(2,1)S(1)} %get-tuple-element.33.g0, bf16[2,512,128]{2,1,0:T(8,128)(2,1)S(1)} %collective-permute-done.8.g1, ...), custom_call_target="tpu_custom_call" | custom-call | flops 1811939328 | bytes 3407900 | tf_op jit(solution)/shard_map/pallas_call | solution.py:22
  45.2 5.6 %collective-permute-done.10.recv1 = bf16[304,384]{1,0:T(8,128)(2,1)S(1)} collective-permute-done((bf16[304,384]{1,0:T(8,128)(2,1)S(1)}, bf16[304,384]{1,0:T(8,128)(2,1)S(1)}, u32[]{:S(2)}, u32[]{:S(2)}) %collective-permute-start.10) | collective-permute-done | bytes 233504 | tf_op jit(solution)/shard_map/ppermute | solution.py:16
  51.4 2.4 %collective-permute-start.11 = (bf16[160,384]{1,0:T(8,128)(2,1)S(1)}, bf16[160,384]{1,0:T(8,128)(2,1)S(1)}, u32[]{:S(2)}, u32[]{:S(2)}) collective-permute-start(bf16[160,384]{1,0:T(8,128)(2,1)S(1)} %get-tuple-element.26), channel_id=1, source_target_pairs={{0,16},{8,24},{16,0},{24,8},{1,17},{9,25},{17,1},{25,9},{2,18},{10... | collective-permute-start | bytes 368648 | tf_op jit(solution)/shard_map/ppermute | solution.py:16
  53.8 5.4 %collective-permute-done.11.recv2 = bf16[160,384]{1,0:T(8,128)(2,1)S(1)} collective-permute-done((bf16[160,384]{1,0:T(8,128)(2,1)S(1)}, bf16[160,384]{1,0:T(8,128)(2,1)S(1)}, u32[]{:S(2)}, u32[]{:S(2)}) %collective-permute-start.11) | collective-permute-done | bytes 122912 | tf_op jit(solution)/shard_map/ppermute | solution.py:16
  59.8 4.3 %collective-permute-start.13 = (bf16[160,384]{1,0:T(8,128)(2,1)S(1)}, bf16[160,384]{1,0:T(8,128)(2,1)S(1)}, u32[]{:S(2)}, u32[]{:S(2)}) collective-permute-start(bf16[160,384]{1,0:T(8,128)(2,1)S(1)} %get-tuple-element.28), channel_id=1, source_target_pairs={{0,8},{8,0},{16,24},{24,16},{1,9},{9,1},{17,25},{25,17},{2,10},{10... | collective-permute-start | bytes 368648 | tf_op jit(solution)/shard_map/ppermute | solution.py:16
  64.4 2.7 %collective-permute-start.14 = (bf16[160,384]{1,0:T(8,128)(2,1)S(1)}, bf16[160,384]{1,0:T(8,128)(2,1)S(1)}, u32[]{:S(2)}, u32[]{:S(2)}) collective-permute-start(bf16[160,384]{1,0:T(8,128)(2,1)S(1)} %collective-permute-done.12), channel_id=1, source_target_pairs={{0,8},{8,0},{16,24},{24,16},{1,9},{9,1},{17,25},{25,17},{2,10},{10... | collective-permute-start | bytes 368648 | tf_op jit(solution)/shard_map/ppermute | solution.py:16
  67.1 3.2 %collective-permute-done.14 = bf16[160,384]{1,0:T(8,128)(2,1)S(1)} collective-permute-done((bf16[160,384]{1,0:T(8,128)(2,1)S(1)}, bf16[160,384]{1,0:T(8,128)(2,1)S(1)}, u32[]{:S(2)}, u32[]{:S(2)}) %collective-permute-start.14) | collective-permute-done | bytes 122912 | tf_op jit(solution)/shard_map/ppermute | solution.py:16
  71.6 7.5 %collective-permute-done.15.dx = bf16[4,160,384]{2,1,0:T(8,128)(2,1)S(1)} collective-permute-done((bf16[4,160,384]{2,1,0:T(8,128)(2,1)S(1)}, bf16[4,160,384]{2,1,0:T(8,128)(2,1)S(1)}, u32[]{:S(2)}, u32[]{:S(2)}) %collective-permute-start.15) | collective-permute-done | bytes 491552 | tf_op jit(solution)/shard_map/ppermute | solution.py:16
  79.3 5.1 %collective-permute-start.16 = (bf16[2,4,160,384]{3,2,1,0:T(8,128)(2,1)S(1)}, bf16[2,4,160,384]{3,2,1,0:T(8,128)(2,1)S(1)}, u32[]{:S(2)}, u32[]{:S(2)}) collective-permute-start(bf16[2,4,160,384]{3,2,1,0:T(8,128)(2,1)S(1)} %pad_maximum_fusion), channel_id=1, source_target_pairs={{0,2},{2,0},{4,6},{6,4},{1,3},{3,1},{5,7},{7,5},{8,10},{10,8},{12,... | collective-permute-start | bytes 2949128 | tf_op jit(solution)/shard_map/ppermute | solution.py:16
  84.5 2.9 %collective-permute-start.5 = (bf16[512,256]{1,0:T(8,128)(2,1)S(1)}, bf16[512,256]{1,0:T(8,128)(2,1)S(1)}, u32[]{:S(2)}, u32[]{:S(2)}) collective-permute-start(bf16[512,256]{1,0:T(8,128)(2,1)S(1)} %get-tuple-element.36), channel_id=1, source_target_pairs={{2,4},{4,2},{3,5},{5,3},{10,12},{12,10},{11,13},{13,11},{18,20},{2... | collective-permute-start | bytes 786440 | tf_op jit(solution)/shard_map/ppermute | solution.py:223
  87.5 4.7 %collective-permute-done.5.far = bf16[512,256]{1,0:T(8,128)(2,1)S(1)} collective-permute-done((bf16[512,256]{1,0:T(8,128)(2,1)S(1)}, bf16[512,256]{1,0:T(8,128)(2,1)S(1)}, u32[]{:S(2)}, u32[]{:S(2)}) %collective-permute-start.5) | collective-permute-done | bytes 262176 | tf_op jit(solution)/shard_map/ppermute | solution.py:223
  92.2 5.4 %shard_map.77 = bf16[1024,128]{1,0:T(8,128)(2,1)} custom-call(s32[7]{0:T(128)S(1)} %stack.55.pos, bf16[2,512,128]{2,1,0:T(8,128)(2,1)S(1)} %bitcast.37, bf16[2,512,128]{2,1,0:T(8,128)(2,1)S(1)} %collective-permute-done.3.go, bf16[512,256]{1,0:T(8,128)(2,1)S(1)} %collective-permute-done.4.near, bf16[512,256]{1,0:T(8,128)(2,1)S(1)} %collective-permute-done.5.far, ...), custom_call_target="tpu_custom_call" | custom-call | flops 1811939328 | bytes 2818076 | tf_op jit(solution)/shard_map/pallas_call | solution.py:22
  97.6 4.6 %shard_map.82 = (f32[3,3,3,128,256]{4,3,2,1,0:T(8,128)}, f32[8,128]{1,0:T(8,128)S(1)}) custom-call(s32[7]{0:T(128)S(1)} %stack.55.pos, bf16[4,160,384]{2,1,0:T(8,128)(2,1)S(1)} %get-tuple-element.39.d, bf16[4,160,384]{2,1,0:T(8,128)(2,1)S(1)} %collective-permute-done.15.dx, bf16[2,4,160,384]{3,2,1,0:T(8,128)(2,1)S(1)} %collective-permute-done.16.e, ...), custom_call_target="tpu_custom_call" | custom-call | tf_op jit(solution)/shard_map/pallas_call | solution.py:328
  (40 shorter events, 10.8 us)
Async XLA Ops:
  1.6 4.8 %collective-permute-start = (bf16[512,128]{1,0:T(8,128)(2,1)S(1)}, bf16[512,128]{1,0:T(8,128)(2,1)S(1)}, u32[]{:S(2)}, u32[]{:S(2)}) collective-permute-start(bf16[512,128]{1,0:T(8,128)(2,1)S(1)} %bitcast.43), channel_id=1, source_target_pairs={{0,2},{2,0},{4,6},{6,4},{1,3},{3,1},{5,7},{7,5},{8,10},{10,8},{12,... | collective-permute-start | bytes 393224 | tf_op jit(solution)/shard_map/ppermute | solution.py:16
  1.8 7.1 %collective-permute-start.1 = (bf16[512,128]{1,0:T(8,128)(2,1)S(1)}, bf16[512,128]{1,0:T(8,128)(2,1)S(1)}, u32[]{:S(2)}, u32[]{:S(2)}) collective-permute-start(bf16[512,128]{1,0:T(8,128)(2,1)S(1)} %bitcast.42), channel_id=1, source_target_pairs={{2,4},{4,2},{3,5},{5,3},{10,12},{12,10},{11,13},{13,11},{18,20},{2... | collective-permute-start | bytes 393224 | tf_op jit(solution)/shard_map/ppermute | solution.py:223
  8.9 1.0 copy-start
  9.8 1.5 %copy-start.4 = (bf16[3,3,3,128,256]{4,3,2,1,0:T(8,128)(2,1)S(1)}, bf16[3,3,3,128,256]{4,3,2,1,0:T(8,128)(2,1)}, u32[]{:S(2)}) copy-start(bf16[3,3,3,128,256]{4,3,2,1,0:T(8,128)(2,1)} %param.5) | copy-start | bytes 5308420
  11.3 8.5 %copy-start.2 = (bf16[1,2,32,16,128]{4,3,2,1,0:T(8,128)(2,1)S(1)}, bf16[1,2,32,16,128]{4,3,2,1,0:T(8,128)(2,1)}, u32[]{:S(2)}) copy-start(bf16[1,2,32,16,128]{4,3,2,1,0:T(8,128)(2,1)} %param.7) | copy-start | bytes 786436
  11.3 8.5 %copy-start.3 = (bf16[128]{0:T(256)(128)(2,1)S(1)}, bf16[128]{0:T(256)(128)(2,1)}, u32[]{:S(2)}) copy-start(bf16[128]{0:T(256)(128)(2,1)} %param.6) | copy-start | bytes 772
  11.3 11.4 %copy-start.1 = (bf16[1,2,32,16,128]{4,3,2,1,0:T(8,128)(2,1)S(1)}, bf16[1,2,32,16,128]{4,3,2,1,0:T(8,128)(2,1)}, u32[]{:S(2)}) copy-start(bf16[1,2,32,16,128]{4,3,2,1,0:T(8,128)(2,1)} %param.4) | copy-start | bytes 786436
  14.1 5.7 %collective-permute-start.2 = (bf16[1024,128]{1,0:T(8,128)(2,1)S(1)}, bf16[1024,128]{1,0:T(8,128)(2,1)S(1)}, u32[]{:S(2)}, u32[]{:S(2)}) collective-permute-start(bf16[1024,128]{1,0:T(8,128)(2,1)S(1)} %get-tuple-element.19), channel_id=1, source_target_pairs={{0,1},{1,0},{2,3},{3,2},{4,5},{5,4},{6,7},{7,6},{8,9},{9,8},{10,11... | collective-permute-start | bytes 786440 | tf_op jit(solution)/shard_map/ppermute | solution.py:16
  21.3 5.2 %collective-permute-start.3 = (bf16[2,512,128]{2,1,0:T(8,128)(2,1)S(1)}, bf16[2,512,128]{2,1,0:T(8,128)(2,1)S(1)}, u32[]{:S(2)}, u32[]{:S(2)}) collective-permute-start(bf16[2,512,128]{2,1,0:T(8,128)(2,1)S(1)} %bitcast.35), channel_id=1, source_target_pairs={{0,1},{1,0},{2,3},{3,2},{4,5},{5,4},{6,7},{7,6},{8,9},{9,8},{10,11... | collective-permute-start | bytes 786440 | tf_op jit(solution)/shard_map/ppermute | solution.py:16
  22.7 5.2 %collective-permute-start.6 = (bf16[2,512,128]{2,1,0:T(8,128)(2,1)S(1)}, bf16[2,512,128]{2,1,0:T(8,128)(2,1)S(1)}, u32[]{:S(2)}, u32[]{:S(2)}) collective-permute-start(bf16[2,512,128]{2,1,0:T(8,128)(2,1)S(1)} %bitcast.30), channel_id=1, source_target_pairs={{0,4},{2,6},{4,0},{6,2},{1,5},{3,7},{5,1},{7,3},{8,12},{10,14},{12... | collective-permute-start | bytes 786440 | tf_op jit(solution)/shard_map/ppermute | solution.py:16
  26.6 8.3 %collective-permute-start.8 = (bf16[2,512,128]{2,1,0:T(8,128)(2,1)S(1)}, bf16[2,512,128]{2,1,0:T(8,128)(2,1)S(1)}, u32[]{:S(2)}, u32[]{:S(2)}) collective-permute-start(bf16[2,512,128]{2,1,0:T(8,128)(2,1)S(1)} %get-tuple-element.32), channel_id=1, source_target_pairs={{0,4},{2,6},{4,0},{6,2},{1,5},{3,7},{5,1},{7,3},{8,12},{10,14},{12... | collective-permute-start | bytes 786440 | tf_op jit(solution)/shard_map/ppermute | solution.py:16
  28.0 9.7 %collective-permute-start.7 = (bf16[4,512,128]{2,1,0:T(8,128)(2,1)S(1)}, bf16[4,512,128]{2,1,0:T(8,128)(2,1)S(1)}, u32[]{:S(2)}, u32[]{:S(2)}) collective-permute-start(bf16[4,512,128]{2,1,0:T(8,128)(2,1)S(1)} %pad_maximum_fusion.1), channel_id=1, source_target_pairs={{0,2},{2,0},{4,6},{6,4},{1,3},{3,1},{5,7},{7,5},{8,10},{10,8},{12,... | collective-permute-start | bytes 1572872 | tf_op jit(solution)/shard_map/ppermute | solution.py:16
  34.9 4.3 %collective-permute-start.9 = (bf16[4,512,128]{2,1,0:T(8,128)(2,1)S(1)}, bf16[4,512,128]{2,1,0:T(8,128)(2,1)S(1)}, u32[]{:S(2)}, u32[]{:S(2)}) collective-permute-start(bf16[4,512,128]{2,1,0:T(8,128)(2,1)S(1)} %pad_maximum_fusion.2), channel_id=1, source_target_pairs={{0,2},{2,0},{4,6},{6,4},{1,3},{3,1},{5,7},{7,5},{8,10},{10,8},{12,... | collective-permute-start | bytes 1572872 | tf_op jit(solution)/shard_map/ppermute | solution.py:16
  43.8 7.0 %collective-permute-start.10 = (bf16[304,384]{1,0:T(8,128)(2,1)S(1)}, bf16[304,384]{1,0:T(8,128)(2,1)S(1)}, u32[]{:S(2)}, u32[]{:S(2)}) collective-permute-start(bf16[304,384]{1,0:T(8,128)(2,1)S(1)} %get-tuple-element.23), channel_id=1, source_target_pairs={{0,8},{8,0},{16,24},{24,16},{1,9},{9,1},{17,25},{25,17},{2,10},{10... | collective-permute-start | bytes 700424 | tf_op jit(solution)/shard_map/ppermute | solution.py:16
  51.4 7.8 %collective-permute-start.11 = (bf16[160,384]{1,0:T(8,128)(2,1)S(1)}, bf16[160,384]{1,0:T(8,128)(2,1)S(1)}, u32[]{:S(2)}, u32[]{:S(2)}) collective-permute-start(bf16[160,384]{1,0:T(8,128)(2,1)S(1)} %get-tuple-element.26), channel_id=1, source_target_pairs={{0,16},{8,24},{16,0},{24,8},{1,17},{9,25},{17,1},{25,9},{2,18},{10... | collective-permute-start | bytes 368648 | tf_op jit(solution)/shard_map/ppermute | solution.py:16
  59.2 33.0 %copy-start.5 = (bf16[3,3,3,128,256]{4,3,2,1,0:T(8,128)(2,1)S(1)}, bf16[3,3,3,128,256]{4,3,2,1,0:T(8,128)(2,1)}, u32[]{:S(2)}) copy-start(bf16[3,3,3,128,256]{4,3,2,1,0:T(8,128)(2,1)} %param.5) | copy-start | bytes 5308420
  59.7 4.7 %collective-permute-start.12 = (bf16[160,384]{1,0:T(8,128)(2,1)S(1)}, bf16[160,384]{1,0:T(8,128)(2,1)S(1)}, u32[]{:S(2)}, u32[]{:S(2)}) collective-permute-start(bf16[160,384]{1,0:T(8,128)(2,1)S(1)} %get-tuple-element.28), channel_id=1, source_target_pairs={{0,16},{8,24},{16,0},{24,8},{1,17},{9,25},{17,1},{25,9},{2,18},{10... | collective-permute-start | bytes 368648 | tf_op jit(solution)/shard_map/ppermute | solution.py:16
  59.8 7.3 %collective-permute-start.13 = (bf16[160,384]{1,0:T(8,128)(2,1)S(1)}, bf16[160,384]{1,0:T(8,128)(2,1)S(1)}, u32[]{:S(2)}, u32[]{:S(2)}) collective-permute-start(bf16[160,384]{1,0:T(8,128)(2,1)S(1)} %get-tuple-element.28), channel_id=1, source_target_pairs={{0,8},{8,0},{16,24},{24,16},{1,9},{9,1},{17,25},{25,17},{2,10},{10... | collective-permute-start | bytes 368648 | tf_op jit(solution)/shard_map/ppermute | solution.py:16
  64.4 5.9 %collective-permute-start.14 = (bf16[160,384]{1,0:T(8,128)(2,1)S(1)}, bf16[160,384]{1,0:T(8,128)(2,1)S(1)}, u32[]{:S(2)}, u32[]{:S(2)}) collective-permute-start(bf16[160,384]{1,0:T(8,128)(2,1)S(1)} %collective-permute-done.12), channel_id=1, source_target_pairs={{0,8},{8,0},{16,24},{24,16},{1,9},{9,1},{17,25},{25,17},{2,10},{10... | collective-permute-start | bytes 368648 | tf_op jit(solution)/shard_map/ppermute | solution.py:16
  70.5 8.7 %collective-permute-start.15 = (bf16[4,160,384]{2,1,0:T(8,128)(2,1)S(1)}, bf16[4,160,384]{2,1,0:T(8,128)(2,1)S(1)}, u32[]{:S(2)}, u32[]{:S(2)}) collective-permute-start(bf16[4,160,384]{2,1,0:T(8,128)(2,1)S(1)} %get-tuple-element.39.d), channel_id=1, source_target_pairs={{0,4},{2,6},{4,0},{6,2},{1,5},{3,7},{5,1},{7,3},{8,12},{10,14},{12... | collective-permute-start | bytes 1474568 | tf_op jit(solution)/shard_map/ppermute | solution.py:16
  79.3 18.3 %collective-permute-start.16 = (bf16[2,4,160,384]{3,2,1,0:T(8,128)(2,1)S(1)}, bf16[2,4,160,384]{3,2,1,0:T(8,128)(2,1)S(1)}, u32[]{:S(2)}, u32[]{:S(2)}) collective-permute-start(bf16[2,4,160,384]{3,2,1,0:T(8,128)(2,1)S(1)} %pad_maximum_fusion), channel_id=1, source_target_pairs={{0,2},{2,0},{4,6},{6,4},{1,3},{3,1},{5,7},{7,5},{8,10},{10,8},{12,... | collective-permute-start | bytes 2949128 | tf_op jit(solution)/shard_map/ppermute | solution.py:16
  84.5 7.7 %collective-permute-start.5 = (bf16[512,256]{1,0:T(8,128)(2,1)S(1)}, bf16[512,256]{1,0:T(8,128)(2,1)S(1)}, u32[]{:S(2)}, u32[]{:S(2)}) collective-permute-start(bf16[512,256]{1,0:T(8,128)(2,1)S(1)} %get-tuple-element.36), channel_id=1, source_target_pairs={{2,4},{4,2},{3,5},{5,3},{10,12},{12,10},{11,13},{13,11},{18,20},{2... | collective-permute-start | bytes 786440 | tf_op jit(solution)/shard_map/ppermute | solution.py:223
  87.4 4.8 %collective-permute-start.4 = (bf16[512,256]{1,0:T(8,128)(2,1)S(1)}, bf16[512,256]{1,0:T(8,128)(2,1)S(1)}, u32[]{:S(2)}, u32[]{:S(2)}) collective-permute-start(bf16[512,256]{1,0:T(8,128)(2,1)S(1)} %get-tuple-element.37), channel_id=1, source_target_pairs={{0,2},{2,0},{4,6},{6,4},{1,3},{3,1},{5,7},{7,5},{8,10},{10,8},{12,... | collective-permute-start | bytes 786440 | tf_op jit(solution)/shard_map/ppermute | solution.py:16

commit v2 on v0

v2 whole, which is shorter than its diff:
```python
import functools

import jax
import jax.numpy as jnp
from jax import lax
from jax.experimental import pallas as pl
from jax.experimental.pallas import tpu as pltpu
from jax.sharding import PartitionSpec as P

BF = jnp.bfloat16
F32 = jnp.float32
MIB = 1 << 20


def swap(value, axis, bit):
    return lax.ppermute(value, axis, [(i, i ^ bit) for i in range(lax.axis_size(axis))])


def vmem_call(body, outs, scratch, flops, *args, left=(), after=(), limit=20):
    shapes = [jax.ShapeDtypeStruct(s, d) for s, d in outs]
    count, waited = len(args), len(after)

    def inner(*refs):
        body(*refs[:count], *refs[count + waited :])

    specs = [pl.BlockSpec(memory_space=pl.ANY if n in left else pltpu.VMEM) for n in range(1, count)]
    return pl.pallas_call(
        inner,
        out_shape=shapes,
        in_specs=[pl.BlockSpec(memory_space=pltpu.SMEM)] + specs + [pl.BlockSpec(memory_space=pl.ANY)] * waited,
        out_specs=[pl.BlockSpec(memory_space=pltpu.VMEM)] * len(shapes),
        scratch_shapes=scratch,
        compiler_params=pltpu.CompilerParams(vmem_limit_bytes=limit * MIB),
        cost_estimate=pl.CostEstimate(flops=4 * flops + 10**9, bytes_accessed=MIB, transcendentals=0),
    )(*args, *after)


def shift_y(value, step, ny):
    rows = value.shape[0]
    y = lax.broadcasted_iota(jnp.int32, value.shape, 0) % ny
    rolled = pltpu.roll(value, (-step) % rows, 0)
    return jnp.where(y == (0 if step < 0 else ny - 1), 0.0, rolled)


def put_plane(buf, at, value, ny, flip):
    cells, lanes = value.shape
    wide = value.astype(F32)
    edge = jnp.zeros((ny, 3 * lanes), BF)
    buf[at, 0:ny, :] = edge
    buf[at, ny + cells : 2 * ny + cells, :] = edge
    for c in range(3):
        step = (1 - c) if flip else (c - 1)
        moved = value if step == 0 else shift_y(wide, step, ny).astype(BF)
        buf[at, ny : ny + cells, c * lanes : (c + 1) * lanes] = moved


def near_body(ny, pos, plane, vol_n, vol_f, w, own, send, kept, held, buf, sem):
    copy = pltpu.make_async_copy(w, held, sem)
    copy.start()
    put_plane(kept, 0, vol_n[...], ny, False)
    put_plane(kept, 1, vol_f[...], ny, False)
    outer_body(ny, pos, plane, kept, w, own, send, buf)
    copy.wait()


def outer_body(ny, pos, plane, kept, w, own, send, buf):
    cells = plane.shape[0]
    y, depth, at = pos[1], pos[7], pos[8]
    half = own.shape[1]
    put_plane(buf, 0, plane[...], ny, False)
    total = tap(kept.at[at], w, 1, ny, cells) + tap(kept.at[1 - at], w, 2 - depth, ny, cells)
    total = total + tap(buf.at[0], w, depth, ny, cells)
    own[...] = jnp.where(y == 0, total[:, :half], total[:, half:])
    send[...] = jnp.where(y == 0, total[:, half:], total[:, :half]).astype(BF)


def tap(field, w, depth, ny, cells):
    lhs = jnp.concatenate([field[b * ny : b * ny + cells, :] for b in range(3)], axis=1)
    return jnp.dot(lhs, w[depth], preferred_element_type=F32)


def gate(pos, plane, own, recv, bias, cot):
    pre = own[...] + recv[...].astype(F32) + bias[...].astype(F32)
    s = 1.0 / (1.0 + jnp.exp(-pre))
    return (pre * s).astype(BF), (cot[plane].astype(F32) * s * (1.0 + pre * (1.0 - s))).astype(BF)


def near_gate_body(pos, own, recv, bias, cot, act, grad):
    act[...], grad[...] = gate(pos, 1 - pos[0], own, recv, bias, cot)


def far_gate_body(pos, own, recv, bias, cot, act, grad):
    act[...], grad[...] = gate(pos, pos[0], own, recv, bias, cot)


def pack_body(pos, *refs):
    out, at = refs[-1], 0
    for ref in refs[:-1]:
        if len(ref.shape) == 3:
            for n in range(ref.shape[0]):
                out[at + n] = ref[n]
            at += ref.shape[0]
        else:
            out[at] = ref[...]
            at += 1


def pack(pos, *arrays, after=()):
    count = sum(a.shape[0] if a.ndim == 3 else 1 for a in arrays)
    return vmem_call(
        pack_body, [((count,) + arrays[0].shape[-2:], arrays[0].dtype)], [], 0, pos, *arrays, after=after
    )[0]


def volume_body(pos, v0, v1, v2, v3, ends, vt):
    planes, cells, lanes = v0.shape
    mine, k = pos[2], pos[3]
    keep = lanes // 2

    def put(at, value):
        turned = value.astype(F32).T
        turned = jnp.where(k == 0, turned[:keep], turned[keep:]).astype(BF)
        for a in range(3):
            vt[at + 2 - a, a * keep : (a + 1) * keep, :] = turned

    put(0, ends[0])
    put(4 * planes + 1, ends[1])
    for p in range(planes):
        for who, field in enumerate((v0, v1, v2, v3)):
            put((mine ^ who) * planes + p + 1, field[p])


def kernel_terms(ny, pos, near, vt, grads, buf, acc, before):
    cells, lanes = grads[0][1].shape
    mine, odd = pos[2], pos[0]
    bsum = jnp.zeros((1, lanes), F32)
    where = []
    for n, (who, ref) in enumerate(grads):
        own_odd = odd if who in (0, 2) else 1 - odd
        where.append((mine ^ who) * 2 + (1 - own_odd if near else own_odd) + 2)
        value = ref[...]
        put_plane(buf, n, value, ny, True)
        bsum = bsum + jnp.sum(value.astype(F32), axis=0, keepdims=True)
    lhs = jnp.concatenate([vt[at] for at in where], axis=1)
    for b in range(3):
        rhs = jnp.concatenate(
            [buf[n, (2 - b) * ny : (2 - b) * ny + cells, :] for n in range(len(grads))], axis=0
        )
        summed = jnp.dot(lhs, rhs, preferred_element_type=F32)
        acc[b] = summed if before is None else summed + before[b]
    return bsum


def near_kernel_body(ny, pos, vt, g0, g1, g2, g3, keep_f, acc, total, sent, buf):
    sent[...] = keep_f[...]
    bsum = kernel_terms(ny, pos, True, vt, ((0, g0), (1, g1), (2, g2), (3, g3)), buf, acc, None)
    total[...] = jnp.broadcast_to(bsum, total.shape)


def mid_kernel_body(ny, pos, vt, g0, g2, acc0, total0, acc, total, buf):
    bsum = kernel_terms(ny, pos, False, vt, ((0, g0), (2, g2)), buf, acc, acc0)
    total[...] = total0[...] + jnp.broadcast_to(bsum, total.shape)


def far_kernel_body(ny, pos, vt, g1, g3, acc0, total0, acc, total, buf):
    bsum = kernel_terms(ny, pos, False, vt, ((1, g1), (3, g3)), buf, acc, acc0)
    total[...] = total0[...] + jnp.broadcast_to(bsum, total.shape)


def last_kernel_body(ny, pos, vt, g1, g3, acc0, total0, keep, s1, s2, s3, total, buf, acc):
    far_kernel_body(ny, pos, vt, g1, g3, acc0, total0, acc, total, buf)
    cut_body(pos, acc, total, keep, s1, s2, s3)


def cut_body(pos, acc, total, keep, s1, s2, s3):
    part = keep.shape[0] // 9
    mine = pos[4]
    for b in range(3):
        for a in range(3):
            rows = slice((3 * b + a) * part, (3 * b + a + 1) * part)
            keep[rows, :] = acc[b, pl.ds(pl.multiple_of((4 * a + mine) * part, part), part), :]
            for who, ref in ((1, s1), (2, s2), (3, s3)):
                at = pl.multiple_of((4 * a + (mine ^ who)) * part, part)
                ref[rows, :] = acc[b, pl.ds(at, part), :].astype(BF)
    for ref in (s1, s2, s3):
        ref[9 * part : 9 * part + 16, :] = split_rows(total)


def split_rows(total):
    value = jnp.broadcast_to(total[0:1, :], (16, total.shape[1]))
    high = value.astype(BF)
    rest = value - high.astype(F32)
    mid = rest.astype(BF)
    low = (rest - mid.astype(F32)).astype(BF)
    return jnp.concatenate([high, mid, low], axis=1)


def joined(rows):
    n = rows.shape[1] // 3
    wide = rows[0:8, :].astype(F32)
    return wide[:, :n] + wide[:, n : 2 * n] + wide[:, 2 * n :]


def sum_body(factor, pos, keep, r1, r2, r3, total, quarter, quarter_b, total3):
    rows = keep.shape[0]
    tails = [joined(ref[rows : rows + 16, :]) for ref in (r1, r2, r3)]
    total3[...] = ((total[...] + tails[0]) + (tails[1] + tails[2])) * factor
    one = keep[...] + r1[0:rows, :].astype(F32)
    two = r2[0:rows, :].astype(F32) + r3[0:rows, :].astype(F32)
    quarter[...] = ((one + two) * factor).astype(BF)
    quarter_b[0:rows, :] = quarter[...]
    quarter_b[rows : rows + 16, :] = split_rows(total3)


def place(pos, pieces, out, wide, sems):
    x, k, mine = pos[6], pos[3], pos[4]
    half = out.shape[2] // 2
    copies = []
    for n, (who, j, piece) in enumerate(pieces):
        for b in range(3):
            for a in range(3):
                for c in range(3):
                    rows = slice((3 * b + a) * 16, (3 * b + a + 1) * 16)
                    wide[n, (a * 3 + b) * 3 + c] = piece[rows, c * half : (c + 1) * half].astype(F32)
        row = pl.multiple_of((k ^ (who >> 1)) * 64 + (mine ^ j) * 16, 16)
        lane = pl.multiple_of((x ^ (who & 1)) * half, half)
        copy = pltpu.make_async_copy(wide.at[n], out.at[:, pl.ds(row, 16), pl.ds(lane, half)], sems.at[n])
        copy.start()
        copies.append(copy)
    for copy in copies:
        copy.wait()


def round_body(pos, q, q1, q2, x0, one_z, two_x, four_c):
    one_z[...] = q2[...]
    two_x[0], two_x[1] = q1[...], q2[...]
    four_c[0], four_c[1], four_c[2], four_c[3] = q[...], q1[...], q2[...], x0[0 : q.shape[0], :]


def next_round_body(pos, q3, x12, one_x, three_c):
    one_x[...] = q3[...]
    three_c[0], three_c[1], three_c[2] = q3[...], x12[0], x12[1]


def first_spread_body(pos, own, core, out, done, wide, sems):
    kinds = ((0, 0), (0, 1), (0, 2), (1, 0))
    pieces = [(who, j, own.at[n]) for n, (who, j) in enumerate(kinds)]
    pieces += [(who + 2, j, core.at[n]) for n, (who, j) in enumerate(kinds)]
    place(pos, pieces, out, wide, sems)
    done[...] = jnp.zeros_like(done)


def next_spread_body(pos, own, core, before, out, done, wide, sems):
    kinds = ((0, 3), (1, 1), (1, 2))
    pieces = [(who, j, own.at[n]) for n, (who, j) in enumerate(kinds)]
    pieces += [(who + 2, j, core.at[n]) for n, (who, j) in enumerate(kinds)]
    place(pos, pieces, out, wide, sems)
    done[...] = jnp.zeros_like(done)


def last_spread_body(pos, x0, x3, core3, total3, before, out, bias_out, wide, sems):
    place(pos, [(1, 3, x3), (3, 3, core3)], out, wide, sems)
    rows = x3.shape[0]
    other = joined(x0[rows : rows + 16, :])[0:1, :]
    bias_out[...] = jnp.where(pos[6] == pos[1], total3[0:1, :], other)


def spread(body, shape, small, after, pos, *arrays, alias=False):
    whole = pl.BlockSpec(memory_space=pltpu.VMEM)
    anywhere = pl.BlockSpec(memory_space=pl.ANY)
    count, waited = 1 + len(arrays), len(after)

    def inner(*refs):
        body(*refs[:count], *refs[count + waited :])

    specs = [pl.BlockSpec(memory_space=pltpu.SMEM)] + [whole] * (len(arrays) - alias) + [anywhere] * alias
    return pl.pallas_call(
        inner,
        out_shape=[jax.ShapeDtypeStruct(shape, F32), jax.ShapeDtypeStruct(*small)],
        in_specs=specs + [anywhere] * waited,
        out_specs=[anywhere, whole],
        scratch_shapes=[pltpu.VMEM((8, shape[0], 16, shape[2] // 2), F32), pltpu.SemaphoreType.DMA((8,))],
        input_output_aliases={count - 1: 0} if alias else {},
        compiler_params=pltpu.CompilerParams(vmem_limit_bytes=20 * MIB),
        cost_estimate=pl.CostEstimate(flops=1, bytes_accessed=1, transcendentals=0),
    )(pos, *arrays, *after)


def whole(x, keep, other):
    first = jnp.where(x == 0, keep, other)
    return jnp.concatenate([first, jnp.where(x == 0, other, keep)], axis=1)


def input_taps(ny, fields, depths, wt, cells, buf, out_rows):
    lanes = buf.shape[2] // 3
    for n, field in enumerate(fields):
        put_plane(buf, n, field, ny, True)
    acc = jnp.zeros((cells, wt.shape[1]), F32)
    for n, depth in enumerate(depths):
        for b in range(3):
            for c in range(3):
                lhs = buf[n, (2 - b) * ny : (2 - b) * ny + cells, c * lanes : (c + 1) * lanes]
                acc = acc + lax.dot_general(
                    lhs, wt[depth * 9 + b * 3 + c], (((1,), (1,)), ((), ())), preferred_element_type=F32
                )
    return acc.astype(BF)


def near_input_body(ny, pos, kn, on, kf, of, near, near_o, wt, act_n, act_f, out, act, buf):
    odd, x = pos[0], pos[6]
    fields = (whole(x, kf[...], of[...]), whole(x, kn[...], on[...]), whole(x, near[...], near_o[...]))
    out[...] = input_taps(ny, fields, (2 - 2 * odd, 1, 2 * odd), wt, kn.shape[0], buf, out)
    act[1 - odd] = act_n[...]
    act[odd] = act_f[...]


def far_input_body(inside, ny, pos, kn, on, kf, of, far, far_o, wt, ig_n, out, done, buf):
    odd, x, mine = pos[0], pos[6], pos[2]
    beyond = far[...]
    if inside:
        beyond = jnp.where((mine == 0) | (mine == 3), jnp.zeros_like(beyond), beyond)
    fields = (whole(x, kn[...], on[...]), whole(x, kf[...], of[...]), whole(x, beyond, far_o[...]))
    out[odd] = input_taps(ny, fields, (2 * odd, 1, 2 - 2 * odd), wt, kn.shape[0], buf, out)
    out[1 - odd] = ig_n[...]
    done[...] = jnp.zeros_like(done)


def per_device(volumes, weight, bias, cotangent):
    samples, planes, nx, ny, local_in = volumes.shape
    outputs = weight.shape[4]
    local_out = bias.shape[0]
    plane = nx * ny
    cells = planes * plane
    slabs = lax.axis_size("slab")
    s, z, y = lax.axis_index("slab"), lax.axis_index("dp"), lax.axis_index("chan")
    odd, mine, x = s % 2, s % 4, (s // 2) % 2
    near_depth, far_depth = 2 - 2 * odd, 2 * odd
    pos = jnp.stack([odd, y, mine, odd, z, z, x, near_depth, 0 * x]).astype(jnp.int32)
    pos_far = jnp.stack([odd, y, mine, odd, z, z, x, far_depth, 0 * x + 1]).astype(jnp.int32)
    factor = float(samples * cells * slabs * lax.axis_size("dp")) ** -0.5
    padded = plane + 2 * ny
    macs = plane * 27 * local_in * outputs

    def next_pair(value):
        pairs = [(i, i + 1) for i in range(1, slabs - 1, 2)]
        return lax.ppermute(value, "slab", pairs + [(j, i) for i, j in pairs])

    vol = volumes.reshape(planes, plane, local_in)
    w = weight.reshape(3, 9 * local_in, outputs)
    vol_n = jnp.where(odd == 0, vol[1], vol[0])
    vol_f = jnp.where(odd == 0, vol[0], vol[1])
    near, far = swap(vol_n, "slab", 1), next_pair(vol_f)
    ends = group_ends(vol, slabs)
    wide, thin = ((plane, local_out), F32), ((plane, local_out), BF)
    one = [pltpu.VMEM((1, padded, 3 * local_in), BF)]
    own_n, send_n, kept, held = vmem_call(
        functools.partial(near_body, ny),
        [wide, thin, ((2, padded, 3 * local_in), BF), (w.shape, BF)],
        one + [pltpu.SemaphoreType.DMA(())],
        macs,
        pos, near, vol_n, vol_f, w,
    )
    recv_n = swap(send_n, "chan", 1)
    own_f, send_f = vmem_call(functools.partial(outer_body, ny), [wide, thin], one, macs, pos_far, far, kept, held)
    recv_f = swap(send_f, "chan", 1)
    vol_x = swap(vol, "slab", 2)
    vol_c, vol_cx = swap(vol, "slab", 1), swap(vol_x, "slab", 1)

    bias_row, cot = bias.reshape(1, local_out), cotangent.reshape(planes, plane, local_out)
    act_n, g_n = vmem_call(near_gate_body, [thin, thin], [], 0, pos, own_n, recv_n, bias_row, cot)
    g_ny = swap(g_n, "chan", 1)
    act_f, g_f = vmem_call(far_gate_body, [thin, thin], [], 0, pos, own_f, recv_f, bias_row, cot, after=(g_n,))
    g_fy = swap(g_f, "chan", 1)
    lanes = 3 * local_out

    def routed(mine_g, other_g):
        keep, send = jnp.where(x == y, mine_g, other_g), jnp.where(x == y, other_g, mine_g)
        return keep, send, swap(send, "slab", 2)

    keep_n, send_n, got_n = routed(g_n, g_ny)
    core_n = swap(keep_n, "slab", 1), swap(got_n, "slab", 1)
    keep_f, send_f, got_f = routed(g_f, g_fy)
    vt = vmem_call(
        volume_body,
        [((4 * planes + 4, 3 * local_in // 2, plane), BF)],
        [],
        0,
        pos, vol, vol_c, vol_x, vol_cx, ends,
        after=(g_f,),
    )[0]
    acc_shape = (3, 3 * local_in // 2, lanes)
    buf = pltpu.VMEM((4, padded, lanes), BF)
    acc0, total0, sent = vmem_call(
        functools.partial(near_kernel_body, ny),
        [(acc_shape, F32), ((8, local_out), F32), thin],
        [buf],
        2 * macs,
        pos, vt, keep_n, core_n[0], got_n, core_n[1], keep_f,
    )
    core_f = swap(keep_f, "slab", 1), swap(pack(pos, got_f, after=(acc0,))[0], "slab", 1)
    pair = pltpu.VMEM((2, padded, lanes), BF)
    sums = [(acc_shape, F32), ((8, local_out), F32)]
    acc1, total1 = vmem_call(
        functools.partial(mid_kernel_body, ny), sums, [pair], macs, pos, vt, keep_f, got_f, acc0, total0
    )
    rows = 9 * local_in // 8
    cut = [((rows, lanes), F32)] + [((rows + 16, lanes), BF)] * 3
    if slabs == 4:
        keep, s1, s2, s3, total = vmem_call(
            functools.partial(last_kernel_body, ny),
            cut + [((8, local_out), F32)],
            [pair, pltpu.VMEM(acc_shape, F32)],
            macs,
            pos, vt, *core_f, acc1, total1,
        )
    else:
        acc, total = vmem_call(
            functools.partial(far_kernel_body, ny), sums, [pair], macs, pos, vt, *core_f, acc1, total1
        )
        bit = 4
        while bit < slabs:
            acc, total = acc + swap(acc, "slab", bit), total + swap(total, "slab", bit)
            bit *= 2
        keep, s1, s2, s3 = vmem_call(cut_body, cut, [], 0, pos, acc, total)
    r1, r2, r3 = swap(s1, "dp", 1), swap(s2, "dp", 2), swap(s3, "dp", 3)

    wt = weight.reshape(27, local_in, outputs)
    ig_buf = pltpu.VMEM((3, padded, 3 * outputs), BF)
    ig_n, act = vmem_call(
        functools.partial(near_input_body, ny),
        [((plane, local_in), BF), ((planes, plane, local_out), BF)],
        [ig_buf],
        2 * macs,
        pos, keep_n, send_n, keep_f, send_f, core_n[0], swap(send_n, "slab", 1), wt, act_n, act_f,
        after=(s1,),
    )
    far_keep = core_f[1]
    if slabs > 4:
        far_keep = jnp.where((mine == 0) | (mine == 3), next_pair(send_f), far_keep)
    ig, ig_done = vmem_call(
        functools.partial(far_input_body, slabs == 4, ny),
        [((planes, plane, local_in), BF), ((8, 128), F32)],
        [ig_buf],
        2 * macs,
        pos, keep_n, send_n, keep_f, send_f, far_keep, next_pair(sent), wt, ig_n,
        after=(s1,),
    )
    quarter, quarter_b, total3 = vmem_call(
        functools.partial(sum_body, factor),
        [((rows, lanes), BF), ((rows + 16, lanes), BF), ((8, local_out), F32)],
        [],
        0,
        pos, keep, r1, r2, r3, total,
        after=(ig_done,),
    )
    q1, q2, x0 = swap(quarter, "dp", 1), swap(quarter, "dp", 2), swap(quarter_b, "slab", 2)
    one_z, two_x, four_c = vmem_call(
        round_body,
        [(quarter.shape, BF), ((2,) + quarter.shape, BF), ((4,) + quarter.shape, BF)],
        [],
        0,
        pos, quarter, q1, q2, x0,
    )
    q3, x12, core = swap(one_z, "dp", 1), swap(two_x, "slab", 2), swap(four_c, "slab", 1)
    one_x, three_c = vmem_call(
        next_round_body, [(quarter.shape, BF), ((3,) + quarter.shape, BF)], [], 0, pos, q3, x12, after=(core,)
    )
    x3, core_b = swap(one_x, "slab", 2), swap(three_c, "slab", 1)
    out_shape = (27, local_in, outputs)
    token = (8, 128), F32
    out, _ = spread(first_spread_body, out_shape, token, (one_x,), pos, four_c, core)
    out, done = spread(next_spread_body, out_shape, token, (), pos, three_c, core_b, out, alias=True)
    core_x3 = swap(pack(pos, x3, after=(done,))[0], "slab", 1)
    last = (1, local_out), F32
    weight_grad, bias_grad = spread(
        last_spread_body, out_shape, last, (), pos, x0, x3, core_x3, total3, out, alias=True
    )
    shape = (samples, planes, nx, ny)
    return (
        act.reshape(shape + (local_out,)),
        ig.reshape(shape + (local_in,)),
        weight_grad.reshape(weight.shape),
        bias_grad[0],
    )


def group_ends(vol, slabs):
    before, after = jnp.zeros_like(vol[0]), jnp.zeros_like(vol[0])
    for group in range(4 if slabs > 4 else 0):
        up = [(i - 1, i + group) for i in range(4, slabs, 4)]
        down = [(i + 4, i + group) for i in range(0, slabs - 4, 4)]
        before = before + lax.ppermute(vol[vol.shape[0] - 1], "slab", up)
        after = after + lax.ppermute(vol[0], "slab", down)
    return jnp.stack([before, after])


def solution(mesh):
    placed = (
        P("dp", "slab", None, None, "chan"),
        P(None, None, None, "chan", None),
        P("chan"),
        P("dp", "slab", None, None, "chan"),
    )
    return jax.shard_map(
        per_device,
        mesh=mesh,
        in_specs=placed,
        out_specs=(
            P("dp", "slab", None, None, "chan"),
            P("dp", "slab", None, None, "chan"),
            P(None, None, None, "chan", None),
            P("chan"),
        ),
        check_vma=False,
    )
```

time: 188 us -> 83.4 us (0.44)
  waiting for transfers between devices: 72.2 us -> 19.7 us
  blocking collectives: 38.3 us -> 0 us
  Pallas kernels: 0 us -> 27 us
  local copies, waits for them, and re-layouts: 26.8 us -> 1.7 us
  starting transfers between devices: 13 us -> 32.4 us
  between operations: 14.4 us -> 1.13 us
  matrix products: 10.8 us -> 0 us
  other arithmetic: 10.3 us -> 1.04 us
    psum x1 -> x0, waiting for transfers between devices: 64.4 us -> none  [per_device(): kernel_sum, bias_sum = lax.psum((stacked, bias_term), ('dp', 'slab'))]
    psum x1 -> x0, blocking collectives: 30.4 us -> none  [per_device(): kernel_sum, bias_sum = lax.psum((stacked, bias_term), ('dp', 'slab'))]
    pallas_call x0 -> x18, Pallas kernels: none -> 27 us  [the longest x15 21 us: vmem_call(): pl.pallas_call(inner, out_shape=shapes, in_specs=[pl.BlockSpec(memory_spa...]
    ppermute x4 -> x29, starting transfers between devices: 12.9 us -> 32.4 us  [the longest x27 25.8 us: swap(): lax.ppermute(value, axis, [(i, i ^ bit) for i in range(lax.axis_size(axis...]
    ppermute x4 -> x29, waiting for transfers between devices: 1.57 us -> 19.7 us  [the longest x27 19.7 us: swap(): lax.ppermute(value, axis, [(i, i ^ bit) for i in range(lax.axis_size(axis...]
    dot_general x9 -> x0, matrix products: 10.8 us -> none  [the longest x3 4.9 us: per_device(): accum = accum + jnp.dot(block, flipped, preferred_element_type=jnp.float32)]
    reshape x3 -> x0, local copies, waits for them, and re-layouts: 9.43 us -> none  [plane_patches(): return block.reshape(-1, block.shape[4])]
    all_gather x1 -> x0, blocking collectives: 7.96 us -> none  [per_device(): lax.all_gather(grad_pre.reshape(samples, planes, rows_x, rows_y, local_ou...]
  transfers between devices with their start and end apart: 6 -> 29, of which waited for: 3 -> 12; matrix products, arithmetic and copies ran while one was open for 15% -> 0% of each run, Pallas kernels for 0% -> 27%
where the time goes in v2:
time: 83.4 us; the launch traced here: 82.9 us
  starting transfers between devices  32.4 us (39%)
  Pallas kernels  27 us (32%)
  waiting for transfers between devices  19.7 us (24%)
  local copies, waits for them, and re-layouts  1.7 us (2%)
  between operations  1.13 us (1%)
  other arithmetic  1.04 us (1%)
    ppermute x27, starting transfers between devices, swap(): lax.ppermute(value, axis, [(i, i ^ bit) for i in range(lax.axis_size(axis...  25.8 us
    pallas_call x15, Pallas kernels, vmem_call(): pl.pallas_call(inner, out_shape=shapes, in_specs=[pl.BlockSpec(memory_spa...  21 us
    ppermute x27, waiting for transfers between devices, swap(): lax.ppermute(value, axis, [(i, i ^ bit) for i in range(lax.axis_size(axis...  19.7 us
    ppermute x2, starting transfers between devices, next_pair(): return lax.ppermute(value, 'slab', pairs + [(j, i) for i, j in pairs])  6.55 us
    pallas_call x3, Pallas kernels, spread(): pl.pallas_call(inner, out_shape=[jax.ShapeDtypeStruct(shape, F32), jax.Sh...  5.98 us
  transfers between devices with their start and end apart: 29, of which 12 were waited for; matrix products, arithmetic and copies ran while one was open for 0% of the time, Pallas kernels for 27%

profile of v2, /device:TPU:1, one launch (start us, length us, event | category | flops | bytes accessed | tf_op | source)
XLA Modules:
  0.0 82.9 jit_solution(17906147418134623867)
XLA Ops:
  1.8 4.5 %collective-permute-start.3 = (bf16[512,128]{1,0:T(8,128)(2,1)S(1)}, bf16[512,128]{1,0:T(8,128)(2,1)S(1)}, u32[]{:S(2)}, u32[]{:S(2)}) collective-permute-start(bf16[512,128]{1,0:T(8,128)(2,1)S(1)} %bitcast.23), channel_id=1, source_target_pairs={{2,4},{4,2},{3,5},{5,3},{10,12},{12,10},{11,13},{13,11},{18,20},{2... | collective-permute-start | bytes 393224 | tf_op jit(solution)/shard_map/ppermute | solution.py:346
  6.5 1.5 %copy-done.1 = bf16[3,3,3,128,256]{4,3,2,1,0:T(8,128)(2,1)S(1)} copy-done((bf16[3,3,3,128,256]{4,3,2,1,0:T(8,128)(2,1)S(1)}, bf16[3,3,3,128,256]{4,3,2,1,0:T(8,128)(2,1)}, u32[]{:S(2)}) %copy-start.1) | copy-done | bytes 1769496
  7.9 2.4 %shard_map.75 = (f32[512,128]{1,0:T(8,128)S(1)}, bf16[512,128]{1,0:T(8,128)(2,1)S(1)}, bf16[2,544,384]{2,1,0:T(8,128)(2,1)S(1)}, bf16[3,1152,256]{2,1,0:T(8,128)(2,1)S(1)}) custom-call(s32[9]{0:T(128)S(1)} %stack.45.refs_0_, bf16[512,128]{1,0:T(8,128)(2,1)S(1)} %collective-permute-done.refs_1_, bf16[512,128]{1,0:T(8,128)(2,1)S(1)} %bitcast.26, ...), custom_call_target="tpu_custom_call" | custom-call | flops 2811939328 | bytes 1048576 | tf_op jit(solution)/shard_map/pallas_call | solution.py:27
  11.7 1.7 %shard_map.77 = (f32[512,128]{1,0:T(8,128)S(1)}, bf16[512,128]{1,0:T(8,128)(2,1)S(1)}) custom-call(s32[9]{0:T(128)S(1)} %stack.47.refs_0_, bf16[512,128]{1,0:T(8,128)(2,1)S(1)} %collective-permute-done.3.refs_1_, bf16[2,544,384]{2,1,0:T(8,128)(2,1)S(1)} %get-tuple-element.44.refs_2_, bf16[3,1152,256]{2,1,0:T(8,128)(2,1)S(1)} %get-tuple-element.45.refs_3_), custom_call_target="tpu_custom_call" | custom-call | flops 2811939328 | bytes 1048576 | tf_op jit(solution)/shard_map/pallas_call | solution.py:27
  15.3 2.3 %collective-permute-start.2 = (bf16[512,128]{1,0:T(8,128)(2,1)S(1)}, bf16[512,128]{1,0:T(8,128)(2,1)S(1)}, u32[]{:S(2)}, u32[]{:S(2)}) collective-permute-start(bf16[512,128]{1,0:T(8,128)(2,1)S(1)} %get-tuple-element.43.refs_5_), channel_id=1, source_target_pairs={{0,1},{1,0},{2,3},{3,2},{4,5},{5,4},{6,7},{7,6},{8,9},{9,8},{10,11... | collective-permute-start | bytes 393224 | tf_op jit(solution)/shard_map/ppermute | solution.py:16
  20.5 3.5 %collective-permute-start.8 = (bf16[2,512,128]{2,1,0:T(8,128)(2,1)S(1)}, bf16[2,512,128]{2,1,0:T(8,128)(2,1)S(1)}, u32[]{:S(2)}, u32[]{:S(2)}) collective-permute-start(bf16[2,512,128]{2,1,0:T(8,128)(2,1)S(1)} %bitcast.21), channel_id=1, source_target_pairs={{0,2},{2,0},{4,6},{6,4},{1,3},{3,1},{5,7},{7,5},{8,10},{10,8},{12,... | collective-permute-start | bytes 786440 | tf_op jit(solution)/shard_map/ppermute | solution.py:16
  25.0 2.2 %collective-permute-start.10 = (bf16[2,512,128]{2,1,0:T(8,128)(2,1)S(1)}, bf16[2,512,128]{2,1,0:T(8,128)(2,1)S(1)}, u32[]{:S(2)}, u32[]{:S(2)}) collective-permute-start(bf16[2,512,128]{2,1,0:T(8,128)(2,1)S(1)} %collective-permute-done.9.refs_3_), channel_id=1, source_target_pairs={{0,2},{2,0},{4,6},{6,4},{1,3},{3,1},{5,7},{7,5},{8,10},{10,8},{12,... | collective-permute-start | bytes 786440 | tf_op jit(solution)/shard_map/ppermute | solution.py:16
  30.6 2.2 %shard_map.80 = (f32[3,192,384]{2,1,0:T(8,128)S(1)}, f32[8,128]{1,0:T(8,128)S(1)}, bf16[512,128]{1,0:T(8,128)(2,1)S(1)}) custom-call(s32[9]{0:T(128)S(1)} %stack.45.refs_0_, bf16[12,192,512]{2,1,0:T(8,128)(2,1)S(1)} %shard_map.79.refs_1_, bf16[512,128]{1,0:T(8,128)(2,1)S(1)} %get-tuple-element.81.refs_2_.refs_1_, ...), custom_call_target="tpu_custom_call" | custom-call | flops 4623878656 | bytes 1048576 | tf_op jit(solution)/shard_map/pallas_call | solution.py:27
  32.7 1.6 %collective-permute-done.12.refs_1_.refs_3_ = bf16[512,128]{1,0:T(8,128)(2,1)S(1)} collective-permute-done((bf16[512,128]{1,0:T(8,128)(2,1)S(1)}, bf16[512,128]{1,0:T(8,128)(2,1)S(1)}, u32[]{:S(2)}, u32[]{:S(2)}) %collective-permute-start.12) | collective-permute-done | bytes 131104 | tf_op jit(solution)/shard_map/ppermute | solution.py:16
  35.8 2.1 %collective-permute-start.16 = (bf16[512,128]{1,0:T(8,128)(2,1)S(1)}, bf16[512,128]{1,0:T(8,128)(2,1)S(1)}, u32[]{:S(2)}, u32[]{:S(2)}) collective-permute-start(bf16[512,128]{1,0:T(8,128)(2,1)S(1)} %get-tuple-element.57), channel_id=1, source_target_pairs={{2,4},{4,2},{3,5},{5,3},{10,12},{12,10},{11,13},{13,11},{18,20},{2... | collective-permute-start | bytes 393224 | tf_op jit(solution)/shard_map/ppermute | solution.py:346
  37.9 1.5 %shard_map.82 = (f32[3,192,384]{2,1,0:T(8,128)S(1)}, f32[8,128]{1,0:T(8,128)S(1)}) custom-call(s32[9]{0:T(128)S(1)} %stack.45.refs_0_, bf16[12,192,512]{2,1,0:T(8,128)(2,1)S(1)} %shard_map.79.refs_1_, bf16[512,128]{1,0:T(8,128)(2,1)S(1)} %get-tuple-element.79.refs_6_.refs_2_.refs_3_, bf16[512,128]{1,0:T(8,128)(2,1)S(1)} %collective-permute-done.12.refs_1_.refs_3_, ...), custom_call_target="tpu_custom_call" | custom-call | flops 2811939328 | bytes 1048576 | tf_op jit(solution)/shard_map/pallas_call | solution.py:27
  39.4 1.5 %shard_map.83 = (f32[144,384]{1,0:T(8,128)S(1)}, bf16[160,384]{1,0:T(8,128)(2,1)S(1)}, bf16[160,384]{1,0:T(8,128)(2,1)S(1)}, bf16[160,384]{1,0:T(8,128)(2,1)S(1)}, f32[8,128]{1,0:T(8,128)S(1)}) custom-call(s32[9]{0:T(128)S(1)} %stack.45.refs_0_, bf16[12,192,512]{2,1,0:T(8,128)(2,1)S(1)} %shard_map.79.refs_1_, ...), custom_call_target="tpu_custom_call" | custom-call | flops 2811939328 | bytes 1048576 | tf_op jit(solution)/shard_map/pallas_call | solution.py:27
  40.9 2.2 %collective-permute-start.18 = (bf16[160,384]{1,0:T(8,128)(2,1)S(1)}, bf16[160,384]{1,0:T(8,128)(2,1)S(1)}, u32[]{:S(2)}, u32[]{:S(2)}) collective-permute-start(bf16[160,384]{1,0:T(8,128)(2,1)S(1)} %get-tuple-element.61), channel_id=1, source_target_pairs={{0,16},{8,24},{16,0},{24,8},{1,17},{9,25},{17,1},{25,9},{2,18},{10... | collective-permute-start | bytes 368648 | tf_op jit(solution)/shard_map/ppermute | solution.py:16
  44.4 3.2 %shard_map.84 = (bf16[512,128]{1,0:T(8,128)(2,1)S(1)}, bf16[2,512,128]{2,1,0:T(8,128)(2,1)}) custom-call(s32[9]{0:T(128)S(1)} %stack.45.refs_0_, bf16[512,128]{1,0:T(8,128)(2,1)S(1)} %get-tuple-element.81.refs_2_.refs_1_, bf16[512,128]{1,0:T(8,128)(2,1)S(1)} %get-tuple-element.80.refs_2_, bf16[512,128]{1,0:T(8,128)(2,1)S(1)} %get-tuple-element.79.refs_6_.refs_2_.refs_3_, ...), custom_call_target="tpu_custom_call" | custom-call | flops 4623878656 | bytes 1048576 | tf_op jit(solution)/shard_map/pallas_call | solution.py:27
  47.6 3.3 %shard_map.85 = (bf16[2,512,128]{2,1,0:T(8,128)(2,1)}, f32[8,128]{1,0:T(8,128)S(1)}) custom-call(s32[9]{0:T(128)S(1)} %stack.45.refs_0_, bf16[512,128]{1,0:T(8,128)(2,1)S(1)} %get-tuple-element.81.refs_2_.refs_1_, bf16[512,128]{1,0:T(8,128)(2,1)S(1)} %get-tuple-element.80.refs_2_, bf16[512,128]{1,0:T(8,128)(2,1)S(1)} %get-tuple-element.79.refs_6_.refs_2_.refs_3_, ...), custom_call_target="tpu_custom_call" | custom-call | flops 4623878656 | bytes 1048576 | tf_op jit(solution)/shard_map/pallas_call | solution.py:27
  54.1 2.8 %collective-permute-start.22 = (bf16[144,384]{1,0:T(8,128)(2,1)S(1)}, bf16[144,384]{1,0:T(8,128)(2,1)S(1)}, u32[]{:S(2)}, u32[]{:S(2)}) collective-permute-start(bf16[144,384]{1,0:T(8,128)(2,1)S(1)} %get-tuple-element.66.refs_1_), channel_id=1, source_target_pairs={{0,16},{8,24},{16,0},{24,8},{1,17},{9,25},{17,1},{25,9},{2,18},{10... | collective-permute-start | bytes 331784 | tf_op jit(solution)/shard_map/ppermute | solution.py:16
  56.9 5.5 %collective-permute-done.22.refs_3_ = bf16[144,384]{1,0:T(8,128)(2,1)S(1)} collective-permute-done((bf16[144,384]{1,0:T(8,128)(2,1)S(1)}, bf16[144,384]{1,0:T(8,128)(2,1)S(1)}, u32[]{:S(2)}, u32[]{:S(2)}) %collective-permute-start.22) | collective-permute-done | bytes 110624 | tf_op jit(solution)/shard_map/ppermute | solution.py:16
  63.0 1.9 %collective-permute-start.25 = (bf16[4,144,384]{2,1,0:T(8,128)(2,1)S(1)}, bf16[4,144,384]{2,1,0:T(8,128)(2,1)S(1)}, u32[]{:S(2)}, u32[]{:S(2)}) collective-permute-start(bf16[4,144,384]{2,1,0:T(8,128)(2,1)S(1)} %get-tuple-element.69.refs_1_), channel_id=1, source_target_pairs={{0,2},{2,0},{4,6},{6,4},{1,3},{3,1},{5,7},{7,5},{8,10},{10,8},{12,... | collective-permute-start | bytes 1327112 | tf_op jit(solution)/shard_map/ppermute | solution.py:16
  64.9 1.4 %collective-permute-start.24 = (bf16[2,144,384]{2,1,0:T(8,128)(2,1)S(1)}, bf16[2,144,384]{2,1,0:T(8,128)(2,1)S(1)}, u32[]{:S(2)}, u32[]{:S(2)}) collective-permute-start(bf16[2,144,384]{2,1,0:T(8,128)(2,1)S(1)} %get-tuple-element.68), channel_id=1, source_target_pairs={{0,4},{2,6},{4,0},{6,2},{1,5},{3,7},{5,1},{7,3},{8,12},{10,14},{12... | collective-permute-start | bytes 663560 | tf_op jit(solution)/shard_map/ppermute | solution.py:16
  66.8 3.8 %collective-permute-done.23.refs_1_ = bf16[144,384]{1,0:T(8,128)(2,1)S(1)} collective-permute-done((bf16[144,384]{1,0:T(8,128)(2,1)S(1)}, bf16[144,384]{1,0:T(8,128)(2,1)S(1)}, u32[]{:S(2)}, u32[]{:S(2)}) %collective-permute-start.23) | collective-permute-done | bytes 110624 | tf_op jit(solution)/shard_map/ppermute | solution.py:16
  73.4 1.4 %collective-permute-start.26 = (bf16[144,384]{1,0:T(8,128)(2,1)S(1)}, bf16[144,384]{1,0:T(8,128)(2,1)S(1)}, u32[]{:S(2)}, u32[]{:S(2)}) collective-permute-start(bf16[144,384]{1,0:T(8,128)(2,1)S(1)} %get-tuple-element.70.refs_3_), channel_id=1, source_target_pairs={{0,4},{2,6},{4,0},{6,2},{1,5},{3,7},{5,1},{7,3},{8,12},{10,14},{12... | collective-permute-start | bytes 331784 | tf_op jit(solution)/shard_map/ppermute | solution.py:16
  74.8 2.4 %shard_map.89 = (f32[27,128,256]{2,1,0:T(8,128)}, f32[8,128]{1,0:T(8,128)}) custom-call(s32[9]{0:T(128)S(1)} %stack.45.refs_0_, bf16[4,144,384]{2,1,0:T(8,128)(2,1)S(1)} %get-tuple-element.69.refs_1_, bf16[4,144,384]{2,1,0:T(8,128)(2,1)S(1)} %collective-permute-done.25.refs_3_.refs_2_, bf16[144,384]{1,0:T(8,128)(2,1)S(1)} %get-tuple-element.70.refs_3_), custom_call_target="tpu_custom_call" | custom-call | flops 1 | bytes 1 | tf_op jit(solution)/shard_map/pallas_call | solution.py:277
  77.2 1.7 %shard_map.90 = (f32[27,128,256]{2,1,0:T(8,128)}, f32[8,128]{1,0:T(8,128)S(1)}) custom-call(s32[9]{0:T(128)S(1)} %stack.45.refs_0_, bf16[3,144,384]{2,1,0:T(8,128)(2,1)S(1)} %get-tuple-element.71.refs_1_, bf16[3,144,384]{2,1,0:T(8,128)(2,1)S(1)} %collective-permute-done.27.refs_2_, ...), custom_call_target="tpu_custom_call", output_to_operand_aliasing={{0}: (3, {})} | custom-call | flops 1 | bytes 1 | tf_op jit(solution)/shard_map/pallas_call | solution.py:277
  80.9 1.9 %shard_map.92 = (f32[27,128,256]{2,1,0:T(8,128)}, f32[1,128]{1,0:T(1,128)}) custom-call(s32[9]{0:T(128)S(1)} %stack.45.refs_0_, bf16[160,384]{1,0:T(8,128)(2,1)S(1)} %collective-permute-done.20.refs_4_.refs_1_, bf16[144,384]{1,0:T(8,128)(2,1)S(1)} %collective-permute-done.26.refs_1_.refs_2_, ...), custom_call_target="tpu_custom_call", output_to_operand_aliasing={{0}: (5, {})} | custom-call | flops 1 | bytes 1 | tf_op jit(solution)/shard_map/pallas_call | solution.py:277
  (68 shorter events, 23.5 us)
Async XLA Ops:
  1.6 4.8 %collective-permute-start = (bf16[512,128]{1,0:T(8,128)(2,1)S(1)}, bf16[512,128]{1,0:T(8,128)(2,1)S(1)}, u32[]{:S(2)}, u32[]{:S(2)}) collective-permute-start(bf16[512,128]{1,0:T(8,128)(2,1)S(1)} %bitcast.25), channel_id=1, source_target_pairs={{0,2},{2,0},{4,6},{6,4},{1,3},{3,1},{5,7},{7,5},{8,10},{10,8},{12,... | collective-permute-start | bytes 393224 | tf_op jit(solution)/shard_map/ppermute | solution.py:16
  1.8 9.9 %collective-permute-start.3 = (bf16[512,128]{1,0:T(8,128)(2,1)S(1)}, bf16[512,128]{1,0:T(8,128)(2,1)S(1)}, u32[]{:S(2)}, u32[]{:S(2)}) collective-permute-start(bf16[512,128]{1,0:T(8,128)(2,1)S(1)} %bitcast.23), channel_id=1, source_target_pairs={{2,4},{4,2},{3,5},{5,3},{10,12},{12,10},{11,13},{13,11},{18,20},{2... | collective-permute-start | bytes 393224 | tf_op jit(solution)/shard_map/ppermute | solution.py:346
  13.4 5.4 %collective-permute-start.4 = (bf16[512,128]{1,0:T(8,128)(2,1)S(1)}, bf16[512,128]{1,0:T(8,128)(2,1)S(1)}, u32[]{:S(2)}, u32[]{:S(2)}) collective-permute-start(bf16[512,128]{1,0:T(8,128)(2,1)S(1)} %get-tuple-element.47), channel_id=1, source_target_pairs={{0,1},{1,0},{2,3},{3,2},{4,5},{5,4},{6,7},{7,6},{8,9},{9,8},{10,11... | collective-permute-start | bytes 393224 | tf_op jit(solution)/shard_map/ppermute | solution.py:16
  15.3 5.0 %collective-permute-start.2 = (bf16[512,128]{1,0:T(8,128)(2,1)S(1)}, bf16[512,128]{1,0:T(8,128)(2,1)S(1)}, u32[]{:S(2)}, u32[]{:S(2)}) collective-permute-start(bf16[512,128]{1,0:T(8,128)(2,1)S(1)} %get-tuple-element.43.refs_5_), channel_id=1, source_target_pairs={{0,1},{1,0},{2,3},{3,2},{4,5},{5,4},{6,7},{7,6},{8,9},{9,8},{10,11... | collective-permute-start | bytes 393224 | tf_op jit(solution)/shard_map/ppermute | solution.py:16
  17.6 7.4 %collective-permute-start.9 = (bf16[2,512,128]{2,1,0:T(8,128)(2,1)S(1)}, bf16[2,512,128]{2,1,0:T(8,128)(2,1)S(1)}, u32[]{:S(2)}, u32[]{:S(2)}) collective-permute-start(bf16[2,512,128]{2,1,0:T(8,128)(2,1)S(1)} %bitcast.20), channel_id=1, source_target_pairs={{0,4},{2,6},{4,0},{6,2},{1,5},{3,7},{5,1},{7,3},{8,12},{10,14},{12... | collective-permute-start | bytes 786440 | tf_op jit(solution)/shard_map/ppermute | solution.py:16
  19.5 7.7 %collective-permute-start.5 = (bf16[512,128]{1,0:T(8,128)(2,1)S(1)}, bf16[512,128]{1,0:T(8,128)(2,1)S(1)}, u32[]{:S(2)}, u32[]{:S(2)}) collective-permute-start(bf16[512,128]{1,0:T(8,128)(2,1)S(1)} %get-tuple-element.48.refs_6_), channel_id=1, source_target_pairs={{0,1},{1,0},{2,3},{3,2},{4,5},{5,4},{6,7},{7,6},{8,9},{9,8},{10,11... | collective-permute-start | bytes 393224 | tf_op jit(solution)/shard_map/ppermute | solution.py:16
  20.4 7.4 %collective-permute-start.13 = (bf16[512,128]{1,0:T(8,128)(2,1)S(1)}, bf16[512,128]{1,0:T(8,128)(2,1)S(1)}, u32[]{:S(2)}, u32[]{:S(2)}) collective-permute-start(bf16[512,128]{1,0:T(8,128)(2,1)S(1)} %get-tuple-element.80.refs_2_), channel_id=1, source_target_pairs={{0,4},{2,6},{4,0},{6,2},{1,5},{3,7},{5,1},{7,3},{8,12},{10,14},{12... | collective-permute-start | bytes 393224 | tf_op jit(solution)/shard_map/ppermute | solution.py:16
  20.5 8.7 %collective-permute-start.8 = (bf16[2,512,128]{2,1,0:T(8,128)(2,1)S(1)}, bf16[2,512,128]{2,1,0:T(8,128)(2,1)S(1)}, u32[]{:S(2)}, u32[]{:S(2)}) collective-permute-start(bf16[2,512,128]{2,1,0:T(8,128)(2,1)S(1)} %bitcast.21), channel_id=1, source_target_pairs={{0,2},{2,0},{4,6},{6,4},{1,3},{3,1},{5,7},{7,5},{8,10},{10,8},{12,... | collective-permute-start | bytes 786440 | tf_op jit(solution)/shard_map/ppermute | solution.py:16
  27.2 17.1 %collective-permute-start.7 = (bf16[512,128]{1,0:T(8,128)(2,1)S(1)}, bf16[512,128]{1,0:T(8,128)(2,1)S(1)}, u32[]{:S(2)}, u32[]{:S(2)}) collective-permute-start(bf16[512,128]{1,0:T(8,128)(2,1)S(1)} %get-tuple-element.80.refs_2_), channel_id=1, source_target_pairs={{0,2},{2,0},{4,6},{6,4},{1,3},{3,1},{5,7},{7,5},{8,10},{10,8},{12,... | collective-permute-start | bytes 393224 | tf_op jit(solution)/shard_map/ppermute | solution.py:16
  29.2 5.2 %collective-permute-start.12 = (bf16[512,128]{1,0:T(8,128)(2,1)S(1)}, bf16[512,128]{1,0:T(8,128)(2,1)S(1)}, u32[]{:S(2)}, u32[]{:S(2)}) collective-permute-start(bf16[512,128]{1,0:T(8,128)(2,1)S(1)} %get-tuple-element.78.refs_4_), channel_id=1, source_target_pairs={{0,4},{2,6},{4,0},{6,2},{1,5},{3,7},{5,1},{7,3},{8,12},{10,14},{12... | collective-permute-start | bytes 393224 | tf_op jit(solution)/shard_map/ppermute | solution.py:16
  29.3 10.1 %collective-permute-start.11 = (bf16[512,128]{1,0:T(8,128)(2,1)S(1)}, bf16[512,128]{1,0:T(8,128)(2,1)S(1)}, u32[]{:S(2)}, u32[]{:S(2)}) collective-permute-start(bf16[512,128]{1,0:T(8,128)(2,1)S(1)} %get-tuple-element.79.refs_6_.refs_2_.refs_3_), channel_id=1, source_target_pairs={{0,2},{2,0},{4,6},{6,4},{1,3},{3,1},{5,7},{7,5},{8,10},{10,8},{12,... | collective-permute-start | bytes 393224 | tf_op jit(solution)/shard_map/ppermute | solution.py:16
  34.9 4.4 %collective-permute-start.15 = (bf16[512,128]{1,0:T(8,128)(2,1)S(1)}, bf16[512,128]{1,0:T(8,128)(2,1)S(1)}, u32[]{:S(2)}, u32[]{:S(2)}) collective-permute-start(bf16[512,128]{1,0:T(8,128)(2,1)S(1)} %bitcast.32), channel_id=1, source_target_pairs={{0,2},{2,0},{4,6},{6,4},{1,3},{3,1},{5,7},{7,5},{8,10},{10,8},{12,... | collective-permute-start | bytes 393224 | tf_op jit(solution)/shard_map/ppermute | solution.py:16
  35.8 11.8 %collective-permute-start.16 = (bf16[512,128]{1,0:T(8,128)(2,1)S(1)}, bf16[512,128]{1,0:T(8,128)(2,1)S(1)}, u32[]{:S(2)}, u32[]{:S(2)}) collective-permute-start(bf16[512,128]{1,0:T(8,128)(2,1)S(1)} %get-tuple-element.57), channel_id=1, source_target_pairs={{2,4},{4,2},{3,5},{5,3},{10,12},{12,10},{11,13},{13,11},{18,20},{2... | collective-permute-start | bytes 393224 | tf_op jit(solution)/shard_map/ppermute | solution.py:346
  40.9 11.1 %collective-permute-start.18 = (bf16[160,384]{1,0:T(8,128)(2,1)S(1)}, bf16[160,384]{1,0:T(8,128)(2,1)S(1)}, u32[]{:S(2)}, u32[]{:S(2)}) collective-permute-start(bf16[160,384]{1,0:T(8,128)(2,1)S(1)} %get-tuple-element.61), channel_id=1, source_target_pairs={{0,16},{8,24},{16,0},{24,8},{1,17},{9,25},{17,1},{25,9},{2,18},{10... | collective-permute-start | bytes 368648 | tf_op jit(solution)/shard_map/ppermute | solution.py:16
  43.1 9.0 %collective-permute-start.19 = (bf16[160,384]{1,0:T(8,128)(2,1)S(1)}, bf16[160,384]{1,0:T(8,128)(2,1)S(1)}, u32[]{:S(2)}, u32[]{:S(2)}) collective-permute-start(bf16[160,384]{1,0:T(8,128)(2,1)S(1)} %get-tuple-element.62), channel_id=1, source_target_pairs={{0,24},{8,16},{16,8},{24,0},{1,25},{9,17},{17,9},{25,1},{2,26},{10... | collective-permute-start | bytes 368648 | tf_op jit(solution)/shard_map/ppermute | solution.py:16
  44.1 9.2 %collective-permute-start.17 = (bf16[160,384]{1,0:T(8,128)(2,1)S(1)}, bf16[160,384]{1,0:T(8,128)(2,1)S(1)}, u32[]{:S(2)}, u32[]{:S(2)}) collective-permute-start(bf16[160,384]{1,0:T(8,128)(2,1)S(1)} %get-tuple-element.55.refs_10_.refs_9_), channel_id=1, source_target_pairs={{0,8},{8,0},{16,24},{24,16},{1,9},{9,1},{17,25},{25,17},{2,10},{10... | collective-permute-start | bytes 368648 | tf_op jit(solution)/shard_map/ppermute | solution.py:16
  54.0 8.4 %collective-permute-start.20 = (bf16[160,384]{1,0:T(8,128)(2,1)S(1)}, bf16[160,384]{1,0:T(8,128)(2,1)S(1)}, u32[]{:S(2)}, u32[]{:S(2)}) collective-permute-start(bf16[160,384]{1,0:T(8,128)(2,1)S(1)} %get-tuple-element.65), channel_id=1, source_target_pairs={{0,4},{2,6},{4,0},{6,2},{1,5},{3,7},{5,1},{7,3},{8,12},{10,14},{12... | collective-permute-start | bytes 368648 | tf_op jit(solution)/shard_map/ppermute | solution.py:16
  54.1 8.3 %collective-permute-start.22 = (bf16[144,384]{1,0:T(8,128)(2,1)S(1)}, bf16[144,384]{1,0:T(8,128)(2,1)S(1)}, u32[]{:S(2)}, u32[]{:S(2)}) collective-permute-start(bf16[144,384]{1,0:T(8,128)(2,1)S(1)} %get-tuple-element.66.refs_1_), channel_id=1, source_target_pairs={{0,16},{8,24},{16,0},{24,8},{1,17},{9,25},{17,1},{25,9},{2,18},{10... | collective-permute-start | bytes 331784 | tf_op jit(solution)/shard_map/ppermute | solution.py:16
  56.9 5.5 %collective-permute-start.21 = (bf16[144,384]{1,0:T(8,128)(2,1)S(1)}, bf16[144,384]{1,0:T(8,128)(2,1)S(1)}, u32[]{:S(2)}, u32[]{:S(2)}) collective-permute-start(bf16[144,384]{1,0:T(8,128)(2,1)S(1)} %get-tuple-element.66.refs_1_), channel_id=1, source_target_pairs={{0,8},{8,0},{16,24},{24,16},{1,9},{9,1},{17,25},{25,17},{2,10},{10... | collective-permute-start | bytes 331784 | tf_op jit(solution)/shard_map/ppermute | solution.py:16
  63.0 8.9 %collective-permute-start.25 = (bf16[4,144,384]{2,1,0:T(8,128)(2,1)S(1)}, bf16[4,144,384]{2,1,0:T(8,128)(2,1)S(1)}, u32[]{:S(2)}, u32[]{:S(2)}) collective-permute-start(bf16[4,144,384]{2,1,0:T(8,128)(2,1)S(1)} %get-tuple-element.69.refs_1_), channel_id=1, source_target_pairs={{0,2},{2,0},{4,6},{6,4},{1,3},{3,1},{5,7},{7,5},{8,10},{10,8},{12,... | collective-permute-start | bytes 1327112 | tf_op jit(solution)/shard_map/ppermute | solution.py:16
  64.9 7.0 %collective-permute-start.24 = (bf16[2,144,384]{2,1,0:T(8,128)(2,1)S(1)}, bf16[2,144,384]{2,1,0:T(8,128)(2,1)S(1)}, u32[]{:S(2)}, u32[]{:S(2)}) collective-permute-start(bf16[2,144,384]{2,1,0:T(8,128)(2,1)S(1)} %get-tuple-element.68), channel_id=1, source_target_pairs={{0,4},{2,6},{4,0},{6,2},{1,5},{3,7},{5,1},{7,3},{8,12},{10,14},{12... | collective-permute-start | bytes 663560 | tf_op jit(solution)/shard_map/ppermute | solution.py:16
  66.3 4.3 %collective-permute-start.23 = (bf16[144,384]{1,0:T(8,128)(2,1)S(1)}, bf16[144,384]{1,0:T(8,128)(2,1)S(1)}, u32[]{:S(2)}, u32[]{:S(2)}) collective-permute-start(bf16[144,384]{1,0:T(8,128)(2,1)S(1)} %get-tuple-element.67), channel_id=1, source_target_pairs={{0,8},{8,0},{16,24},{24,16},{1,9},{9,1},{17,25},{25,17},{2,10},{10... | collective-permute-start | bytes 331784 | tf_op jit(solution)/shard_map/ppermute | solution.py:16
  72.5 4.7 %collective-permute-start.27 = (bf16[3,144,384]{2,1,0:T(8,128)(2,1)S(1)}, bf16[3,144,384]{2,1,0:T(8,128)(2,1)S(1)}, u32[]{:S(2)}, u32[]{:S(2)}) collective-permute-start(bf16[3,144,384]{2,1,0:T(8,128)(2,1)S(1)} %get-tuple-element.71.refs_1_), channel_id=1, source_target_pairs={{0,2},{2,0},{4,6},{6,4},{1,3},{3,1},{5,7},{7,5},{8,10},{10,8},{12,... | collective-permute-start | bytes 995336 | tf_op jit(solution)/shard_map/ppermute | solution.py:16
  73.4 5.5 %collective-permute-start.26 = (bf16[144,384]{1,0:T(8,128)(2,1)S(1)}, bf16[144,384]{1,0:T(8,128)(2,1)S(1)}, u32[]{:S(2)}, u32[]{:S(2)}) collective-permute-start(bf16[144,384]{1,0:T(8,128)(2,1)S(1)} %get-tuple-element.70.refs_3_), channel_id=1, source_target_pairs={{0,4},{2,6},{4,0},{6,2},{1,5},{3,7},{5,1},{7,3},{8,12},{10,14},{12... | collective-permute-start | bytes 331784 | tf_op jit(solution)/shard_map/ppermute | solution.py:16
  (10 other events, 32.5 us)

commit v3 on v2

v3 whole, which is shorter than its diff:
```python
import functools

import jax
import jax.numpy as jnp
from jax import lax
from jax.experimental import pallas as pl
from jax.experimental.pallas import tpu as pltpu
from jax.sharding import PartitionSpec as P

BF = jnp.bfloat16
F32 = jnp.float32
MIB = 1 << 20


def swap(value, axis, bit):
    return lax.ppermute(value, axis, [(i, i ^ bit) for i in range(lax.axis_size(axis))])


def vmem_call(body, outs, scratch, flops, *args, left=(), after=(), limit=20):
    shapes = [jax.ShapeDtypeStruct(s, d) for s, d in outs]
    count, waited = len(args), len(after)

    def inner(*refs):
        body(*refs[:count], *refs[count + waited :])

    specs = [pl.BlockSpec(memory_space=pl.ANY if n in left else pltpu.VMEM) for n in range(1, count)]
    return pl.pallas_call(
        inner,
        out_shape=shapes,
        in_specs=[pl.BlockSpec(memory_space=pltpu.SMEM)] + specs + [pl.BlockSpec(memory_space=pl.ANY)] * waited,
        out_specs=[pl.BlockSpec(memory_space=pltpu.VMEM)] * len(shapes),
        scratch_shapes=scratch,
        compiler_params=pltpu.CompilerParams(vmem_limit_bytes=limit * MIB),
        cost_estimate=pl.CostEstimate(flops=4 * flops + 10**9, bytes_accessed=MIB, transcendentals=0),
    )(*args, *after)


def shift_y(value, step, ny):
    rows = value.shape[0]
    y = lax.broadcasted_iota(jnp.int32, value.shape, 0) % ny
    rolled = pltpu.roll(value, (-step) % rows, 0)
    return jnp.where(y == (0 if step < 0 else ny - 1), 0.0, rolled)


def put_plane(buf, at, value, ny, flip):
    cells, lanes = value.shape
    wide = value.astype(F32)
    edge = jnp.zeros((ny, 3 * lanes), BF)
    buf[at, 0:ny, :] = edge
    buf[at, ny + cells : 2 * ny + cells, :] = edge
    for c in range(3):
        step = (1 - c) if flip else (c - 1)
        moved = value if step == 0 else shift_y(wide, step, ny).astype(BF)
        buf[at, ny : ny + cells, c * lanes : (c + 1) * lanes] = moved


def near_body(ny, pos, vol_n, vol_f, plane, w, own, send, kept, held, done, buf, sem):
    copy = pltpu.make_async_copy(w, held, sem)
    copy.start()
    put_plane(kept, 0, vol_n[...], ny, False)
    put_plane(kept, 1, vol_f[...], ny, False)
    put_plane(buf, 0, plane[...], ny, False)
    sums(ny, pos, kept.at[0], kept.at[1], buf.at[0], 2 - 2 * pos[0], w, own, send)
    done[...] = jnp.zeros_like(done)
    copy.wait()


def far_body(ny, pos, beyond, kept, w, own, send, buf):
    odd = pos[0]
    put_plane(buf, 0, jnp.where(pos[7] == 0, 0.0, beyond[...].astype(F32)).astype(BF), ny, False)
    sums(ny, pos, kept.at[1], kept.at[0], buf.at[0], 2 * odd, w, own, send)


def sums(ny, pos, middle, inner, outer, depth, w, own, send):
    cells = own.shape[0]
    y, half = pos[1], own.shape[1]
    total = tap(middle, w, 1, ny, cells) + tap(inner, w, 2 - depth, ny, cells) + tap(outer, w, depth, ny, cells)
    own[...] = jnp.where(y == 0, total[:, :half], total[:, half:])
    send[...] = jnp.where(y == 0, total[:, half:], total[:, :half]).astype(BF)


def tap(field, w, depth, ny, cells):
    lhs = jnp.concatenate([field[b * ny : b * ny + cells, :] for b in range(3)], axis=1)
    return jnp.dot(lhs, w[depth], preferred_element_type=F32)


def gate(pos, plane, own, recv, bias, cot):
    pre = own[...] + recv[...].astype(F32) + bias[...].astype(F32)
    s = 1.0 / (1.0 + jnp.exp(-pre))
    return (pre * s).astype(BF), (cot[plane].astype(F32) * s * (1.0 + pre * (1.0 - s))).astype(BF)


def near_gate_body(pos, own, recv, bias, cot, vol_n, act, grad, vol_out):
    act[...], grad[...] = gate(pos, 1 - pos[0], own, recv, bias, cot)
    vol_out[...] = vol_n[...]


def far_gate_body(pos, own, recv, bias, cot, act, grad):
    act[...], grad[...] = gate(pos, pos[0], own, recv, bias, cot)


def held_back(value, *tokens):
    rows, lanes = value.shape
    ready = functools.reduce(jnp.logical_and, [token == token for token in tokens])
    blocks = value.reshape(rows // 8, 8, lanes)
    return jnp.where(ready[None], blocks, jnp.zeros_like(blocks)).reshape(rows, lanes)


def volume_body(pos, n0, f0, n1, f1, n2, f2, n3, f3, ends, vt):
    lanes = n0.shape[1]
    mine, k, odd = pos[2], pos[3], pos[0]
    keep = lanes // 2

    def put(at, value):
        turned = value.astype(F32).T
        turned = jnp.where(k == 0, turned[:keep], turned[keep:]).astype(BF)
        for a in range(3):
            vt[at + 2 - a, a * keep : (a + 1) * keep, :] = turned

    put(0, ends[0])
    put(9, ends[1])
    for who, (near, far) in enumerate(((n0, f0), (n1, f1), (n2, f2), (n3, f3))):
        own_odd = odd if who in (0, 2) else 1 - odd
        put((mine ^ who) * 2 + (1 - own_odd) + 1, near[...])
        put((mine ^ who) * 2 + own_odd + 1, far[...])


def kernel_terms(ny, pos, vt, grads, buf, acc, before):
    cells, lanes = grads[0][2].shape
    mine, odd = pos[2], pos[0]
    bsum = jnp.zeros((1, lanes), F32)
    where = []
    for n, (far, who, ref) in enumerate(grads):
        own_odd = odd if who in (0, 2) else 1 - odd
        where.append((mine ^ who) * 2 + (own_odd if far else 1 - own_odd) + 2)
        value = ref[...]
        put_plane(buf, n, value, ny, True)
        bsum = bsum + jnp.sum(value.astype(F32), axis=0, keepdims=True)
    lhs = jnp.concatenate([vt[at] for at in where], axis=1)
    for b in range(3):
        rhs = [buf[n, (2 - b) * ny : (2 - b) * ny + cells, :] for n in range(len(grads))]
        summed = jnp.dot(lhs, jnp.concatenate(rhs, axis=0), preferred_element_type=F32)
        acc[b] = summed if before is None else summed + before[b]
    return bsum


def first_kernel_body(ny, pos, vt, g0, g1, f0, f1, acc, total, buf):
    grads = ((0, 0, g0), (0, 1, g1), (1, 0, f0), (1, 1, f1))
    bsum = kernel_terms(ny, pos, vt, grads, buf, acc, None)
    total[...] = jnp.broadcast_to(jnp.concatenate([bsum] * 3, axis=1), total.shape)


def second_kernel_body(ny, pos, vt, g2, g3, acc0, total0, acc, total, buf):
    bsum = kernel_terms(ny, pos, vt, ((0, 2, g2), (0, 3, g3)), buf, acc, acc0)
    total[...] = total0[...] + jnp.concatenate([bsum] * 3, axis=1)


def next_kernel_body(who, ny, pos, vt, f, acc0, total0, acc, total, buf):
    bsum = kernel_terms(ny, pos, vt, ((1, who, f),), buf, acc, acc0)
    total[...] = total0[...] + jnp.concatenate([bsum] * 3, axis=1)


def last_kernel_body(ny, pos, vt, f3, acc0, total0, kf, keep, s1, s2, s3, total, sent, buf, acc):
    sent[...] = kf[...]
    next_kernel_body(3, ny, pos, vt, f3, acc0, total0, acc, total, buf)
    cut_body(pos, acc, keep, s1, s2, s3)


def cut_body(pos, acc, keep, s1, s2, s3):
    part = keep.shape[0] // 9
    mine = pos[4]
    for b in range(3):
        for a in range(3):
            rows = slice((3 * b + a) * part, (3 * b + a + 1) * part)
            for who, ref in ((0, keep), (1, s1), (2, s2), (3, s3)):
                at = pl.multiple_of((4 * a + (mine ^ who)) * part, part)
                ref[rows, :] = acc[b, pl.ds(at, part), :].astype(ref.dtype)


def place(pos, pieces, out, wide, sems):
    x, k, mine = pos[6], pos[3], pos[4]
    half = out.shape[2] // 2
    copies = []
    for n, (who, j, piece) in enumerate(pieces):
        for b in range(3):
            for a in range(3):
                for c in range(3):
                    rows = slice((3 * b + a) * 16, (3 * b + a + 1) * 16)
                    wide[n, (a * 3 + b) * 3 + c] = piece[rows, c * half : (c + 1) * half].astype(F32)
        row = pl.multiple_of((k ^ (who >> 1)) * 64 + (mine ^ j) * 16, 16)
        lane = pl.multiple_of((x ^ (who & 1)) * half, half)
        copy = pltpu.make_async_copy(wide.at[n], out.at[:, pl.ds(row, 16), pl.ds(lane, half)], sems.at[n])
        copy.start()
        copies.append(copy)
    for copy in copies:
        copy.wait()


def round_body(pos, q, q1, x0, q2, one_z, two_x, four_c):
    one_z[...] = q2[...]
    two_x[0], two_x[1] = q1[...], q2[...]
    four_c[0], four_c[1], four_c[2], four_c[3] = q[...], q1[...], q2[...], x0[...]


def next_round_body(pos, q3, x12, one_x, three_c):
    one_x[...] = q3[...]
    three_c[0], three_c[1], three_c[2] = q3[...], x12[0], x12[1]


def first_spread_body(pos, own, core, out, done, wide, sems):
    kinds = ((0, 0), (0, 1), (0, 2), (1, 0))
    pieces = [(who, j, own.at[n]) for n, (who, j) in enumerate(kinds)]
    pieces += [(who + 2, j, core.at[n]) for n, (who, j) in enumerate(kinds)]
    place(pos, pieces, out, wide, sems)
    done[...] = jnp.zeros_like(done)


def next_spread_body(pos, own, core, before, out, done, wide, sems):
    kinds = ((0, 3), (1, 1), (1, 2))
    pieces = [(who, j, own.at[n]) for n, (who, j) in enumerate(kinds)]
    pieces += [(who + 2, j, core.at[n]) for n, (who, j) in enumerate(kinds)]
    place(pos, pieces, out, wide, sems)
    done[...] = jnp.zeros_like(done)


def last_spread_body(pos, x3, cx3, before, out, done, wide, sems):
    place(pos, [(1, 3, x3), (3, 3, cx3)], out, wide, sems)
    done[...] = jnp.zeros_like(done)


def spread(body, shape, small, after, pos, *arrays, alias=False):
    whole = pl.BlockSpec(memory_space=pltpu.VMEM)
    anywhere = pl.BlockSpec(memory_space=pl.ANY)
    count, waited = 1 + len(arrays), len(after)

    def inner(*refs):
        body(*refs[:count], *refs[count + waited :])

    specs = [pl.BlockSpec(memory_space=pltpu.SMEM)] + [whole] * (len(arrays) - alias) + [anywhere] * alias
    return pl.pallas_call(
        inner,
        out_shape=[jax.ShapeDtypeStruct(shape, F32), jax.ShapeDtypeStruct(*small)],
        in_specs=specs + [anywhere] * waited,
        out_specs=[anywhere, whole],
        scratch_shapes=[pltpu.VMEM((8, shape[0], 16, shape[2] // 2), F32), pltpu.SemaphoreType.DMA((8,))],
        input_output_aliases={count - 1: 0} if alias else {},
        compiler_params=pltpu.CompilerParams(vmem_limit_bytes=20 * MIB),
        cost_estimate=pl.CostEstimate(flops=1, bytes_accessed=1, transcendentals=0),
    )(pos, *arrays, *after)


def whole(x, keep, other):
    first = jnp.where(x == 0, keep, other)
    return jnp.concatenate([first, jnp.where(x == 0, other, keep)], axis=1)


def input_taps(ny, depth, wt, buf, at):
    cells = buf.shape[1] - 2 * ny
    lanes = buf.shape[2] // 3
    acc = jnp.zeros((cells, wt.shape[1]), F32)
    for b in range(3):
        for c in range(3):
            lhs = buf[at, (2 - b) * ny : (2 - b) * ny + cells, c * lanes : (c + 1) * lanes]
            acc = acc + lax.dot_general(
                lhs, wt[depth * 9 + b * 3 + c], (((1,), (1,)), ((), ())), preferred_element_type=F32
            )
    return acc


def near_input_body(ny, pos, kn, on, kf, of, near, near_o, wt, act_n, act_f, out, partial, act, done, buf):
    odd, x = pos[0], pos[6]
    put_plane(buf, 0, whole(x, kn[...], on[...]), ny, True)
    put_plane(buf, 1, whole(x, kf[...], of[...]), ny, True)
    put_plane(buf, 2, whole(x, near[...], near_o[...]), ny, True)
    total = input_taps(ny, 1, wt, buf, 0) + input_taps(ny, 2 - 2 * odd, wt, buf, 1)
    out[...] = (total + input_taps(ny, 2 * odd, wt, buf, 2)).astype(BF)
    partial[...] = input_taps(ny, 1, wt, buf, 1) + input_taps(ny, 2 * odd, wt, buf, 0)
    done[...] = jnp.zeros_like(done)
    act[1 - odd] = act_n[...]
    act[odd] = act_f[...]


def far_input_body(inside, ny, pos, far, far_o, wt, partial, ig_n, out, done, buf):
    odd, x, mine = pos[0], pos[6], pos[2]
    beyond = whole(x, far[...], far_o[...])
    if inside:
        beyond = jnp.where((mine == 0) | (mine == 3), jnp.zeros_like(beyond), beyond)
    put_plane(buf, 0, beyond, ny, True)
    out[odd] = (partial[...] + input_taps(ny, 2 - 2 * odd, wt, buf, 0)).astype(BF)
    out[1 - odd] = ig_n[...]
    done[...] = jnp.zeros_like(done)


def per_device(volumes, weight, bias, cotangent):
    samples, planes, nx, ny, local_in = volumes.shape
    outputs = weight.shape[4]
    local_out = bias.shape[0]
    plane = nx * ny
    cells = planes * plane
    slabs = lax.axis_size("slab")
    s, z, y = lax.axis_index("slab"), lax.axis_index("dp"), lax.axis_index("chan")
    odd, mine, x = s % 2, s % 4, (s // 2) % 2
    beside = jnp.where((s == 0) | (s == slabs - 1), 0, 1)
    pos = jnp.stack([odd, y, mine, odd, z, z, x, beside]).astype(jnp.int32)
    factor = float(samples * cells * slabs * lax.axis_size("dp")) ** -0.5
    padded = plane + 2 * ny
    macs = plane * 27 * local_in * outputs

    def next_pair(value):
        pairs = [(i, i + 1) for i in range(1, slabs - 1, 2)]
        return lax.ppermute(value, "slab", pairs + [(j, i) for i, j in pairs])

    vol = volumes.reshape(planes, plane, local_in)
    w = weight.reshape(3, 9 * local_in, outputs)
    vol_n = jnp.where(odd == 0, vol[1], vol[0])
    vol_f = jnp.where(odd == 0, vol[0], vol[1])
    near, x_f = swap(vol_n, "slab", 1), swap(vol_f, "slab", 2)
    ends = group_ends(vol, slabs)
    wide, thin = ((plane, local_out), F32), ((plane, local_out), BF)
    one = [pltpu.VMEM((1, padded, 3 * local_in), BF)]
    own_n, send_n, kept, held, done_n = vmem_call(
        functools.partial(near_body, ny),
        [wide, thin, ((2, padded, 3 * local_in), BF), (w.shape, BF), ((8, 128), F32)],
        one + [pltpu.SemaphoreType.DMA(())],
        macs,
        pos, vol_n, vol_f, near, w,
    )
    recv_n = swap(send_n, "chan", 1)
    cx_f = swap(held_back(x_f, done_n), "slab", 1)
    beyond = cx_f
    if slabs > 4:
        beyond = jnp.where((mine == 0) | (mine == 3), next_pair(vol_f), beyond)
    own_f, send_f = vmem_call(functools.partial(far_body, ny), [wide, thin], one, macs, pos, beyond, kept, held)
    recv_f = swap(send_f, "chan", 1)

    bias_row, cot = bias.reshape(1, local_out), cotangent.reshape(planes, plane, local_out)
    act_n, g_n, vol_n2 = vmem_call(
        near_gate_body, [thin, thin, thin], [], 0, pos, own_n, recv_n, bias_row, cot, vol_n
    )
    x_n, core_vf = swap(vol_n2, "slab", 2), swap(vol_f, "slab", 1)
    cx_n = swap(x_n, "slab", 1)
    g_ny = swap(g_n, "chan", 1)
    vt = vmem_call(
        volume_body,
        [((4 * planes + 4, 3 * local_in // 2, plane), BF)],
        [],
        0,
        pos, vol_n, vol_f, near, core_vf, x_n, x_f, cx_n, cx_f, ends,
    )[0]
    act_f, g_f = vmem_call(far_gate_body, [thin, thin], [], 0, pos, own_f, recv_f, bias_row, cot, after=(g_n,))
    g_fy = swap(g_f, "chan", 1)
    lanes = 3 * local_out

    def routed(mine_g, other_g):
        keep, send = jnp.where(x == y, mine_g, other_g), jnp.where(x == y, other_g, mine_g)
        return keep, send, swap(send, "slab", 2)

    keep_n, send_n, got_n = routed(g_n, g_ny)
    core_n = swap(keep_n, "slab", 1), swap(got_n, "slab", 1)
    keep_f, send_f, got_f = routed(g_f, g_fy)
    acc_shape = (3, 3 * local_in // 2, lanes)
    core_f = swap(keep_f, "slab", 1)
    sums_of = [(acc_shape, F32), ((8, lanes), F32)]
    four, two = pltpu.VMEM((4, padded, lanes), BF), pltpu.VMEM((2, padded, lanes), BF)
    first = functools.partial(first_kernel_body, ny)
    acc0, total0 = vmem_call(first, sums_of, [four], 2 * macs, pos, vt, keep_n, core_n[0], keep_f, core_f)
    second = functools.partial(second_kernel_body, ny)
    acc0, total0 = vmem_call(second, sums_of, [two], macs, pos, vt, got_n, core_n[1], acc0, total0)
    last_f = swap(held_back(got_f, total0[:, :local_out]), "slab", 1)
    single = pltpu.VMEM((1, padded, lanes), BF)
    acc1, total1 = vmem_call(
        functools.partial(next_kernel_body, 2, ny), sums_of, [single], macs, pos, vt, got_f, acc0, total0
    )
    rows = 9 * local_in // 8
    cut = [((rows, lanes), F32), ((rows, lanes), BF), ((rows, lanes), F32), ((rows, lanes), BF)]
    if slabs == 4:
        keep, s1, s2, s3, total, sent = vmem_call(
            functools.partial(last_kernel_body, ny),
            cut + [((8, lanes), F32), thin],
            [single, pltpu.VMEM(acc_shape, F32)],
            macs,
            pos, vt, last_f, acc1, total1, keep_f,
        )
    else:
        acc, total = vmem_call(
            functools.partial(next_kernel_body, 3, ny), sums_of, [single], macs, pos, vt, last_f, acc1, total1
        )
        bit = 4
        while bit < slabs:
            acc, total = acc + swap(acc, "slab", bit), total + swap(total, "slab", bit)
            bit *= 2
        keep, s1, s2, s3 = vmem_call(cut_body, cut, [], 0, pos, acc)
        sent = keep_f
    r3, total_z = swap(s3, "dp", 1), swap(total, "dp", 1)
    merged, total_b = (s2 + r3.astype(F32)).astype(BF), total + total_z
    r2, r1, total_z2 = swap(merged, "dp", 2), swap(held_back(s1, total_z), "dp", 1), swap(total_b, "dp", 2)

    sent_x = swap(sent, "slab", 2)
    wt = weight.reshape(27, local_in, outputs)
    ig_buf = pltpu.VMEM((3, padded, 3 * outputs), BF)
    ig_n, partial, act, ig_n_done = vmem_call(
        functools.partial(near_input_body, ny),
        [
            ((plane, local_in), BF), ((plane, local_in), F32), ((planes, plane, local_out), BF), ((8, lanes), F32)
        ],
        [ig_buf],
        2 * macs,
        pos, keep_n, send_n, keep_f, send_f, core_n[0], swap(send_n, "slab", 1), wt, act_n, act_f,
        after=(merged, sent_x),
    )
    far_keep = last_f
    far_send = swap(sent_x, "slab", 1)
    if slabs > 4:
        edge = (mine == 0) | (mine == 3)
        far_keep = jnp.where(edge, next_pair(send_f), far_keep)
        far_send = jnp.where(edge, next_pair(keep_f), far_send)
    ig, ig_done = vmem_call(
        functools.partial(far_input_body, slabs == 4, ny),
        [((planes, plane, local_in), BF), ((8, lanes), F32)],
        [pltpu.VMEM((1, padded, 3 * outputs), BF)],
        0,
        pos, far_keep, far_send, wt, partial, ig_n,
    )
    quarter = held_back(((keep + r1.astype(F32) + r2.astype(F32)) * factor).astype(BF), ig_n_done)
    total3 = (total_b + total_z2) * factor
    q1, q2, x0 = swap(quarter, "dp", 1), swap(quarter, "dp", 2), swap(quarter, "slab", 2)
    total_x = swap(total3, "slab", 2)
    out_shape = (27, local_in, outputs)
    token = (8, lanes), F32
    one_z, two_x, four_c = vmem_call(
        round_body,
        [(quarter.shape, BF), ((2,) + quarter.shape, BF), ((4,) + quarter.shape, BF)],
        [],
        0,
        pos, quarter, q1, x0, q2,
        after=(total_x,),
    )
    q3, x12, core = swap(one_z, "dp", 1), swap(two_x, "slab", 2), swap(four_c, "slab", 1)
    out, done = spread(first_spread_body, out_shape, token, (), pos, four_c, core)
    one_x, three_c = vmem_call(
        next_round_body, [(quarter.shape, BF), ((3,) + quarter.shape, BF)], [], 0, pos, q3, x12, after=(done, ig_done)
    )
    x3, core_b = swap(one_x, "slab", 2), swap(three_c, "slab", 1)
    out, done = spread(next_spread_body, out_shape, token, (), pos, three_c, core_b, out, alias=True)
    core_x3 = swap(held_back(x3, done), "slab", 1)
    weight_grad, _ = spread(last_spread_body, out_shape, token, (), pos, x3, core_x3, out, alias=True)
    bias_grad = jnp.where(x == y, total3, total_x)[0, :local_out]
    shape = (samples, planes, nx, ny)
    return (
        act.reshape(shape + (local_out,)),
        ig.reshape(shape + (local_in,)),
        weight_grad.reshape(weight.shape),
        bias_grad,
    )


def group_ends(vol, slabs):
    before, after = jnp.zeros_like(vol[0]), jnp.zeros_like(vol[0])
    for group in range(4 if slabs > 4 else 0):
        up = [(i - 1, i + group) for i in range(4, slabs, 4)]
        down = [(i + 4, i + group) for i in range(0, slabs - 4, 4)]
        before = before + lax.ppermute(vol[vol.shape[0] - 1], "slab", up)
        after = after + lax.ppermute(vol[0], "slab", down)
    return jnp.stack([before, after])


def solution(mesh):
    placed = (
        P("dp", "slab", None, None, "chan"),
        P(None, None, None, "chan", None),
        P("chan"),
        P("dp", "slab", None, None, "chan"),
    )
    return jax.shard_map(
        per_device,
        mesh=mesh,
        in_specs=placed,
        out_specs=(
            P("dp", "slab", None, None, "chan"),
            P("dp", "slab", None, None, "chan"),
            P(None, None, None, "chan", None),
            P("chan"),
        ),
        check_vma=False,
    )
```

time: 83.4 us -> 75.7 us (0.908)
  waiting for transfers between devices: 19.7 us -> 11.2 us
  starting transfers between devices: 32.4 us -> 34.6 us
  Pallas kernels: 27 us -> 25.2 us
    ppermute x27 -> x34, starting transfers between devices: 25.8 us -> 34.6 us  [swap(): lax.ppermute(value, axis, [(i, i ^ bit) for i in range(lax.axis_size(axis...]
    ppermute x27 -> x34, waiting for transfers between devices: 19.7 us -> 11.2 us  [swap(): lax.ppermute(value, axis, [(i, i ^ bit) for i in range(lax.axis_size(axis...]
    ppermute x2 -> x0, starting transfers between devices: 6.55 us -> none  [next_pair(): return lax.ppermute(value, 'slab', pairs + [(j, i) for i, j in pairs])]
    pallas_call x15 -> x13, Pallas kernels: 21 us -> 19.7 us  [vmem_call(): pl.pallas_call(inner, out_shape=shapes, in_specs=[pl.BlockSpec(memory_spa...]
  transfers between devices with their start and end apart: 29 -> 34, of which waited for: 12 -> 11; matrix products, arithmetic and copies ran while one was open for 0% -> 1% of each run, Pallas kernels for 27% -> 28%
where the time goes in v3:
time: 75.7 us; the launch traced here: 75.2 us
  starting transfers between devices  34.6 us (46%)
  Pallas kernels  25.2 us (33%)
  waiting for transfers between devices  11.2 us (15%)
  other arithmetic  1.75 us (2%)
  local copies, waits for them, and re-layouts  1.61 us (2%)
  between operations  0.91 us (1%)
    ppermute x34, starting transfers between devices, swap(): lax.ppermute(value, axis, [(i, i ^ bit) for i in range(lax.axis_size(axis...  34.6 us
    pallas_call x13, Pallas kernels, vmem_call(): pl.pallas_call(inner, out_shape=shapes, in_specs=[pl.BlockSpec(memory_spa...  19.7 us
    ppermute x34, waiting for transfers between devices, swap(): lax.ppermute(value, axis, [(i, i ^ bit) for i in range(lax.axis_size(axis...  11.2 us
    pallas_call x3, Pallas kernels, spread(): pl.pallas_call(inner, out_shape=[jax.ShapeDtypeStruct(shape, F32), jax.Sh...  5.47 us
  transfers between devices with their start and end apart: 34, of which 11 were waited for; matrix products, arithmetic and copies ran while one was open for 1% of the time, Pallas kernels for 28%

profile of v3, /device:TPU:1, one launch (start us, length us, event | category | flops | bytes accessed | tf_op | source)
XLA Modules:
  0.0 75.2 jit_solution(12840304715760523345)
XLA Ops:
  1.8 2.7 %collective-permute-start.3 = (bf16[512,128]{1,0:T(8,128)(2,1)S(1)}, bf16[512,128]{1,0:T(8,128)(2,1)S(1)}, u32[]{:S(2)}, u32[]{:S(2)}) collective-permute-start(bf16[512,128]{1,0:T(8,128)(2,1)S(1)} %bitcast.27), channel_id=1, source_target_pairs={{0,4},{2,6},{4,0},{6,2},{1,5},{3,7},{5,1},{7,3},{8,12},{10,14},{12... | collective-permute-start | bytes 393224 | tf_op jit(solution)/shard_map/ppermute | solution.py:16
  4.5 1.5 %copy-done = bf16[3,3,3,128,256]{4,3,2,1,0:T(8,128)(2,1)S(1)} copy-done((bf16[3,3,3,128,256]{4,3,2,1,0:T(8,128)(2,1)S(1)}, bf16[3,3,3,128,256]{4,3,2,1,0:T(8,128)(2,1)}, u32[]{:S(2)}) %copy-start) | copy-done | bytes 1769496
  6.0 2.1 %shard_map.75 = (f32[512,128]{1,0:T(8,128)S(1)}, bf16[512,128]{1,0:T(8,128)(2,1)S(1)}, bf16[2,544,384]{2,1,0:T(8,128)(2,1)S(1)}, bf16[3,1152,256]{2,1,0:T(8,128)(2,1)S(1)}, f32[8,128]{1,0:T(8,128)S(1)}) custom-call(s32[8]{0:T(128)S(1)} %stack.32.refs_0_, bf16[512,128]{1,0:T(8,128)(2,1)S(1)} %bitcast.32, bf16[512,128]{1,0:T(8,128)(2,1)S(1)} %bitcast.28, ...), custom_call_target="tpu_custom_call" | custom-call | flops 2811939328 | bytes 1048576 | tf_op jit(solution)/shard_map/pallas_call | solution.py:27
  9.0 1.5 %collective-permute-start.1 = (bf16[512,128]{1,0:T(8,128)(2,1)S(1)}, bf16[512,128]{1,0:T(8,128)(2,1)S(1)}, u32[]{:S(2)}, u32[]{:S(2)}) collective-permute-start(bf16[512,128]{1,0:T(8,128)(2,1)S(1)} %get-tuple-element.45), channel_id=1, source_target_pairs={{0,1},{1,0},{2,3},{3,2},{4,5},{5,4},{6,7},{7,6},{8,9},{9,8},{10,11... | collective-permute-start | bytes 393224 | tf_op jit(solution)/shard_map/ppermute | solution.py:16
  10.5 1.7 %shard_map.77 = (f32[512,128]{1,0:T(8,128)S(1)}, bf16[512,128]{1,0:T(8,128)(2,1)S(1)}) custom-call(s32[8]{0:T(128)S(1)} %stack.32.refs_0_, bf16[512,128]{1,0:T(8,128)(2,1)S(1)} %collective-permute-done.4.refs_1_.refs_8_, bf16[2,544,384]{2,1,0:T(8,128)(2,1)S(1)} %get-tuple-element.48.refs_2_, bf16[3,1152,256]{2,1,0:T(8,128)(2,1)S(1)} %get-tuple-element.49.refs_3_), custom_call_target="tpu_custom_call" | custom-call | flops 2811939328 | bytes 1048576 | tf_op jit(solution)/shard_map/pallas_call | solution.py:27
  14.8 1.5 %collective-permute-start.2 = (bf16[512,128]{1,0:T(8,128)(2,1)S(1)}, bf16[512,128]{1,0:T(8,128)(2,1)S(1)}, u32[]{:S(2)}, u32[]{:S(2)}) collective-permute-start(bf16[512,128]{1,0:T(8,128)(2,1)S(1)} %get-tuple-element.46.refs_5_), channel_id=1, source_target_pairs={{0,1},{1,0},{2,3},{3,2},{4,5},{5,4},{6,7},{7,6},{8,9},{9,8},{10,11... | collective-permute-start | bytes 393224 | tf_op jit(solution)/shard_map/ppermute | solution.py:16
  20.6 2.0 %collective-permute-start.7 = (bf16[512,128]{1,0:T(8,128)(2,1)S(1)}, bf16[512,128]{1,0:T(8,128)(2,1)S(1)}, u32[]{:S(2)}, u32[]{:S(2)}) collective-permute-start(bf16[512,128]{1,0:T(8,128)(2,1)S(1)} %get-tuple-element.87.refs_2_.refs_1_), channel_id=1, source_target_pairs={{0,2},{2,0},{4,6},{6,4},{1,3},{3,1},{5,7},{7,5},{8,10},{10,8},{12,... | collective-permute-start | bytes 393224 | tf_op jit(solution)/shard_map/ppermute | solution.py:16
  27.2 2.2 %shard_map.80 = (f32[3,192,384]{2,1,0:T(8,128)S(1)}, f32[8,384]{1,0:T(8,128)S(1)}) custom-call(s32[8]{0:T(128)S(1)} %stack.32.refs_0_, bf16[12,192,512]{2,1,0:T(8,128)(2,1)S(1)} %shard_map.79.refs_1_, bf16[512,128]{1,0:T(8,128)(2,1)S(1)} %get-tuple-element.87.refs_2_.refs_1_, bf16[512,128]{1,0:T(8,128)(2,1)S(1)} %collective-permute-done.7.refs_3_.refs_5_, ...), custom_call_target="tpu_custom_call" | custom-call | flops 4623878656 | bytes 1048576 | tf_op jit(solution)/shard_map/pallas_call | solution.py:27
  29.3 1.5 %shard_map.81 = (f32[3,192,384]{2,1,0:T(8,128)S(1)}, f32[8,384]{1,0:T(8,128)S(1)}) custom-call(s32[8]{0:T(128)S(1)} %stack.32.refs_0_, bf16[12,192,512]{2,1,0:T(8,128)(2,1)S(1)} %shard_map.79.refs_1_, bf16[512,128]{1,0:T(8,128)(2,1)S(1)} %collective-permute-done.12.refs_2_, bf16[512,128]{1,0:T(8,128)(2,1)S(1)} %collective-permute-done.13.refs_3_, ...), custom_call_target="tpu_custom_call" | custom-call | flops 2811939328 | bytes 1048576 | tf_op jit(solution)/shard_map/pallas_call | solution.py:27
  33.7 1.4 %collective-permute-start.20 = (f32[8,384]{1,0:T(8,128)S(1)}, f32[8,384]{1,0:T(8,128)S(1)}, u32[]{:S(2)}, u32[]{:S(2)}) collective-permute-start(f32[8,384]{1,0:T(8,128)S(1)} %get-tuple-element.71), channel_id=1, source_target_pairs={{0,8},{8,0},{16,24},{24,16},{1,9},{9,1},{17,25},{25,17},{2,10},{10... | collective-permute-start | bytes 36872 | tf_op jit(solution)/shard_map/ppermute | solution.py:16
  36.7 2.3 %collective-permute-start.26 = (f32[8,384]{1,0:T(8,128)S(1)}, f32[8,384]{1,0:T(8,128)S(1)}, u32[]{:S(2)}, u32[]{:S(2)}) collective-permute-start(f32[8,384]{1,0:T(8,128)S(1)} %add.32), channel_id=1, source_target_pairs={{0,16},{8,24},{16,0},{24,8},{1,17},{9,25},{17,1},{25,9},{2,18},{10... | collective-permute-start | bytes 36872 | tf_op jit(solution)/shard_map/ppermute | solution.py:16
  39.1 1.4 %collective-permute-start.21 = (bf16[144,384]{1,0:T(8,128)(2,1)S(1)}, bf16[144,384]{1,0:T(8,128)(2,1)S(1)}, u32[]{:S(2)}, u32[]{:S(2)}) collective-permute-start(bf16[144,384]{1,0:T(8,128)(2,1)S(1)} %bitcast_select_fusion.3), channel_id=1, source_target_pairs={{0,8},{8,0},{16,24},{24,16},{1,9},{9,1},{17,25},{25,17},{2,10},{10... | collective-permute-start | bytes 331784 | tf_op jit(solution)/shard_map/ppermute | solution.py:16
  40.5 2.2 %collective-permute-start.22 = (bf16[144,384]{1,0:T(8,128)(2,1)S(1)}, bf16[144,384]{1,0:T(8,128)(2,1)S(1)}, u32[]{:S(2)}, u32[]{:S(2)}) collective-permute-start(bf16[144,384]{1,0:T(8,128)(2,1)S(1)} %add_convert_fusion.refs_10_), channel_id=1, source_target_pairs={{0,16},{8,24},{16,0},{24,8},{1,17},{9,25},{17,1},{25,9},{2,18},{10... | collective-permute-start | bytes 331784 | tf_op jit(solution)/shard_map/ppermute | solution.py:16
  42.7 4.4 %shard_map.84 = (bf16[512,128]{1,0:T(8,128)(2,1)S(1)}, f32[512,128]{1,0:T(8,128)S(1)}, bf16[2,512,128]{2,1,0:T(8,128)(2,1)}, f32[8,384]{1,0:T(8,128)S(1)}) custom-call(s32[8]{0:T(128)S(1)} %stack.32.refs_0_, bf16[512,128]{1,0:T(8,128)(2,1)S(1)} %get-tuple-element.87.refs_2_.refs_1_, bf16[512,128]{1,0:T(8,128)(2,1)S(1)} %get-tuple-element.86.refs_2_, ...), custom_call_target="tpu_custom_call" | custom-call | flops 4623878656 | bytes 1048576 | tf_op jit(solution)/shard_map/pallas_call | solution.py:27
  47.2 1.5 %collective-permute-start.25 = (bf16[144,384]{1,0:T(8,128)(2,1)S(1)}, bf16[144,384]{1,0:T(8,128)(2,1)S(1)}, u32[]{:S(2)}, u32[]{:S(2)}) collective-permute-start(bf16[144,384]{1,0:T(8,128)(2,1)S(1)} %bitcast_select_fusion.4.refs_1_), channel_id=1, source_target_pairs={{0,16},{8,24},{16,0},{24,8},{1,17},{9,25},{17,1},{25,9},{2,18},{10... | collective-permute-start | bytes 331784 | tf_op jit(solution)/shard_map/ppermute | solution.py:16
  50.3 2.1 %collective-permute-done.27.refs_5_ = f32[8,384]{1,0:T(8,128)S(1)} collective-permute-done((f32[8,384]{1,0:T(8,128)S(1)}, f32[8,384]{1,0:T(8,128)S(1)}, u32[]{:S(2)}, u32[]{:S(2)}) %collective-permute-start.27) | collective-permute-done | bytes 12320 | tf_op jit(solution)/shard_map/ppermute | solution.py:16
  53.1 2.7 %collective-permute-done.23.refs_2_ = bf16[144,384]{1,0:T(8,128)(2,1)S(1)} collective-permute-done((bf16[144,384]{1,0:T(8,128)(2,1)S(1)}, bf16[144,384]{1,0:T(8,128)(2,1)S(1)}, u32[]{:S(2)}, u32[]{:S(2)}) %collective-permute-start.23) | collective-permute-done | bytes 110624 | tf_op jit(solution)/shard_map/ppermute | solution.py:16
  56.4 1.7 %collective-permute-start.30 = (bf16[4,144,384]{2,1,0:T(8,128)(2,1)S(1)}, bf16[4,144,384]{2,1,0:T(8,128)(2,1)S(1)}, u32[]{:S(2)}, u32[]{:S(2)}) collective-permute-start(bf16[4,144,384]{2,1,0:T(8,128)(2,1)S(1)} %get-tuple-element.75.refs_1_), channel_id=1, source_target_pairs={{0,2},{2,0},{4,6},{6,4},{1,3},{3,1},{5,7},{7,5},{8,10},{10,8},{12,... | collective-permute-start | bytes 1327112 | tf_op jit(solution)/shard_map/ppermute | solution.py:16
  59.7 2.1 %shard_map.85 = (bf16[2,512,128]{2,1,0:T(8,128)(2,1)}, f32[8,384]{1,0:T(8,128)S(1)}) custom-call(s32[8]{0:T(128)S(1)} %stack.32.refs_0_, bf16[512,128]{1,0:T(8,128)(2,1)S(1)} %collective-permute-done.16.refs_2_.refs_1_, bf16[512,128]{1,0:T(8,128)(2,1)S(1)} %collective-permute-done.19.refs_2_, bf16[27,128,256]{2,1,0:T(8,128)(2,1)S(1)} %bitcast.37, ...), custom_call_target="tpu_custom_call" | custom-call | flops 1000000000 | bytes 1048576 | tf_op jit(solution)/shard_map/pallas_call | solution.py:27
  61.8 1.8 %shard_map.87 = (f32[27,128,256]{2,1,0:T(8,128)}, f32[8,384]{1,0:T(8,128)S(1)}) custom-call(s32[8]{0:T(128)S(1)} %stack.32.refs_0_, bf16[4,144,384]{2,1,0:T(8,128)(2,1)S(1)} %get-tuple-element.75.refs_1_, bf16[4,144,384]{2,1,0:T(8,128)(2,1)S(1)} %collective-permute-done.30.refs_2_), custom_call_target="tpu_custom_call" | custom-call | flops 1 | bytes 1 | tf_op jit(solution)/shard_map/pallas_call | solution.py:240
  65.3 1.3 %collective-permute-start.32 = (bf16[3,144,384]{2,1,0:T(8,128)(2,1)S(1)}, bf16[3,144,384]{2,1,0:T(8,128)(2,1)S(1)}, u32[]{:S(2)}, u32[]{:S(2)}) collective-permute-start(bf16[3,144,384]{2,1,0:T(8,128)(2,1)S(1)} %get-tuple-element.79.refs_1_), channel_id=1, source_target_pairs={{0,2},{2,0},{4,6},{6,4},{1,3},{3,1},{5,7},{7,5},{8,10},{10,8},{12,... | collective-permute-start | bytes 995336 | tf_op jit(solution)/shard_map/ppermute | solution.py:16
  67.9 1.7 %shard_map.89 = (f32[27,128,256]{2,1,0:T(8,128)}, f32[8,384]{1,0:T(8,128)S(1)}) custom-call(s32[8]{0:T(128)S(1)} %stack.32.refs_0_, bf16[3,144,384]{2,1,0:T(8,128)(2,1)S(1)} %get-tuple-element.79.refs_1_, bf16[3,144,384]{2,1,0:T(8,128)(2,1)S(1)} %collective-permute-done.32.refs_2_, ...), custom_call_target="tpu_custom_call", output_to_operand_aliasing={{0}: (3, {})} | custom-call | flops 1 | bytes 1 | tf_op jit(solution)/shard_map/pallas_call | solution.py:240
  69.6 1.7 %collective-permute-done.31.refs_1_ = bf16[144,384]{1,0:T(8,128)(2,1)S(1)} collective-permute-done((bf16[144,384]{1,0:T(8,128)(2,1)S(1)}, bf16[144,384]{1,0:T(8,128)(2,1)S(1)}, u32[]{:S(2)}, u32[]{:S(2)}) %collective-permute-start.31) | collective-permute-done | bytes 110624 | tf_op jit(solution)/shard_map/ppermute | solution.py:16
  73.2 2.0 %shard_map.90 = (f32[27,128,256]{2,1,0:T(8,128)}, f32[8,384]{1,0:T(8,128)}) custom-call(s32[8]{0:T(128)S(1)} %stack.32.refs_0_, bf16[144,384]{1,0:T(8,128)(2,1)S(1)} %collective-permute-done.31.refs_1_, bf16[144,384]{1,0:T(8,128)(2,1)S(1)} %collective-permute-done.33.refs_2_, f32[27,128,256]{2,1,0:T(8,128)} %get-tuple-element.82.refs_3_), custom_call_target="tpu_custom_call", output_to_operand_aliasing={{0}: (3, {})} | custom-call | flops 1 | bytes 1 | tf_op jit(solution)/shard_map/pallas_call | solution.py:240
  (87 shorter events, 27.4 us)
Async XLA Ops:
  1.8 6.4 %collective-permute-start.3 = (bf16[512,128]{1,0:T(8,128)(2,1)S(1)}, bf16[512,128]{1,0:T(8,128)(2,1)S(1)}, u32[]{:S(2)}, u32[]{:S(2)}) collective-permute-start(bf16[512,128]{1,0:T(8,128)(2,1)S(1)} %bitcast.27), channel_id=1, source_target_pairs={{0,4},{2,6},{4,0},{6,2},{1,5},{3,7},{5,1},{7,3},{8,12},{10,14},{12... | collective-permute-start | bytes 393224 | tf_op jit(solution)/shard_map/ppermute | solution.py:16
  9.0 5.1 %collective-permute-start.1 = (bf16[512,128]{1,0:T(8,128)(2,1)S(1)}, bf16[512,128]{1,0:T(8,128)(2,1)S(1)}, u32[]{:S(2)}, u32[]{:S(2)}) collective-permute-start(bf16[512,128]{1,0:T(8,128)(2,1)S(1)} %get-tuple-element.45), channel_id=1, source_target_pairs={{0,1},{1,0},{2,3},{3,2},{4,5},{5,4},{6,7},{7,6},{8,9},{9,8},{10,11... | collective-permute-start | bytes 393224 | tf_op jit(solution)/shard_map/ppermute | solution.py:16
  12.2 6.4 %collective-permute-start.5 = (bf16[512,128]{1,0:T(8,128)(2,1)S(1)}, bf16[512,128]{1,0:T(8,128)(2,1)S(1)}, u32[]{:S(2)}, u32[]{:S(2)}) collective-permute-start(bf16[512,128]{1,0:T(8,128)(2,1)S(1)} %get-tuple-element.51), channel_id=1, source_target_pairs={{0,1},{1,0},{2,3},{3,2},{4,5},{5,4},{6,7},{7,6},{8,9},{9,8},{10,11... | collective-permute-start | bytes 393224 | tf_op jit(solution)/shard_map/ppermute | solution.py:16
  14.8 4.8 %collective-permute-start.2 = (bf16[512,128]{1,0:T(8,128)(2,1)S(1)}, bf16[512,128]{1,0:T(8,128)(2,1)S(1)}, u32[]{:S(2)}, u32[]{:S(2)}) collective-permute-start(bf16[512,128]{1,0:T(8,128)(2,1)S(1)} %get-tuple-element.46.refs_5_), channel_id=1, source_target_pairs={{0,1},{1,0},{2,3},{3,2},{4,5},{5,4},{6,7},{7,6},{8,9},{9,8},{10,11... | collective-permute-start | bytes 393224 | tf_op jit(solution)/shard_map/ppermute | solution.py:16
  16.3 9.1 %collective-permute-start.9 = (bf16[512,128]{1,0:T(8,128)(2,1)S(1)}, bf16[512,128]{1,0:T(8,128)(2,1)S(1)}, u32[]{:S(2)}, u32[]{:S(2)}) collective-permute-start(bf16[512,128]{1,0:T(8,128)(2,1)S(1)} %bitcast.29), channel_id=1, source_target_pairs={{0,2},{2,0},{4,6},{6,4},{1,3},{3,1},{5,7},{7,5},{8,10},{10,8},{12,... | collective-permute-start | bytes 393224 | tf_op jit(solution)/shard_map/ppermute | solution.py:16
  17.4 5.2 %collective-permute-start.10 = (bf16[512,128]{1,0:T(8,128)(2,1)S(1)}, bf16[512,128]{1,0:T(8,128)(2,1)S(1)}, u32[]{:S(2)}, u32[]{:S(2)}) collective-permute-start(bf16[512,128]{1,0:T(8,128)(2,1)S(1)} %get-tuple-element.55), channel_id=1, source_target_pairs={{0,4},{2,6},{4,0},{6,2},{1,5},{3,7},{5,1},{7,3},{8,12},{10,14},{12... | collective-permute-start | bytes 393224 | tf_op jit(solution)/shard_map/ppermute | solution.py:16
  19.3 4.9 %collective-permute-start.6 = (bf16[512,128]{1,0:T(8,128)(2,1)S(1)}, bf16[512,128]{1,0:T(8,128)(2,1)S(1)}, u32[]{:S(2)}, u32[]{:S(2)}) collective-permute-start(bf16[512,128]{1,0:T(8,128)(2,1)S(1)} %get-tuple-element.52), channel_id=1, source_target_pairs={{0,1},{1,0},{2,3},{3,2},{4,5},{5,4},{6,7},{7,6},{8,9},{9,8},{10,11... | collective-permute-start | bytes 393224 | tf_op jit(solution)/shard_map/ppermute | solution.py:16
  19.7 6.0 %collective-permute-start.12 = (bf16[512,128]{1,0:T(8,128)(2,1)S(1)}, bf16[512,128]{1,0:T(8,128)(2,1)S(1)}, u32[]{:S(2)}, u32[]{:S(2)}) collective-permute-start(bf16[512,128]{1,0:T(8,128)(2,1)S(1)} %get-tuple-element.86.refs_2_), channel_id=1, source_target_pairs={{0,4},{2,6},{4,0},{6,2},{1,5},{3,7},{5,1},{7,3},{8,12},{10,14},{12... | collective-permute-start | bytes 393224 | tf_op jit(solution)/shard_map/ppermute | solution.py:16
  20.6 6.6 %collective-permute-start.7 = (bf16[512,128]{1,0:T(8,128)(2,1)S(1)}, bf16[512,128]{1,0:T(8,128)(2,1)S(1)}, u32[]{:S(2)}, u32[]{:S(2)}) collective-permute-start(bf16[512,128]{1,0:T(8,128)(2,1)S(1)} %get-tuple-element.87.refs_2_.refs_1_), channel_id=1, source_target_pairs={{0,2},{2,0},{4,6},{6,4},{1,3},{3,1},{5,7},{7,5},{8,10},{10,8},{12,... | collective-permute-start | bytes 393224 | tf_op jit(solution)/shard_map/ppermute | solution.py:16
  25.4 5.4 %collective-permute-start.15 = (bf16[512,128]{1,0:T(8,128)(2,1)S(1)}, bf16[512,128]{1,0:T(8,128)(2,1)S(1)}, u32[]{:S(2)}, u32[]{:S(2)}) collective-permute-start(bf16[512,128]{1,0:T(8,128)(2,1)S(1)} %get-tuple-element.84.refs_4_), channel_id=1, source_target_pairs={{0,4},{2,6},{4,0},{6,2},{1,5},{3,7},{5,1},{7,3},{8,12},{10,14},{12... | collective-permute-start | bytes 393224 | tf_op jit(solution)/shard_map/ppermute | solution.py:16
  25.7 3.7 %collective-permute-start.13 = (bf16[512,128]{1,0:T(8,128)(2,1)S(1)}, bf16[512,128]{1,0:T(8,128)(2,1)S(1)}, u32[]{:S(2)}, u32[]{:S(2)}) collective-permute-start(bf16[512,128]{1,0:T(8,128)(2,1)S(1)} %collective-permute-done.12.refs_2_), channel_id=1, source_target_pairs={{0,2},{2,0},{4,6},{6,4},{1,3},{3,1},{5,7},{7,5},{8,10},{10,8},{12,... | collective-permute-start | bytes 393224 | tf_op jit(solution)/shard_map/ppermute | solution.py:16
  35.1 7.6 %collective-permute-start.8 = (bf16[512,128]{1,0:T(8,128)(2,1)S(1)}, bf16[512,128]{1,0:T(8,128)(2,1)S(1)}, u32[]{:S(2)}, u32[]{:S(2)}) collective-permute-start(bf16[512,128]{1,0:T(8,128)(2,1)S(1)} %get-tuple-element.86.refs_2_), channel_id=1, source_target_pairs={{0,2},{2,0},{4,6},{6,4},{1,3},{3,1},{5,7},{7,5},{8,10},{10,8},{12,... | collective-permute-start | bytes 393224 | tf_op jit(solution)/shard_map/ppermute | solution.py:16
  35.6 4.9 %collective-permute-start.17 = (bf16[144,384]{1,0:T(8,128)(2,1)S(1)}, bf16[144,384]{1,0:T(8,128)(2,1)S(1)}, u32[]{:S(2)}, u32[]{:S(2)}) collective-permute-start(bf16[144,384]{1,0:T(8,128)(2,1)S(1)} %get-tuple-element.63), channel_id=1, source_target_pairs={{0,8},{8,0},{16,24},{24,16},{1,9},{9,1},{17,25},{25,17},{2,10},{10... | collective-permute-start | bytes 331784 | tf_op jit(solution)/shard_map/ppermute | solution.py:16
  35.7 6.9 %collective-permute-start.18 = (bf16[512,128]{1,0:T(8,128)(2,1)S(1)}, bf16[512,128]{1,0:T(8,128)(2,1)S(1)}, u32[]{:S(2)}, u32[]{:S(2)}) collective-permute-start(bf16[512,128]{1,0:T(8,128)(2,1)S(1)} %get-tuple-element.64), channel_id=1, source_target_pairs={{0,4},{2,6},{4,0},{6,2},{1,5},{3,7},{5,1},{7,3},{8,12},{10,14},{12... | collective-permute-start | bytes 393224 | tf_op jit(solution)/shard_map/ppermute | solution.py:16
  36.7 13.0 %collective-permute-start.26 = (f32[8,384]{1,0:T(8,128)S(1)}, f32[8,384]{1,0:T(8,128)S(1)}, u32[]{:S(2)}, u32[]{:S(2)}) collective-permute-start(f32[8,384]{1,0:T(8,128)S(1)} %add.32), channel_id=1, source_target_pairs={{0,16},{8,24},{16,0},{24,8},{1,17},{9,25},{17,1},{25,9},{2,18},{10... | collective-permute-start | bytes 36872 | tf_op jit(solution)/shard_map/ppermute | solution.py:16
  39.1 8.0 %collective-permute-start.21 = (bf16[144,384]{1,0:T(8,128)(2,1)S(1)}, bf16[144,384]{1,0:T(8,128)(2,1)S(1)}, u32[]{:S(2)}, u32[]{:S(2)}) collective-permute-start(bf16[144,384]{1,0:T(8,128)(2,1)S(1)} %bitcast_select_fusion.3), channel_id=1, source_target_pairs={{0,8},{8,0},{16,24},{24,16},{1,9},{9,1},{17,25},{25,17},{2,10},{10... | collective-permute-start | bytes 331784 | tf_op jit(solution)/shard_map/ppermute | solution.py:16
  40.5 6.6 %collective-permute-start.22 = (bf16[144,384]{1,0:T(8,128)(2,1)S(1)}, bf16[144,384]{1,0:T(8,128)(2,1)S(1)}, u32[]{:S(2)}, u32[]{:S(2)}) collective-permute-start(bf16[144,384]{1,0:T(8,128)(2,1)S(1)} %add_convert_fusion.refs_10_), channel_id=1, source_target_pairs={{0,16},{8,24},{16,0},{24,8},{1,17},{9,25},{17,1},{25,9},{2,18},{10... | collective-permute-start | bytes 331784 | tf_op jit(solution)/shard_map/ppermute | solution.py:16
  47.2 5.9 %collective-permute-start.25 = (bf16[144,384]{1,0:T(8,128)(2,1)S(1)}, bf16[144,384]{1,0:T(8,128)(2,1)S(1)}, u32[]{:S(2)}, u32[]{:S(2)}) collective-permute-start(bf16[144,384]{1,0:T(8,128)(2,1)S(1)} %bitcast_select_fusion.4.refs_1_), channel_id=1, source_target_pairs={{0,16},{8,24},{16,0},{24,8},{1,17},{9,25},{17,1},{25,9},{2,18},{10... | collective-permute-start | bytes 331784 | tf_op jit(solution)/shard_map/ppermute | solution.py:16
  48.7 4.4 %collective-permute-start.24 = (bf16[144,384]{1,0:T(8,128)(2,1)S(1)}, bf16[144,384]{1,0:T(8,128)(2,1)S(1)}, u32[]{:S(2)}, u32[]{:S(2)}) collective-permute-start(bf16[144,384]{1,0:T(8,128)(2,1)S(1)} %bitcast_select_fusion.4.refs_1_), channel_id=1, source_target_pairs={{0,4},{2,6},{4,0},{6,2},{1,5},{3,7},{5,1},{7,3},{8,12},{10,14},{12... | collective-permute-start | bytes 331784 | tf_op jit(solution)/shard_map/ppermute | solution.py:16
  49.7 6.1 %collective-permute-start.23 = (bf16[144,384]{1,0:T(8,128)(2,1)S(1)}, bf16[144,384]{1,0:T(8,128)(2,1)S(1)}, u32[]{:S(2)}, u32[]{:S(2)}) collective-permute-start(bf16[144,384]{1,0:T(8,128)(2,1)S(1)} %bitcast_select_fusion.4.refs_1_), channel_id=1, source_target_pairs={{0,8},{8,0},{16,24},{24,16},{1,9},{9,1},{17,25},{25,17},{2,10},{10... | collective-permute-start | bytes 331784 | tf_op jit(solution)/shard_map/ppermute | solution.py:16
  56.4 5.4 %collective-permute-start.30 = (bf16[4,144,384]{2,1,0:T(8,128)(2,1)S(1)}, bf16[4,144,384]{2,1,0:T(8,128)(2,1)S(1)}, u32[]{:S(2)}, u32[]{:S(2)}) collective-permute-start(bf16[4,144,384]{2,1,0:T(8,128)(2,1)S(1)} %get-tuple-element.75.refs_1_), channel_id=1, source_target_pairs={{0,2},{2,0},{4,6},{6,4},{1,3},{3,1},{5,7},{7,5},{8,10},{10,8},{12,... | collective-permute-start | bytes 1327112 | tf_op jit(solution)/shard_map/ppermute | solution.py:16
  58.2 6.6 %collective-permute-start.29 = (bf16[2,144,384]{2,1,0:T(8,128)(2,1)S(1)}, bf16[2,144,384]{2,1,0:T(8,128)(2,1)S(1)}, u32[]{:S(2)}, u32[]{:S(2)}) collective-permute-start(bf16[2,144,384]{2,1,0:T(8,128)(2,1)S(1)} %get-tuple-element.74), channel_id=1, source_target_pairs={{0,4},{2,6},{4,0},{6,2},{1,5},{3,7},{5,1},{7,3},{8,12},{10,14},{12... | collective-permute-start | bytes 663560 | tf_op jit(solution)/shard_map/ppermute | solution.py:16
  58.7 5.0 %collective-permute-start.28 = (bf16[144,384]{1,0:T(8,128)(2,1)S(1)}, bf16[144,384]{1,0:T(8,128)(2,1)S(1)}, u32[]{:S(2)}, u32[]{:S(2)}) collective-permute-start(bf16[144,384]{1,0:T(8,128)(2,1)S(1)} %get-tuple-element.73), channel_id=1, source_target_pairs={{0,8},{8,0},{16,24},{24,16},{1,9},{9,1},{17,25},{25,17},{2,10},{10... | collective-permute-start | bytes 331784 | tf_op jit(solution)/shard_map/ppermute | solution.py:16
  66.7 4.6 %collective-permute-start.31 = (bf16[144,384]{1,0:T(8,128)(2,1)S(1)}, bf16[144,384]{1,0:T(8,128)(2,1)S(1)}, u32[]{:S(2)}, u32[]{:S(2)}) collective-permute-start(bf16[144,384]{1,0:T(8,128)(2,1)S(1)} %get-tuple-element.78), channel_id=1, source_target_pairs={{0,4},{2,6},{4,0},{6,2},{1,5},{3,7},{5,1},{7,3},{8,12},{10,14},{12... | collective-permute-start | bytes 331784 | tf_op jit(solution)/shard_map/ppermute | solution.py:16
  (14 other events, 43.9 us)

commit v4 on v3

--- a/solution.py
+++ b/solution.py
@@ -177,6 +177,15 @@
                 ref[rows, :] = acc[b, pl.ds(at, part), :].astype(ref.dtype)
 
 
+def split_rows(total):
+    value = jnp.broadcast_to(total[0:1, :], (16, total.shape[1]))
+    high = value.astype(BF)
+    rest = value - high.astype(F32)
+    mid = rest.astype(BF)
+    low = (rest - mid.astype(F32)).astype(BF)
+    return jnp.concatenate([high, mid, low], axis=1)
+
+
 def place(pos, pieces, out, wide, sems):
     x, k, mine = pos[6], pos[3], pos[4]
     half = out.shape[2] // 2
@@ -196,35 +205,40 @@
         copy.wait()
 
 
-def round_body(pos, q, q1, x0, q2, one_z, two_x, four_c):
-    one_z[...] = q2[...]
-    two_x[0], two_x[1] = q1[...], q2[...]
+def round_body(pos, q, x0, q1, q2, one_z, one_x, x0_z, four_c):
+    one_z[...], one_x[...], x0_z[...] = q2[...], q2[...], x0[...]
     four_c[0], four_c[1], four_c[2], four_c[3] = q[...], q1[...], q2[...], x0[...]
 
 
-def next_round_body(pos, q3, x12, one_x, three_c):
-    one_x[...] = q3[...]
-    three_c[0], three_c[1], three_c[2] = q3[...], x12[0], x12[1]
+def next_round_body(pos, q3, x2, total, last_x, two_c):
+    rows = q3.shape[0]
+    last_x[0:rows, :] = q3[...]
+    last_x[rows : rows + 16, :] = split_rows(total[:, : total.shape[1] // 3])
+    two_c[0], two_c[1] = q3[...], x2[...]
+
+
+def both_cores(kinds, own, core):
+    pieces = [(who, j, own.at[n]) for n, (who, j) in enumerate(kinds)]
+    return pieces + [(who + 2, j, core.at[n]) for n, (who, j) in enumerate(kinds)]
 
 
 def first_spread_body(pos, own, core, out, done, wide, sems):
-    kinds = ((0, 0), (0, 1), (0, 2), (1, 0))
-    pieces = [(who, j, own.at[n]) for n, (who, j) in enumerate(kinds)]
-    pieces += [(who + 2, j, core.at[n]) for n, (who, j) in enumerate(kinds)]
+    place(pos, both_cores(((0, 0), (0, 1), (0, 2), (1, 0)), own, core), out, wide, sems)
+    done[...] = jnp.zeros_like(done)
+
+
+def next_spread_body(pos, own, core, before, out, done, wide, sems):
+    place(pos, both_cores(((0, 3), (1, 2)), own, core), out, wide, sems)
+    done[...] = jnp.zeros_like(done)
+
+
+def last_spread_body(pos, own, core, before, out, done, wide, sems):
+    rows = own.shape[0] // 2
+    pieces = []
+    for n, (who, j) in enumerate(((1, 1), (1, 3))):
+        pieces.append((who, j, own.at[n * rows : (n + 1) * rows]))
+        pieces.append((who + 2, j, core.at[n * rows : (n + 1) * rows]))
     place(pos, pieces, out, wide, sems)
-    done[...] = jnp.zeros_like(done)
-
-
-def next_spread_body(pos, own, core, before, out, done, wide, sems):
-    kinds = ((0, 3), (1, 1), (1, 2))
-    pieces = [(who, j, own.at[n]) for n, (who, j) in enumerate(kinds)]
-    pieces += [(who + 2, j, core.at[n]) for n, (who, j) in enumerate(kinds)]
-    place(pos, pieces, out, wide, sems)
-    done[...] = jnp.zeros_like(done)
-
-
-def last_spread_body(pos, x3, cx3, before, out, done, wide, sems):
-    place(pos, [(1, 3, x3), (3, 3, cx3)], out, wide, sems)
     done[...] = jnp.zeros_like(done)
 
 
@@ -254,16 +268,15 @@
     return jnp.concatenate([first, jnp.where(x == 0, other, keep)], axis=1)
 
 
-def input_taps(ny, depth, wt, buf, at):
+def input_taps(ny, depths, wt, buf, at):
     cells = buf.shape[1] - 2 * ny
     lanes = buf.shape[2] // 3
-    acc = jnp.zeros((cells, wt.shape[1]), F32)
+    acc = jnp.zeros((cells, len(depths) * wt.shape[1]), F32)
     for b in range(3):
         for c in range(3):
             lhs = buf[at, (2 - b) * ny : (2 - b) * ny + cells, c * lanes : (c + 1) * lanes]
-            acc = acc + lax.dot_general(
-                lhs, wt[depth * 9 + b * 3 + c], (((1,), (1,)), ((), ())), preferred_element_type=F32
-            )
+            rhs = jnp.concatenate([wt[depth * 9 + b * 3 + c] for depth in depths], axis=0)
+            acc = acc + lax.dot_general(lhs, rhs, (((1,), (1,)), ((), ())), preferred_element_type=F32)
     return acc
 
 
@@ -272,9 +285,11 @@
     put_plane(buf, 0, whole(x, kn[...], on[...]), ny, True)
     put_plane(buf, 1, whole(x, kf[...], of[...]), ny, True)
     put_plane(buf, 2, whole(x, near[...], near_o[...]), ny, True)
-    total = input_taps(ny, 1, wt, buf, 0) + input_taps(ny, 2 - 2 * odd, wt, buf, 1)
-    out[...] = (total + input_taps(ny, 2 * odd, wt, buf, 2)).astype(BF)
-    partial[...] = input_taps(ny, 1, wt, buf, 1) + input_taps(ny, 2 * odd, wt, buf, 0)
+    half = out.shape[1]
+    both = input_taps(ny, (1, 2 * odd), wt, buf, 0)
+    swapped = input_taps(ny, (2 - 2 * odd, 1), wt, buf, 1)
+    out[...] = (both[:, :half] + swapped[:, :half] + input_taps(ny, (2 * odd,), wt, buf, 2)).astype(BF)
+    partial[...] = both[:, half:] + swapped[:, half:]
     done[...] = jnp.zeros_like(done)
     act[1 - odd] = act_n[...]
     act[odd] = act_f[...]
@@ -286,7 +301,7 @@
     if inside:
         beyond = jnp.where((mine == 0) | (mine == 3), jnp.zeros_like(beyond), beyond)
     put_plane(buf, 0, beyond, ny, True)
-    out[odd] = (partial[...] + input_taps(ny, 2 - 2 * odd, wt, buf, 0)).astype(BF)
+    out[odd] = (partial[...] + input_taps(ny, (2 - 2 * odd,), wt, buf, 0)).astype(BF)
     out[1 - odd] = ig_n[...]
     done[...] = jnp.zeros_like(done)
 
@@ -391,9 +406,9 @@
             bit *= 2
         keep, s1, s2, s3 = vmem_call(cut_body, cut, [], 0, pos, acc)
         sent = keep_f
-    r3, total_z = swap(s3, "dp", 1), swap(total, "dp", 1)
-    merged, total_b = (s2 + r3.astype(F32)).astype(BF), total + total_z
-    r2, r1, total_z2 = swap(merged, "dp", 2), swap(held_back(s1, total_z), "dp", 1), swap(total_b, "dp", 2)
+    r3, r1, total_z2 = swap(s3, "dp", 1), swap(s1, "dp", 1), swap(total, "dp", 2)
+    merged, total_a = (s2 + r3.astype(F32)).astype(BF), total + total_z2
+    r2 = swap(merged, "dp", 2)
 
     sent_x = swap(sent, "slab", 2)
     wt = weight.reshape(27, local_in, outputs)
@@ -421,30 +436,38 @@
         0,
         pos, far_keep, far_send, wt, partial, ig_n,
     )
-    quarter = held_back(((keep + r1.astype(F32) + r2.astype(F32)) * factor).astype(BF), ig_n_done)
-    total3 = (total_b + total_z2) * factor
+    quarter = held_back(((keep + r1.astype(F32) + r2.astype(F32)) * factor).astype(BF), ig_n_done, total_z2)
+    total_z1 = swap(total_a, "dp", 1)
     q1, q2, x0 = swap(quarter, "dp", 1), swap(quarter, "dp", 2), swap(quarter, "slab", 2)
-    total_x = swap(total3, "slab", 2)
+    total_b = total_a + total_z1
     out_shape = (27, local_in, outputs)
     token = (8, lanes), F32
-    one_z, two_x, four_c = vmem_call(
+    one_z, one_x, x0_z, four_c = vmem_call(
         round_body,
-        [(quarter.shape, BF), ((2,) + quarter.shape, BF), ((4,) + quarter.shape, BF)],
+        [(quarter.shape, BF)] * 3 + [((4,) + quarter.shape, BF)],
         [],
         0,
-        pos, quarter, q1, x0, q2,
-        after=(total_x,),
-    )
-    q3, x12, core = swap(one_z, "dp", 1), swap(two_x, "slab", 2), swap(four_c, "slab", 1)
+        pos, quarter, x0, q1, q2,
+        after=(total_z1, ig_done),
+    )
+    q3, x2, x1, core = swap(one_z, "dp", 1), swap(one_x, "slab", 2), swap(x0_z, "dp", 1), swap(four_c, "slab", 1)
     out, done = spread(first_spread_body, out_shape, token, (), pos, four_c, core)
-    one_x, three_c = vmem_call(
-        next_round_body, [(quarter.shape, BF), ((3,) + quarter.shape, BF)], [], 0, pos, q3, x12, after=(done, ig_done)
-    )
-    x3, core_b = swap(one_x, "slab", 2), swap(three_c, "slab", 1)
-    out, done = spread(next_spread_body, out_shape, token, (), pos, three_c, core_b, out, alias=True)
-    core_x3 = swap(held_back(x3, done), "slab", 1)
-    weight_grad, _ = spread(last_spread_body, out_shape, token, (), pos, x3, core_x3, out, alias=True)
-    bias_grad = jnp.where(x == y, total3, total_x)[0, :local_out]
+    last_x, two_c = vmem_call(
+        next_round_body,
+        [((rows + 16, lanes), BF), ((2,) + quarter.shape, BF)],
+        [],
+        0,
+        pos, q3, x2, total_b,
+        after=(done,),
+    )
+    x3, core_b = swap(last_x, "slab", 2), swap(two_c, "slab", 1)
+    out, done = spread(next_spread_body, out_shape, token, (), pos, two_c, core_b, out, alias=True)
+    x3 = held_back(x3, done)
+    pair_x = jnp.concatenate([x1, x3[:rows]], axis=0)
+    core_x = swap(pair_x, "slab", 1)
+    weight_grad, _ = spread(last_spread_body, out_shape, token, (), pos, pair_x, core_x, out, alias=True)
+    tail = x3[rows : rows + 1].astype(F32).reshape(3, local_out)
+    bias_grad = jnp.where(x == y, total_b[0, :local_out], tail[0] + tail[1] + tail[2]) * factor
     shape = (samples, planes, nx, ny)
     return (
         act.reshape(shape + (local_out,)),

time: 75.7 us -> 73.3 us (0.968)
  Pallas kernels: 25.2 us -> 23.9 us
  waiting for transfers between devices: 11.2 us -> 9.93 us
    pallas_call x13, Pallas kernels: 19.7 us -> 18.4 us  [vmem_call(): pl.pallas_call(inner, out_shape=shapes, in_specs=[pl.BlockSpec(memory_spa...]
    ppermute x34, waiting for transfers between devices: 11.2 us -> 9.93 us  [swap(): lax.ppermute(value, axis, [(i, i ^ bit) for i in range(lax.axis_size(axis...]
  transfers between devices with their start and end apart: 34 -> 34, of which waited for: 11 -> 11; matrix products, arithmetic and copies ran while one was open for 1% -> 1% of each run, Pallas kernels for 28% -> 27%
where the time goes in v4:
time: 73.3 us; the launch traced here: 72.8 us
  starting transfers between devices  34.7 us (47%)
  Pallas kernels  23.9 us (33%)
  waiting for transfers between devices  9.93 us (14%)
  other arithmetic  1.76 us (2%)
  local copies, waits for them, and re-layouts  1.62 us (2%)
  between operations  0.91 us (1%)
    ppermute x34, starting transfers between devices, swap(): lax.ppermute(value, axis, [(i, i ^ bit) for i in range(lax.axis_size(axis...  34.7 us
    pallas_call x13, Pallas kernels, vmem_call(): pl.pallas_call(inner, out_shape=shapes, in_specs=[pl.BlockSpec(memory_spa...  18.4 us
    ppermute x34, waiting for transfers between devices, swap(): lax.ppermute(value, axis, [(i, i ^ bit) for i in range(lax.axis_size(axis...  9.93 us
    pallas_call x3, Pallas kernels, spread(): pl.pallas_call(inner, out_shape=[jax.ShapeDtypeStruct(shape, F32), jax.Sh...  5.47 us
    unnamed x8, local copies, waits for them, and re-layouts  1.49 us
  transfers between devices with their start and end apart: 34, of which 11 were waited for; matrix products, arithmetic and copies ran while one was open for 1% of the time, Pallas kernels for 27%

profile of v4, /device:TPU:1, one launch (start us, length us, event | category | flops | bytes accessed | tf_op | source)
XLA Modules:
  0.0 72.8 jit_solution(13372945462963929202)
XLA Ops:
  1.8 2.7 %collective-permute-start.3 = (bf16[512,128]{1,0:T(8,128)(2,1)S(1)}, bf16[512,128]{1,0:T(8,128)(2,1)S(1)}, u32[]{:S(2)}, u32[]{:S(2)}) collective-permute-start(bf16[512,128]{1,0:T(8,128)(2,1)S(1)} %bitcast.28), channel_id=1, source_target_pairs={{0,4},{2,6},{4,0},{6,2},{1,5},{3,7},{5,1},{7,3},{8,12},{10,14},{12... | collective-permute-start | bytes 393224 | tf_op jit(solution)/shard_map/ppermute | solution.py:16
  4.5 1.5 %copy-done = bf16[3,3,3,128,256]{4,3,2,1,0:T(8,128)(2,1)S(1)} copy-done((bf16[3,3,3,128,256]{4,3,2,1,0:T(8,128)(2,1)S(1)}, bf16[3,3,3,128,256]{4,3,2,1,0:T(8,128)(2,1)}, u32[]{:S(2)}) %copy-start) | copy-done | bytes 1769496
  6.0 2.1 %shard_map.75 = (f32[512,128]{1,0:T(8,128)S(1)}, bf16[512,128]{1,0:T(8,128)(2,1)S(1)}, bf16[2,544,384]{2,1,0:T(8,128)(2,1)S(1)}, bf16[3,1152,256]{2,1,0:T(8,128)(2,1)S(1)}, f32[8,128]{1,0:T(8,128)S(1)}) custom-call(s32[8]{0:T(128)S(1)} %stack.32.refs_0_, bf16[512,128]{1,0:T(8,128)(2,1)S(1)} %bitcast.33, bf16[512,128]{1,0:T(8,128)(2,1)S(1)} %bitcast.29, ...), custom_call_target="tpu_custom_call" | custom-call | flops 2811939328 | bytes 1048576 | tf_op jit(solution)/shard_map/pallas_call | solution.py:27
  9.0 1.5 %collective-permute-start.1 = (bf16[512,128]{1,0:T(8,128)(2,1)S(1)}, bf16[512,128]{1,0:T(8,128)(2,1)S(1)}, u32[]{:S(2)}, u32[]{:S(2)}) collective-permute-start(bf16[512,128]{1,0:T(8,128)(2,1)S(1)} %get-tuple-element.46), channel_id=1, source_target_pairs={{0,1},{1,0},{2,3},{3,2},{4,5},{5,4},{6,7},{7,6},{8,9},{9,8},{10,11... | collective-permute-start | bytes 393224 | tf_op jit(solution)/shard_map/ppermute | solution.py:16
  10.5 1.7 %shard_map.77 = (f32[512,128]{1,0:T(8,128)S(1)}, bf16[512,128]{1,0:T(8,128)(2,1)S(1)}) custom-call(s32[8]{0:T(128)S(1)} %stack.32.refs_0_, bf16[512,128]{1,0:T(8,128)(2,1)S(1)} %collective-permute-done.4.refs_1_.refs_8_, bf16[2,544,384]{2,1,0:T(8,128)(2,1)S(1)} %get-tuple-element.49.refs_2_, bf16[3,1152,256]{2,1,0:T(8,128)(2,1)S(1)} %get-tuple-element.50.refs_3_), custom_call_target="tpu_custom_call" | custom-call | flops 2811939328 | bytes 1048576 | tf_op jit(solution)/shard_map/pallas_call | solution.py:27
  14.8 1.5 %collective-permute-start.2 = (bf16[512,128]{1,0:T(8,128)(2,1)S(1)}, bf16[512,128]{1,0:T(8,128)(2,1)S(1)}, u32[]{:S(2)}, u32[]{:S(2)}) collective-permute-start(bf16[512,128]{1,0:T(8,128)(2,1)S(1)} %get-tuple-element.47.refs_5_), channel_id=1, source_target_pairs={{0,1},{1,0},{2,3},{3,2},{4,5},{5,4},{6,7},{7,6},{8,9},{9,8},{10,11... | collective-permute-start | bytes 393224 | tf_op jit(solution)/shard_map/ppermute | solution.py:16
  20.6 2.0 %collective-permute-start.7 = (bf16[512,128]{1,0:T(8,128)(2,1)S(1)}, bf16[512,128]{1,0:T(8,128)(2,1)S(1)}, u32[]{:S(2)}, u32[]{:S(2)}) collective-permute-start(bf16[512,128]{1,0:T(8,128)(2,1)S(1)} %get-tuple-element.89.refs_2_.refs_1_), channel_id=1, source_target_pairs={{0,2},{2,0},{4,6},{6,4},{1,3},{3,1},{5,7},{7,5},{8,10},{10,8},{12,... | collective-permute-start | bytes 393224 | tf_op jit(solution)/shard_map/ppermute | solution.py:16
  27.2 2.1 %shard_map.80 = (f32[3,192,384]{2,1,0:T(8,128)S(1)}, f32[8,384]{1,0:T(8,128)S(1)}) custom-call(s32[8]{0:T(128)S(1)} %stack.32.refs_0_, bf16[12,192,512]{2,1,0:T(8,128)(2,1)S(1)} %shard_map.79.refs_1_, bf16[512,128]{1,0:T(8,128)(2,1)S(1)} %get-tuple-element.89.refs_2_.refs_1_, bf16[512,128]{1,0:T(8,128)(2,1)S(1)} %collective-permute-done.7.refs_3_.refs_5_, ...), custom_call_target="tpu_custom_call" | custom-call | flops 4623878656 | bytes 1048576 | tf_op jit(solution)/shard_map/pallas_call | solution.py:27
  29.3 1.4 %shard_map.81 = (f32[3,192,384]{2,1,0:T(8,128)S(1)}, f32[8,384]{1,0:T(8,128)S(1)}) custom-call(s32[8]{0:T(128)S(1)} %stack.32.refs_0_, bf16[12,192,512]{2,1,0:T(8,128)(2,1)S(1)} %shard_map.79.refs_1_, bf16[512,128]{1,0:T(8,128)(2,1)S(1)} %collective-permute-done.12.refs_2_, bf16[512,128]{1,0:T(8,128)(2,1)S(1)} %collective-permute-done.13.refs_3_, ...), custom_call_target="tpu_custom_call" | custom-call | flops 2811939328 | bytes 1048576 | tf_op jit(solution)/shard_map/pallas_call | solution.py:27
  33.7 1.4 %collective-permute-start.17 = (bf16[144,384]{1,0:T(8,128)(2,1)S(1)}, bf16[144,384]{1,0:T(8,128)(2,1)S(1)}, u32[]{:S(2)}, u32[]{:S(2)}) collective-permute-start(bf16[144,384]{1,0:T(8,128)(2,1)S(1)} %get-tuple-element.64), channel_id=1, source_target_pairs={{0,8},{8,0},{16,24},{24,16},{1,9},{9,1},{17,25},{25,17},{2,10},{10... | collective-permute-start | bytes 331784 | tf_op jit(solution)/shard_map/ppermute | solution.py:16
  35.6 2.3 %collective-permute-start.20 = (f32[8,384]{1,0:T(8,128)S(1)}, f32[8,384]{1,0:T(8,128)S(1)}, u32[]{:S(2)}, u32[]{:S(2)}) collective-permute-start(f32[8,384]{1,0:T(8,128)S(1)} %get-tuple-element.71), channel_id=1, source_target_pairs={{0,16},{8,24},{16,0},{24,8},{1,17},{9,25},{17,1},{25,9},{2,18},{10... | collective-permute-start | bytes 36872 | tf_op jit(solution)/shard_map/ppermute | solution.py:16
  39.0 1.6 %collective-permute-start.22 = (bf16[144,384]{1,0:T(8,128)(2,1)S(1)}, bf16[144,384]{1,0:T(8,128)(2,1)S(1)}, u32[]{:S(2)}, u32[]{:S(2)}) collective-permute-start(bf16[144,384]{1,0:T(8,128)(2,1)S(1)} %add_convert_fusion.refs_10_), channel_id=1, source_target_pairs={{0,16},{8,24},{16,0},{24,8},{1,17},{9,25},{17,1},{25,9},{2,18},{10... | collective-permute-start | bytes 331784 | tf_op jit(solution)/shard_map/ppermute | solution.py:16
  40.6 2.0 %collective-permute-done.18.refs_11_ = bf16[512,128]{1,0:T(8,128)(2,1)S(1)} collective-permute-done((bf16[512,128]{1,0:T(8,128)(2,1)S(1)}, bf16[512,128]{1,0:T(8,128)(2,1)S(1)}, u32[]{:S(2)}, u32[]{:S(2)}) %collective-permute-start.18) | collective-permute-done | bytes 131104 | tf_op jit(solution)/shard_map/ppermute | solution.py:16
  42.5 1.4 %collective-permute-start.19 = (bf16[512,128]{1,0:T(8,128)(2,1)S(1)}, bf16[512,128]{1,0:T(8,128)(2,1)S(1)}, u32[]{:S(2)}, u32[]{:S(2)}) collective-permute-start(bf16[512,128]{1,0:T(8,128)(2,1)S(1)} %collective-permute-done.18.refs_11_), channel_id=1, source_target_pairs={{0,2},{2,0},{4,6},{6,4},{1,3},{3,1},{5,7},{7,5},{8,10},{10,8},{12,... | collective-permute-start | bytes 393224 | tf_op jit(solution)/shard_map/ppermute | solution.py:16
  44.0 3.2 %shard_map.84 = (bf16[512,128]{1,0:T(8,128)(2,1)S(1)}, f32[512,128]{1,0:T(8,128)S(1)}, bf16[2,512,128]{2,1,0:T(8,128)(2,1)}, f32[8,384]{1,0:T(8,128)S(1)}) custom-call(s32[8]{0:T(128)S(1)} %stack.32.refs_0_, bf16[512,128]{1,0:T(8,128)(2,1)S(1)} %get-tuple-element.89.refs_2_.refs_1_, bf16[512,128]{1,0:T(8,128)(2,1)S(1)} %get-tuple-element.88.refs_2_, ...), custom_call_target="tpu_custom_call" | custom-call | flops 4623878656 | bytes 1048576 | tf_op jit(solution)/shard_map/pallas_call | solution.py:27
  47.4 1.7 %collective-permute-start.24 = (bf16[144,384]{1,0:T(8,128)(2,1)S(1)}, bf16[144,384]{1,0:T(8,128)(2,1)S(1)}, u32[]{:S(2)}, u32[]{:S(2)}) collective-permute-start(bf16[144,384]{1,0:T(8,128)(2,1)S(1)} %bitcast_select_fusion.2.refs_1_), channel_id=1, source_target_pairs={{0,8},{8,0},{16,24},{24,16},{1,9},{9,1},{17,25},{25,17},{2,10},{10... | collective-permute-start | bytes 331784 | tf_op jit(solution)/shard_map/ppermute | solution.py:16
  49.8 2.1 %shard_map.85 = (bf16[2,512,128]{2,1,0:T(8,128)(2,1)}, f32[8,384]{1,0:T(8,128)S(1)}) custom-call(s32[8]{0:T(128)S(1)} %stack.32.refs_0_, bf16[512,128]{1,0:T(8,128)(2,1)S(1)} %collective-permute-done.16.refs_2_.refs_1_, bf16[512,128]{1,0:T(8,128)(2,1)S(1)} %collective-permute-done.19.refs_2_, bf16[27,128,256]{2,1,0:T(8,128)(2,1)S(1)} %bitcast.38, ...), custom_call_target="tpu_custom_call" | custom-call | flops 1000000000 | bytes 1048576 | tf_op jit(solution)/shard_map/pallas_call | solution.py:27
  53.0 1.7 %collective-permute-done.25.refs_4_ = bf16[144,384]{1,0:T(8,128)(2,1)S(1)} collective-permute-done((bf16[144,384]{1,0:T(8,128)(2,1)S(1)}, bf16[144,384]{1,0:T(8,128)(2,1)S(1)}, u32[]{:S(2)}, u32[]{:S(2)}) %collective-permute-start.25) | collective-permute-done | bytes 110624 | tf_op jit(solution)/shard_map/ppermute | solution.py:16
  55.3 1.6 %collective-permute-start.30 = (bf16[4,144,384]{2,1,0:T(8,128)(2,1)S(1)}, bf16[4,144,384]{2,1,0:T(8,128)(2,1)S(1)}, u32[]{:S(2)}, u32[]{:S(2)}) collective-permute-start(bf16[4,144,384]{2,1,0:T(8,128)(2,1)S(1)} %get-tuple-element.78.refs_1_), channel_id=1, source_target_pairs={{0,2},{2,0},{4,6},{6,4},{1,3},{3,1},{5,7},{7,5},{8,10},{10,8},{12,... | collective-permute-start | bytes 1327112 | tf_op jit(solution)/shard_map/ppermute | solution.py:16
  58.4 1.8 %shard_map.87 = (f32[27,128,256]{2,1,0:T(8,128)}, f32[8,384]{1,0:T(8,128)S(1)}) custom-call(s32[8]{0:T(128)S(1)} %stack.32.refs_0_, bf16[4,144,384]{2,1,0:T(8,128)(2,1)S(1)} %get-tuple-element.78.refs_1_, bf16[4,144,384]{2,1,0:T(8,128)(2,1)S(1)} %collective-permute-done.30.refs_2_), custom_call_target="tpu_custom_call" | custom-call | flops 1 | bytes 1 | tf_op jit(solution)/shard_map/pallas_call | solution.py:254
  60.2 1.4 %collective-permute-done.28.refs_1_ = bf16[144,384]{1,0:T(8,128)(2,1)S(1)} collective-permute-done((bf16[144,384]{1,0:T(8,128)(2,1)S(1)}, bf16[144,384]{1,0:T(8,128)(2,1)S(1)}, u32[]{:S(2)}, u32[]{:S(2)}) %collective-permute-start.28) | collective-permute-done | bytes 110624 | tf_op jit(solution)/shard_map/ppermute | solution.py:16
  64.0 1.5 %collective-permute-start.27 = (bf16[144,384]{1,0:T(8,128)(2,1)S(1)}, bf16[144,384]{1,0:T(8,128)(2,1)S(1)}, u32[]{:S(2)}, u32[]{:S(2)}) collective-permute-start(bf16[144,384]{1,0:T(8,128)(2,1)S(1)} %get-tuple-element.75), channel_id=1, source_target_pairs={{0,8},{8,0},{16,24},{24,16},{1,9},{9,1},{17,25},{25,17},{2,10},{10... | collective-permute-start | bytes 331784 | tf_op jit(solution)/shard_map/ppermute | solution.py:16
  65.5 1.5 %shard_map.89 = (f32[27,128,256]{2,1,0:T(8,128)}, f32[8,384]{1,0:T(8,128)S(1)}) custom-call(s32[8]{0:T(128)S(1)} %stack.32.refs_0_, bf16[2,144,384]{2,1,0:T(8,128)(2,1)S(1)} %get-tuple-element.80.refs_1_, bf16[2,144,384]{2,1,0:T(8,128)(2,1)S(1)} %collective-permute-done.31.refs_2_, ...), custom_call_target="tpu_custom_call", output_to_operand_aliasing={{0}: (3, {})} | custom-call | flops 1 | bytes 1 | tf_op jit(solution)/shard_map/pallas_call | solution.py:254
  70.7 2.1 %shard_map.90 = (f32[27,128,256]{2,1,0:T(8,128)}, f32[8,384]{1,0:T(8,128)}) custom-call(s32[8]{0:T(128)S(1)} %stack.32.refs_0_, bf16[288,384]{1,0:T(8,128)(2,1)S(1)} %pad_maximum_fusion.refs_1_, bf16[288,384]{1,0:T(8,128)(2,1)S(1)} %collective-permute-done.33.refs_2_, f32[27,128,256]{2,1,0:T(8,128)} %get-tuple-element.84.refs_3_), custom_call_target="tpu_custom_call", output_to_operand_aliasing={{0}: (3, {})} | custom-call | flops 1 | bytes 1 | tf_op jit(solution)/shard_map/pallas_call | solution.py:254
  (88 shorter events, 28.1 us)
Async XLA Ops:
  1.8 6.4 %collective-permute-start.3 = (bf16[512,128]{1,0:T(8,128)(2,1)S(1)}, bf16[512,128]{1,0:T(8,128)(2,1)S(1)}, u32[]{:S(2)}, u32[]{:S(2)}) collective-permute-start(bf16[512,128]{1,0:T(8,128)(2,1)S(1)} %bitcast.28), channel_id=1, source_target_pairs={{0,4},{2,6},{4,0},{6,2},{1,5},{3,7},{5,1},{7,3},{8,12},{10,14},{12... | collective-permute-start | bytes 393224 | tf_op jit(solution)/shard_map/ppermute | solution.py:16
  9.0 5.1 %collective-permute-start.1 = (bf16[512,128]{1,0:T(8,128)(2,1)S(1)}, bf16[512,128]{1,0:T(8,128)(2,1)S(1)}, u32[]{:S(2)}, u32[]{:S(2)}) collective-permute-start(bf16[512,128]{1,0:T(8,128)(2,1)S(1)} %get-tuple-element.46), channel_id=1, source_target_pairs={{0,1},{1,0},{2,3},{3,2},{4,5},{5,4},{6,7},{7,6},{8,9},{9,8},{10,11... | collective-permute-start | bytes 393224 | tf_op jit(solution)/shard_map/ppermute | solution.py:16
  12.2 6.4 %collective-permute-start.5 = (bf16[512,128]{1,0:T(8,128)(2,1)S(1)}, bf16[512,128]{1,0:T(8,128)(2,1)S(1)}, u32[]{:S(2)}, u32[]{:S(2)}) collective-permute-start(bf16[512,128]{1,0:T(8,128)(2,1)S(1)} %get-tuple-element.52), channel_id=1, source_target_pairs={{0,1},{1,0},{2,3},{3,2},{4,5},{5,4},{6,7},{7,6},{8,9},{9,8},{10,11... | collective-permute-start | bytes 393224 | tf_op jit(solution)/shard_map/ppermute | solution.py:16
  14.8 4.8 %collective-permute-start.2 = (bf16[512,128]{1,0:T(8,128)(2,1)S(1)}, bf16[512,128]{1,0:T(8,128)(2,1)S(1)}, u32[]{:S(2)}, u32[]{:S(2)}) collective-permute-start(bf16[512,128]{1,0:T(8,128)(2,1)S(1)} %get-tuple-element.47.refs_5_), channel_id=1, source_target_pairs={{0,1},{1,0},{2,3},{3,2},{4,5},{5,4},{6,7},{7,6},{8,9},{9,8},{10,11... | collective-permute-start | bytes 393224 | tf_op jit(solution)/shard_map/ppermute | solution.py:16
  16.3 9.1 %collective-permute-start.9 = (bf16[512,128]{1,0:T(8,128)(2,1)S(1)}, bf16[512,128]{1,0:T(8,128)(2,1)S(1)}, u32[]{:S(2)}, u32[]{:S(2)}) collective-permute-start(bf16[512,128]{1,0:T(8,128)(2,1)S(1)} %bitcast.30), channel_id=1, source_target_pairs={{0,2},{2,0},{4,6},{6,4},{1,3},{3,1},{5,7},{7,5},{8,10},{10,8},{12,... | collective-permute-start | bytes 393224 | tf_op jit(solution)/shard_map/ppermute | solution.py:16
  17.4 5.2 %collective-permute-start.10 = (bf16[512,128]{1,0:T(8,128)(2,1)S(1)}, bf16[512,128]{1,0:T(8,128)(2,1)S(1)}, u32[]{:S(2)}, u32[]{:S(2)}) collective-permute-start(bf16[512,128]{1,0:T(8,128)(2,1)S(1)} %get-tuple-element.56), channel_id=1, source_target_pairs={{0,4},{2,6},{4,0},{6,2},{1,5},{3,7},{5,1},{7,3},{8,12},{10,14},{12... | collective-permute-start | bytes 393224 | tf_op jit(solution)/shard_map/ppermute | solution.py:16
  19.3 4.9 %collective-permute-start.6 = (bf16[512,128]{1,0:T(8,128)(2,1)S(1)}, bf16[512,128]{1,0:T(8,128)(2,1)S(1)}, u32[]{:S(2)}, u32[]{:S(2)}) collective-permute-start(bf16[512,128]{1,0:T(8,128)(2,1)S(1)} %get-tuple-element.53), channel_id=1, source_target_pairs={{0,1},{1,0},{2,3},{3,2},{4,5},{5,4},{6,7},{7,6},{8,9},{9,8},{10,11... | collective-permute-start | bytes 393224 | tf_op jit(solution)/shard_map/ppermute | solution.py:16
  19.7 6.0 %collective-permute-start.12 = (bf16[512,128]{1,0:T(8,128)(2,1)S(1)}, bf16[512,128]{1,0:T(8,128)(2,1)S(1)}, u32[]{:S(2)}, u32[]{:S(2)}) collective-permute-start(bf16[512,128]{1,0:T(8,128)(2,1)S(1)} %get-tuple-element.88.refs_2_), channel_id=1, source_target_pairs={{0,4},{2,6},{4,0},{6,2},{1,5},{3,7},{5,1},{7,3},{8,12},{10,14},{12... | collective-permute-start | bytes 393224 | tf_op jit(solution)/shard_map/ppermute | solution.py:16
  20.6 6.6 %collective-permute-start.7 = (bf16[512,128]{1,0:T(8,128)(2,1)S(1)}, bf16[512,128]{1,0:T(8,128)(2,1)S(1)}, u32[]{:S(2)}, u32[]{:S(2)}) collective-permute-start(bf16[512,128]{1,0:T(8,128)(2,1)S(1)} %get-tuple-element.89.refs_2_.refs_1_), channel_id=1, source_target_pairs={{0,2},{2,0},{4,6},{6,4},{1,3},{3,1},{5,7},{7,5},{8,10},{10,8},{12,... | collective-permute-start | bytes 393224 | tf_op jit(solution)/shard_map/ppermute | solution.py:16
  25.4 5.3 %collective-permute-start.15 = (bf16[512,128]{1,0:T(8,128)(2,1)S(1)}, bf16[512,128]{1,0:T(8,128)(2,1)S(1)}, u32[]{:S(2)}, u32[]{:S(2)}) collective-permute-start(bf16[512,128]{1,0:T(8,128)(2,1)S(1)} %get-tuple-element.86.refs_4_), channel_id=1, source_target_pairs={{0,4},{2,6},{4,0},{6,2},{1,5},{3,7},{5,1},{7,3},{8,12},{10,14},{12... | collective-permute-start | bytes 393224 | tf_op jit(solution)/shard_map/ppermute | solution.py:16
  33.7 5.3 %collective-permute-start.17 = (bf16[144,384]{1,0:T(8,128)(2,1)S(1)}, bf16[144,384]{1,0:T(8,128)(2,1)S(1)}, u32[]{:S(2)}, u32[]{:S(2)}) collective-permute-start(bf16[144,384]{1,0:T(8,128)(2,1)S(1)} %get-tuple-element.64), channel_id=1, source_target_pairs={{0,8},{8,0},{16,24},{24,16},{1,9},{9,1},{17,25},{25,17},{2,10},{10... | collective-permute-start | bytes 331784 | tf_op jit(solution)/shard_map/ppermute | solution.py:16
  35.0 8.9 %collective-permute-start.8 = (bf16[512,128]{1,0:T(8,128)(2,1)S(1)}, bf16[512,128]{1,0:T(8,128)(2,1)S(1)}, u32[]{:S(2)}, u32[]{:S(2)}) collective-permute-start(bf16[512,128]{1,0:T(8,128)(2,1)S(1)} %get-tuple-element.88.refs_2_), channel_id=1, source_target_pairs={{0,2},{2,0},{4,6},{6,4},{1,3},{3,1},{5,7},{7,5},{8,10},{10,8},{12,... | collective-permute-start | bytes 393224 | tf_op jit(solution)/shard_map/ppermute | solution.py:16
  35.6 11.6 %collective-permute-start.20 = (f32[8,384]{1,0:T(8,128)S(1)}, f32[8,384]{1,0:T(8,128)S(1)}, u32[]{:S(2)}, u32[]{:S(2)}) collective-permute-start(f32[8,384]{1,0:T(8,128)S(1)} %get-tuple-element.71), channel_id=1, source_target_pairs={{0,16},{8,24},{16,0},{24,8},{1,17},{9,25},{17,1},{25,9},{2,18},{10... | collective-permute-start | bytes 36872 | tf_op jit(solution)/shard_map/ppermute | solution.py:16
  37.9 9.3 %collective-permute-start.21 = (bf16[144,384]{1,0:T(8,128)(2,1)S(1)}, bf16[144,384]{1,0:T(8,128)(2,1)S(1)}, u32[]{:S(2)}, u32[]{:S(2)}) collective-permute-start(bf16[144,384]{1,0:T(8,128)(2,1)S(1)} %get-tuple-element.73), channel_id=1, source_target_pairs={{0,8},{8,0},{16,24},{24,16},{1,9},{9,1},{17,25},{25,17},{2,10},{10... | collective-permute-start | bytes 331784 | tf_op jit(solution)/shard_map/ppermute | solution.py:16
  38.0 4.5 %collective-permute-start.18 = (bf16[512,128]{1,0:T(8,128)(2,1)S(1)}, bf16[512,128]{1,0:T(8,128)(2,1)S(1)}, u32[]{:S(2)}, u32[]{:S(2)}) collective-permute-start(bf16[512,128]{1,0:T(8,128)(2,1)S(1)} %get-tuple-element.65), channel_id=1, source_target_pairs={{0,4},{2,6},{4,0},{6,2},{1,5},{3,7},{5,1},{7,3},{8,12},{10,14},{12... | collective-permute-start | bytes 393224 | tf_op jit(solution)/shard_map/ppermute | solution.py:16
  39.0 8.3 %collective-permute-start.22 = (bf16[144,384]{1,0:T(8,128)(2,1)S(1)}, bf16[144,384]{1,0:T(8,128)(2,1)S(1)}, u32[]{:S(2)}, u32[]{:S(2)}) collective-permute-start(bf16[144,384]{1,0:T(8,128)(2,1)S(1)} %add_convert_fusion.refs_10_), channel_id=1, source_target_pairs={{0,16},{8,24},{16,0},{24,8},{1,17},{9,25},{17,1},{25,9},{2,18},{10... | collective-permute-start | bytes 331784 | tf_op jit(solution)/shard_map/ppermute | solution.py:16
  42.5 7.3 %collective-permute-start.19 = (bf16[512,128]{1,0:T(8,128)(2,1)S(1)}, bf16[512,128]{1,0:T(8,128)(2,1)S(1)}, u32[]{:S(2)}, u32[]{:S(2)}) collective-permute-start(bf16[512,128]{1,0:T(8,128)(2,1)S(1)} %collective-permute-done.18.refs_11_), channel_id=1, source_target_pairs={{0,2},{2,0},{4,6},{6,4},{1,3},{3,1},{5,7},{7,5},{8,10},{10,8},{12,... | collective-permute-start | bytes 393224 | tf_op jit(solution)/shard_map/ppermute | solution.py:16
  47.3 7.4 %collective-permute-start.25 = (bf16[144,384]{1,0:T(8,128)(2,1)S(1)}, bf16[144,384]{1,0:T(8,128)(2,1)S(1)}, u32[]{:S(2)}, u32[]{:S(2)}) collective-permute-start(bf16[144,384]{1,0:T(8,128)(2,1)S(1)} %bitcast_select_fusion.2.refs_1_), channel_id=1, source_target_pairs={{0,16},{8,24},{16,0},{24,8},{1,17},{9,25},{17,1},{25,9},{2,18},{10... | collective-permute-start | bytes 331784 | tf_op jit(solution)/shard_map/ppermute | solution.py:16
  47.4 7.3 %collective-permute-start.24 = (bf16[144,384]{1,0:T(8,128)(2,1)S(1)}, bf16[144,384]{1,0:T(8,128)(2,1)S(1)}, u32[]{:S(2)}, u32[]{:S(2)}) collective-permute-start(bf16[144,384]{1,0:T(8,128)(2,1)S(1)} %bitcast_select_fusion.2.refs_1_), channel_id=1, source_target_pairs={{0,8},{8,0},{16,24},{24,16},{1,9},{9,1},{17,25},{25,17},{2,10},{10... | collective-permute-start | bytes 331784 | tf_op jit(solution)/shard_map/ppermute | solution.py:16
  49.1 5.6 %collective-permute-start.23 = (bf16[144,384]{1,0:T(8,128)(2,1)S(1)}, bf16[144,384]{1,0:T(8,128)(2,1)S(1)}, u32[]{:S(2)}, u32[]{:S(2)}) collective-permute-start(bf16[144,384]{1,0:T(8,128)(2,1)S(1)} %bitcast_select_fusion.2.refs_1_), channel_id=1, source_target_pairs={{0,4},{2,6},{4,0},{6,2},{1,5},{3,7},{5,1},{7,3},{8,12},{10,14},{12... | collective-permute-start | bytes 331784 | tf_op jit(solution)/shard_map/ppermute | solution.py:16
  57.0 4.6 %collective-permute-start.28 = (bf16[144,384]{1,0:T(8,128)(2,1)S(1)}, bf16[144,384]{1,0:T(8,128)(2,1)S(1)}, u32[]{:S(2)}, u32[]{:S(2)}) collective-permute-start(bf16[144,384]{1,0:T(8,128)(2,1)S(1)} %get-tuple-element.76), channel_id=1, source_target_pairs={{0,8},{8,0},{16,24},{24,16},{1,9},{9,1},{17,25},{25,17},{2,10},{10... | collective-permute-start | bytes 331784 | tf_op jit(solution)/shard_map/ppermute | solution.py:16
  57.0 4.6 %collective-permute-start.29 = (bf16[144,384]{1,0:T(8,128)(2,1)S(1)}, bf16[144,384]{1,0:T(8,128)(2,1)S(1)}, u32[]{:S(2)}, u32[]{:S(2)}) collective-permute-start(bf16[144,384]{1,0:T(8,128)(2,1)S(1)} %get-tuple-element.77), channel_id=1, source_target_pairs={{0,4},{2,6},{4,0},{6,2},{1,5},{3,7},{5,1},{7,3},{8,12},{10,14},{12... | collective-permute-start | bytes 331784 | tf_op jit(solution)/shard_map/ppermute | solution.py:16
  63.1 4.9 %collective-permute-start.32 = (bf16[160,384]{1,0:T(8,128)(2,1)S(1)}, bf16[160,384]{1,0:T(8,128)(2,1)S(1)}, u32[]{:S(2)}, u32[]{:S(2)}) collective-permute-start(bf16[160,384]{1,0:T(8,128)(2,1)S(1)} %get-tuple-element.83), channel_id=1, source_target_pairs={{0,4},{2,6},{4,0},{6,2},{1,5},{3,7},{5,1},{7,3},{8,12},{10,14},{12... | collective-permute-start | bytes 368648 | tf_op jit(solution)/shard_map/ppermute | solution.py:16
  64.0 4.3 %collective-permute-start.27 = (bf16[144,384]{1,0:T(8,128)(2,1)S(1)}, bf16[144,384]{1,0:T(8,128)(2,1)S(1)}, u32[]{:S(2)}, u32[]{:S(2)}) collective-permute-start(bf16[144,384]{1,0:T(8,128)(2,1)S(1)} %get-tuple-element.75), channel_id=1, source_target_pairs={{0,8},{8,0},{16,24},{24,16},{1,9},{9,1},{17,25},{25,17},{2,10},{10... | collective-permute-start | bytes 331784 | tf_op jit(solution)/shard_map/ppermute | solution.py:16
  (14 other events, 49.2 us)

commit v5 on v4

--- a/solution.py
+++ b/solution.py
@@ -16,18 +16,24 @@
     return lax.ppermute(value, axis, [(i, i ^ bit) for i in range(lax.axis_size(axis))])
 
 
-def vmem_call(body, outs, scratch, flops, *args, left=(), after=(), limit=20):
+def position():
+    s, z, y = lax.axis_index("slab"), lax.axis_index("dp"), lax.axis_index("chan")
+    odd = s & 1
+    beside = jnp.where((s == 0) | (s == lax.axis_size("slab") - 1), 0, 1)
+    return odd, y, s & 3, odd, z, z, (s >> 1) & 1, beside
+
+
+def vmem_call(body, outs, scratch, flops, *args, after=(), limit=20):
     shapes = [jax.ShapeDtypeStruct(s, d) for s, d in outs]
     count, waited = len(args), len(after)
 
     def inner(*refs):
-        body(*refs[:count], *refs[count + waited :])
-
-    specs = [pl.BlockSpec(memory_space=pl.ANY if n in left else pltpu.VMEM) for n in range(1, count)]
+        body(position(), *refs[:count], *refs[count + waited :])
+
     return pl.pallas_call(
         inner,
         out_shape=shapes,
-        in_specs=[pl.BlockSpec(memory_space=pltpu.SMEM)] + specs + [pl.BlockSpec(memory_space=pl.ANY)] * waited,
+        in_specs=[pl.BlockSpec(memory_space=pltpu.VMEM)] * count + [pl.BlockSpec(memory_space=pl.ANY)] * waited,
         out_specs=[pl.BlockSpec(memory_space=pltpu.VMEM)] * len(shapes),
         scratch_shapes=scratch,
         compiler_params=pltpu.CompilerParams(vmem_limit_bytes=limit * MIB),
@@ -242,25 +248,23 @@
     done[...] = jnp.zeros_like(done)
 
 
-def spread(body, shape, small, after, pos, *arrays, alias=False):
+def spread(body, shape, small, *arrays, alias=False):
     whole = pl.BlockSpec(memory_space=pltpu.VMEM)
     anywhere = pl.BlockSpec(memory_space=pl.ANY)
-    count, waited = 1 + len(arrays), len(after)
 
     def inner(*refs):
-        body(*refs[:count], *refs[count + waited :])
-
-    specs = [pl.BlockSpec(memory_space=pltpu.SMEM)] + [whole] * (len(arrays) - alias) + [anywhere] * alias
+        body(position(), *refs)
+
     return pl.pallas_call(
         inner,
         out_shape=[jax.ShapeDtypeStruct(shape, F32), jax.ShapeDtypeStruct(*small)],
-        in_specs=specs + [anywhere] * waited,
+        in_specs=[whole] * (len(arrays) - alias) + [anywhere] * alias,
         out_specs=[anywhere, whole],
         scratch_shapes=[pltpu.VMEM((8, shape[0], 16, shape[2] // 2), F32), pltpu.SemaphoreType.DMA((8,))],
-        input_output_aliases={count - 1: 0} if alias else {},
+        input_output_aliases={len(arrays) - 1: 0} if alias else {},
         compiler_params=pltpu.CompilerParams(vmem_limit_bytes=20 * MIB),
         cost_estimate=pl.CostEstimate(flops=1, bytes_accessed=1, transcendentals=0),
-    )(pos, *arrays, *after)
+    )(*arrays)
 
 
 def whole(x, keep, other):
@@ -315,8 +319,6 @@
     slabs = lax.axis_size("slab")
     s, z, y = lax.axis_index("slab"), lax.axis_index("dp"), lax.axis_index("chan")
     odd, mine, x = s % 2, s % 4, (s // 2) % 2
-    beside = jnp.where((s == 0) | (s == slabs - 1), 0, 1)
-    pos = jnp.stack([odd, y, mine, odd, z, z, x, beside]).astype(jnp.int32)
     factor = float(samples * cells * slabs * lax.axis_size("dp")) ** -0.5
     padded = plane + 2 * ny
     macs = plane * 27 * local_in * outputs
@@ -338,19 +340,19 @@
         [wide, thin, ((2, padded, 3 * local_in), BF), (w.shape, BF), ((8, 128), F32)],
         one + [pltpu.SemaphoreType.DMA(())],
         macs,
-        pos, vol_n, vol_f, near, w,
+        vol_n, vol_f, near, w,
     )
     recv_n = swap(send_n, "chan", 1)
     cx_f = swap(held_back(x_f, done_n), "slab", 1)
     beyond = cx_f
     if slabs > 4:
         beyond = jnp.where((mine == 0) | (mine == 3), next_pair(vol_f), beyond)
-    own_f, send_f = vmem_call(functools.partial(far_body, ny), [wide, thin], one, macs, pos, beyond, kept, held)
+    own_f, send_f = vmem_call(functools.partial(far_body, ny), [wide, thin], one, macs, beyond, kept, held)
     recv_f = swap(send_f, "chan", 1)
 
     bias_row, cot = bias.reshape(1, local_out), cotangent.reshape(planes, plane, local_out)
     act_n, g_n, vol_n2 = vmem_call(
-        near_gate_body, [thin, thin, thin], [], 0, pos, own_n, recv_n, bias_row, cot, vol_n
+        near_gate_body, [thin, thin, thin], [], 0, own_n, recv_n, bias_row, cot, vol_n
     )
     x_n, core_vf = swap(vol_n2, "slab", 2), swap(vol_f, "slab", 1)
     cx_n = swap(x_n, "slab", 1)
@@ -360,9 +362,9 @@
         [((4 * planes + 4, 3 * local_in // 2, plane), BF)],
         [],
         0,
-        pos, vol_n, vol_f, near, core_vf, x_n, x_f, cx_n, cx_f, ends,
+        vol_n, vol_f, near, core_vf, x_n, x_f, cx_n, cx_f, ends,
     )[0]
-    act_f, g_f = vmem_call(far_gate_body, [thin, thin], [], 0, pos, own_f, recv_f, bias_row, cot, after=(g_n,))
+    act_f, g_f = vmem_call(far_gate_body, [thin, thin], [], 0, own_f, recv_f, bias_row, cot, after=(g_n,))
     g_fy = swap(g_f, "chan", 1)
     lanes = 3 * local_out
 
@@ -378,13 +380,13 @@
     sums_of = [(acc_shape, F32), ((8, lanes), F32)]
     four, two = pltpu.VMEM((4, padded, lanes), BF), pltpu.VMEM((2, padded, lanes), BF)
     first = functools.partial(first_kernel_body, ny)
-    acc0, total0 = vmem_call(first, sums_of, [four], 2 * macs, pos, vt, keep_n, core_n[0], keep_f, core_f)
+    acc0, total0 = vmem_call(first, sums_of, [four], 2 * macs, vt, keep_n, core_n[0], keep_f, core_f)
     second = functools.partial(second_kernel_body, ny)
-    acc0, total0 = vmem_call(second, sums_of, [two], macs, pos, vt, got_n, core_n[1], acc0, total0)
+    acc0, total0 = vmem_call(second, sums_of, [two], macs, vt, got_n, core_n[1], acc0, total0)
     last_f = swap(held_back(got_f, total0[:, :local_out]), "slab", 1)
     single = pltpu.VMEM((1, padded, lanes), BF)
     acc1, total1 = vmem_call(
-        functools.partial(next_kernel_body, 2, ny), sums_of, [single], macs, pos, vt, got_f, acc0, total0
+        functools.partial(next_kernel_body, 2, ny), sums_of, [single], macs, vt, got_f, acc0, total0
     )
     rows = 9 * local_in // 8
     cut = [((rows, lanes), F32), ((rows, lanes), BF), ((rows, lanes), F32), ((rows, lanes), BF)]
@@ -394,17 +396,17 @@
             cut + [((8, lanes), F32), thin],
             [single, pltpu.VMEM(acc_shape, F32)],
             macs,
-            pos, vt, last_f, acc1, total1, keep_f,
+            vt, last_f, acc1, total1, keep_f,
         )
     else:
         acc, total = vmem_call(
-            functools.partial(next_kernel_body, 3, ny), sums_of, [single], macs, pos, vt, last_f, acc1, total1
+            functools.partial(next_kernel_body, 3, ny), sums_of, [single], macs, vt, last_f, acc1, total1
         )
         bit = 4
         while bit < slabs:
             acc, total = acc + swap(acc, "slab", bit), total + swap(total, "slab", bit)
             bit *= 2
-        keep, s1, s2, s3 = vmem_call(cut_body, cut, [], 0, pos, acc)
+        keep, s1, s2, s3 = vmem_call(cut_body, cut, [], 0, acc)
         sent = keep_f
     r3, r1, total_z2 = swap(s3, "dp", 1), swap(s1, "dp", 1), swap(total, "dp", 2)
     merged, total_a = (s2 + r3.astype(F32)).astype(BF), total + total_z2
@@ -420,7 +422,7 @@
         ],
         [ig_buf],
         2 * macs,
-        pos, keep_n, send_n, keep_f, send_f, core_n[0], swap(send_n, "slab", 1), wt, act_n, act_f,
+        keep_n, send_n, keep_f, send_f, core_n[0], swap(send_n, "slab", 1), wt, act_n, act_f,
         after=(merged, sent_x),
     )
     far_keep = last_f
@@ -434,7 +436,7 @@
         [((planes, plane, local_in), BF), ((8, lanes), F32)],
         [pltpu.VMEM((1, padded, 3 * outputs), BF)],
         0,
-        pos, far_keep, far_send, wt, partial, ig_n,
+        far_keep, far_send, wt, partial, ig_n,
     )
     quarter = held_back(((keep + r1.astype(F32) + r2.astype(F32)) * factor).astype(BF), ig_n_done, total_z2)
     total_z1 = swap(total_a, "dp", 1)
@@ -447,25 +449,25 @@
         [(quarter.shape, BF)] * 3 + [((4,) + quarter.shape, BF)],
         [],
         0,
-        pos, quarter, x0, q1, q2,
+        quarter, x0, q1, q2,
         after=(total_z1, ig_done),
     )
     q3, x2, x1, core = swap(one_z, "dp", 1), swap(one_x, "slab", 2), swap(x0_z, "dp", 1), swap(four_c, "slab", 1)
-    out, done = spread(first_spread_body, out_shape, token, (), pos, four_c, core)
+    out, done = spread(first_spread_body, out_shape, token, four_c, core)
     last_x, two_c = vmem_call(
         next_round_body,
         [((rows + 16, lanes), BF), ((2,) + quarter.shape, BF)],
         [],
         0,
-        pos, q3, x2, total_b,
+        q3, x2, total_b,
         after=(done,),
     )
     x3, core_b = swap(last_x, "slab", 2), swap(two_c, "slab", 1)
-    out, done = spread(next_spread_body, out_shape, token, (), pos, two_c, core_b, out, alias=True)
+    out, done = spread(next_spread_body, out_shape, token, two_c, core_b, out, alias=True)
     x3 = held_back(x3, done)
     pair_x = jnp.concatenate([x1, x3[:rows]], axis=0)
     core_x = swap(pair_x, "slab", 1)
-    weight_grad, _ = spread(last_spread_body, out_shape, token, (), pos, pair_x, core_x, out, alias=True)
+    weight_grad, _ = spread(last_spread_body, out_shape, token, pair_x, core_x, out, alias=True)
     tail = x3[rows : rows + 1].astype(F32).reshape(3, local_out)
     bias_grad = jnp.where(x == y, total_b[0, :local_out], tail[0] + tail[1] + tail[2]) * factor
     shape = (samples, planes, nx, ny)

time: 73.3 us -> 69.8 us (0.952)
  Pallas kernels: 23.9 us -> 15.3 us
  waiting for transfers between devices: 9.93 us -> 14.3 us
  starting transfers between devices: 34.7 us -> 35.6 us
    pallas_call x13, Pallas kernels: 18.4 us -> 11.5 us  [vmem_call(): pl.pallas_call(inner, out_shape=shapes, in_specs=[pl.BlockSpec(memory_spa...]
    ppermute x34, waiting for transfers between devices: 9.93 us -> 14.3 us  [swap(): lax.ppermute(value, axis, [(i, i ^ bit) for i in range(lax.axis_size(axis...]
    pallas_call x3, Pallas kernels: 5.47 us -> 3.86 us  [spread(): pl.pallas_call(inner, out_shape=[jax.ShapeDtypeStruct(shape, F32), jax.Sh...]
    ppermute x34, starting transfers between devices: 34.7 us -> 35.6 us  [swap(): lax.ppermute(value, axis, [(i, i ^ bit) for i in range(lax.axis_size(axis...]
  transfers between devices with their start and end apart: 34 -> 34, of which waited for: 11 -> 14; matrix products, arithmetic and copies ran while one was open for 1% -> 1% of each run, Pallas kernels for 27% -> 19%
where the time goes in v5:
time: 69.8 us; the launch traced here: 69.3 us
  starting transfers between devices  35.6 us (51%)
  Pallas kernels  15.3 us (22%)
  waiting for transfers between devices  14.3 us (20%)
  other arithmetic  1.76 us (3%)
  local copies, waits for them, and re-layouts  1.54 us (2%)
  between operations  0.87 us (1%)
    ppermute x34, starting transfers between devices, swap(): lax.ppermute(value, axis, [(i, i ^ bit) for i in range(lax.axis_size(axis...  35.6 us
    ppermute x34, waiting for transfers between devices, swap(): lax.ppermute(value, axis, [(i, i ^ bit) for i in range(lax.axis_size(axis...  14.3 us
    pallas_call x13, Pallas kernels, vmem_call(): pl.pallas_call(inner, out_shape=shapes, in_specs=[pl.BlockSpec(memory_spa...  11.5 us
    pallas_call x3, Pallas kernels, spread(): pl.pallas_call(inner, out_shape=[jax.ShapeDtypeStruct(shape, F32), jax.Sh...  3.86 us
    unnamed x8, local copies, waits for them, and re-layouts  1.49 us
  transfers between devices with their start and end apart: 34, of which 14 were waited for; matrix products, arithmetic and copies ran while one was open for 1% of the time, Pallas kernels for 19%

profile of v5, /device:TPU:1, one launch (start us, length us, event | category | flops | bytes accessed | tf_op | source)
XLA Modules:
  0.0 69.3 jit_solution(12067196901568946109)
XLA Ops:
  1.8 2.7 %collective-permute-start.3 = (bf16[512,128]{1,0:T(8,128)(2,1)S(1)}, bf16[512,128]{1,0:T(8,128)(2,1)S(1)}, u32[]{:S(2)}, u32[]{:S(2)}) collective-permute-start(bf16[512,128]{1,0:T(8,128)(2,1)S(1)} %bitcast.22), channel_id=1, source_target_pairs={{0,4},{2,6},{4,0},{6,2},{1,5},{3,7},{5,1},{7,3},{8,12},{10,14},{12... | collective-permute-start | bytes 393224 | tf_op jit(solution)/shard_map/ppermute | solution.py:16
  4.4 1.5 %copy-done = bf16[3,3,3,128,256]{4,3,2,1,0:T(8,128)(2,1)S(1)} copy-done((bf16[3,3,3,128,256]{4,3,2,1,0:T(8,128)(2,1)S(1)}, bf16[3,3,3,128,256]{4,3,2,1,0:T(8,128)(2,1)}, u32[]{:S(2)}) %copy-start) | copy-done | bytes 1769496
  5.9 1.5 %shard_map.75 = (f32[512,128]{1,0:T(8,128)S(1)}, bf16[512,128]{1,0:T(8,128)(2,1)S(1)}, bf16[2,544,384]{2,1,0:T(8,128)(2,1)S(1)}, bf16[3,1152,256]{2,1,0:T(8,128)(2,1)S(1)}, f32[8,128]{1,0:T(8,128)S(1)}) custom-call(bf16[512,128]{1,0:T(8,128)(2,1)S(1)} %bitcast.27, bf16[512,128]{1,0:T(8,128)(2,1)S(1)} %bitcast.23, ...), custom_call_target="tpu_custom_call" | custom-call | flops 2811939328 | bytes 1048576 | tf_op jit(solution)/shard_map/pallas_call | solution.py:33
  9.0 1.5 %collective-permute-start.1 = (bf16[512,128]{1,0:T(8,128)(2,1)S(1)}, bf16[512,128]{1,0:T(8,128)(2,1)S(1)}, u32[]{:S(2)}, u32[]{:S(2)}) collective-permute-start(bf16[512,128]{1,0:T(8,128)(2,1)S(1)} %get-tuple-element.46), channel_id=1, source_target_pairs={{0,1},{1,0},{2,3},{3,2},{4,5},{5,4},{6,7},{7,6},{8,9},{9,8},{10,11... | collective-permute-start | bytes 393224 | tf_op jit(solution)/shard_map/ppermute | solution.py:16
  12.7 1.4 %collective-permute-done.1.refs_1_ = bf16[512,128]{1,0:T(8,128)(2,1)S(1)} collective-permute-done((bf16[512,128]{1,0:T(8,128)(2,1)S(1)}, bf16[512,128]{1,0:T(8,128)(2,1)S(1)}, u32[]{:S(2)}, u32[]{:S(2)}) %collective-permute-start.1) | collective-permute-done | bytes 131104 | tf_op jit(solution)/shard_map/ppermute | solution.py:16
  14.2 1.5 %collective-permute-start.2 = (bf16[512,128]{1,0:T(8,128)(2,1)S(1)}, bf16[512,128]{1,0:T(8,128)(2,1)S(1)}, u32[]{:S(2)}, u32[]{:S(2)}) collective-permute-start(bf16[512,128]{1,0:T(8,128)(2,1)S(1)} %get-tuple-element.47.refs_4_), channel_id=1, source_target_pairs={{0,1},{1,0},{2,3},{3,2},{4,5},{5,4},{6,7},{7,6},{8,9},{9,8},{10,11... | collective-permute-start | bytes 393224 | tf_op jit(solution)/shard_map/ppermute | solution.py:16
  15.8 1.6 %collective-permute-start.9 = (bf16[512,128]{1,0:T(8,128)(2,1)S(1)}, bf16[512,128]{1,0:T(8,128)(2,1)S(1)}, u32[]{:S(2)}, u32[]{:S(2)}) collective-permute-start(bf16[512,128]{1,0:T(8,128)(2,1)S(1)} %bitcast.24), channel_id=1, source_target_pairs={{0,2},{2,0},{4,6},{6,4},{1,3},{3,1},{5,7},{7,5},{8,10},{10,8},{12,... | collective-permute-start | bytes 393224 | tf_op jit(solution)/shard_map/ppermute | solution.py:16
  18.9 1.5 %collective-permute-start.12 = (bf16[512,128]{1,0:T(8,128)(2,1)S(1)}, bf16[512,128]{1,0:T(8,128)(2,1)S(1)}, u32[]{:S(2)}, u32[]{:S(2)}) collective-permute-start(bf16[512,128]{1,0:T(8,128)(2,1)S(1)} %get-tuple-element.88.refs_1_), channel_id=1, source_target_pairs={{0,4},{2,6},{4,0},{6,2},{1,5},{3,7},{5,1},{7,3},{8,12},{10,14},{12... | collective-permute-start | bytes 393224 | tf_op jit(solution)/shard_map/ppermute | solution.py:16
  20.4 2.0 %collective-permute-start.7 = (bf16[512,128]{1,0:T(8,128)(2,1)S(1)}, bf16[512,128]{1,0:T(8,128)(2,1)S(1)}, u32[]{:S(2)}, u32[]{:S(2)}) collective-permute-start(bf16[512,128]{1,0:T(8,128)(2,1)S(1)} %get-tuple-element.89.refs_1_.refs_0_), channel_id=1, source_target_pairs={{0,2},{2,0},{4,6},{6,4},{1,3},{3,1},{5,7},{7,5},{8,10},{10,8},{12,... | collective-permute-start | bytes 393224 | tf_op jit(solution)/shard_map/ppermute | solution.py:16
  26.5 1.6 %shard_map.80 = (f32[3,192,384]{2,1,0:T(8,128)S(1)}, f32[8,384]{1,0:T(8,128)S(1)}) custom-call(bf16[12,192,512]{2,1,0:T(8,128)(2,1)S(1)} %shard_map.79.refs_0_, bf16[512,128]{1,0:T(8,128)(2,1)S(1)} %get-tuple-element.89.refs_1_.refs_0_, bf16[512,128]{1,0:T(8,128)(2,1)S(1)} %collective-permute-done.7.refs_2_.refs_4_, ...), custom_call_target="tpu_custom_call" | custom-call | flops 4623878656 | bytes 1048576 | tf_op jit(solution)/shard_map/pallas_call | solution.py:33
  34.4 2.3 %collective-permute-start.20 = (f32[8,384]{1,0:T(8,128)S(1)}, f32[8,384]{1,0:T(8,128)S(1)}, u32[]{:S(2)}, u32[]{:S(2)}) collective-permute-start(f32[8,384]{1,0:T(8,128)S(1)} %get-tuple-element.71), channel_id=1, source_target_pairs={{0,16},{8,24},{16,0},{24,8},{1,17},{9,25},{17,1},{25,9},{2,18},{10... | collective-permute-start | bytes 36872 | tf_op jit(solution)/shard_map/ppermute | solution.py:16
  37.2 2.0 %collective-permute-start.22 = (bf16[144,384]{1,0:T(8,128)(2,1)S(1)}, bf16[144,384]{1,0:T(8,128)(2,1)S(1)}, u32[]{:S(2)}, u32[]{:S(2)}) collective-permute-start(bf16[144,384]{1,0:T(8,128)(2,1)S(1)} %add_convert_fusion.refs_9_), channel_id=1, source_target_pairs={{0,16},{8,24},{16,0},{24,8},{1,17},{9,25},{17,1},{25,9},{2,18},{10... | collective-permute-start | bytes 331784 | tf_op jit(solution)/shard_map/ppermute | solution.py:16
  39.1 2.2 %collective-permute-done.18.refs_10_ = bf16[512,128]{1,0:T(8,128)(2,1)S(1)} collective-permute-done((bf16[512,128]{1,0:T(8,128)(2,1)S(1)}, bf16[512,128]{1,0:T(8,128)(2,1)S(1)}, u32[]{:S(2)}, u32[]{:S(2)}) %collective-permute-start.18) | collective-permute-done | bytes 131104 | tf_op jit(solution)/shard_map/ppermute | solution.py:16
  41.4 1.4 %collective-permute-start.19 = (bf16[512,128]{1,0:T(8,128)(2,1)S(1)}, bf16[512,128]{1,0:T(8,128)(2,1)S(1)}, u32[]{:S(2)}, u32[]{:S(2)}) collective-permute-start(bf16[512,128]{1,0:T(8,128)(2,1)S(1)} %collective-permute-done.18.refs_10_), channel_id=1, source_target_pairs={{0,2},{2,0},{4,6},{6,4},{1,3},{3,1},{5,7},{7,5},{8,10},{10,8},{12,... | collective-permute-start | bytes 393224 | tf_op jit(solution)/shard_map/ppermute | solution.py:16
  42.8 2.7 %shard_map.84 = (bf16[512,128]{1,0:T(8,128)(2,1)S(1)}, f32[512,128]{1,0:T(8,128)S(1)}, bf16[2,512,128]{2,1,0:T(8,128)(2,1)}, f32[8,384]{1,0:T(8,128)S(1)}) custom-call(bf16[512,128]{1,0:T(8,128)(2,1)S(1)} %get-tuple-element.89.refs_1_.refs_0_, bf16[512,128]{1,0:T(8,128)(2,1)S(1)} %get-tuple-element.88.refs_1_, ...), custom_call_target="tpu_custom_call" | custom-call | flops 4623878656 | bytes 1048576 | tf_op jit(solution)/shard_map/pallas_call | solution.py:33
  45.7 2.0 %collective-permute-start.24 = (bf16[144,384]{1,0:T(8,128)(2,1)S(1)}, bf16[144,384]{1,0:T(8,128)(2,1)S(1)}, u32[]{:S(2)}, u32[]{:S(2)}) collective-permute-start(bf16[144,384]{1,0:T(8,128)(2,1)S(1)} %bitcast_select_fusion.2.refs_0_), channel_id=1, source_target_pairs={{0,8},{8,0},{16,24},{24,16},{1,9},{9,1},{17,25},{25,17},{2,10},{10... | collective-permute-start | bytes 331784 | tf_op jit(solution)/shard_map/ppermute | solution.py:16
  48.0 1.6 %shard_map.85 = (bf16[2,512,128]{2,1,0:T(8,128)(2,1)}, f32[8,384]{1,0:T(8,128)S(1)}) custom-call(bf16[512,128]{1,0:T(8,128)(2,1)S(1)} %collective-permute-done.16.refs_1_.refs_0_, bf16[512,128]{1,0:T(8,128)(2,1)S(1)} %collective-permute-done.19.refs_1_, bf16[27,128,256]{2,1,0:T(8,128)(2,1)S(1)} %bitcast.32, f32[512,128]{1,0:T(8,128)S(1)} %get-tuple-element.67.refs_3_, ...), custom_call_target="tpu_custom_call" | custom-call | flops 1000000000 | bytes 1048576 | tf_op jit(solution)/shard_map/pallas_call | solution.py:33
  49.6 2.1 %collective-permute-done.26.refs_4_ = f32[8,384]{1,0:T(8,128)S(1)} collective-permute-done((f32[8,384]{1,0:T(8,128)S(1)}, f32[8,384]{1,0:T(8,128)S(1)}, u32[]{:S(2)}, u32[]{:S(2)}) %collective-permute-start.26) | collective-permute-done | bytes 12320 | tf_op jit(solution)/shard_map/ppermute | solution.py:16
  51.7 1.4 %collective-permute-done.25.refs_3_ = bf16[144,384]{1,0:T(8,128)(2,1)S(1)} collective-permute-done((bf16[144,384]{1,0:T(8,128)(2,1)S(1)}, bf16[144,384]{1,0:T(8,128)(2,1)S(1)}, u32[]{:S(2)}, u32[]{:S(2)}) %collective-permute-start.25) | collective-permute-done | bytes 110624 | tf_op jit(solution)/shard_map/ppermute | solution.py:16
  53.1 1.6 %collective-permute-start.30 = (bf16[4,144,384]{2,1,0:T(8,128)(2,1)S(1)}, bf16[4,144,384]{2,1,0:T(8,128)(2,1)S(1)}, u32[]{:S(2)}, u32[]{:S(2)}) collective-permute-start(bf16[4,144,384]{2,1,0:T(8,128)(2,1)S(1)} %get-tuple-element.78.refs_0_), channel_id=1, source_target_pairs={{0,2},{2,0},{4,6},{6,4},{1,3},{3,1},{5,7},{7,5},{8,10},{10,8},{12,... | collective-permute-start | bytes 1327112 | tf_op jit(solution)/shard_map/ppermute | solution.py:16
  57.4 1.9 %collective-permute-done.28.refs_0_ = bf16[144,384]{1,0:T(8,128)(2,1)S(1)} collective-permute-done((bf16[144,384]{1,0:T(8,128)(2,1)S(1)}, bf16[144,384]{1,0:T(8,128)(2,1)S(1)}, u32[]{:S(2)}, u32[]{:S(2)}) %collective-permute-start.28) | collective-permute-done | bytes 110624 | tf_op jit(solution)/shard_map/ppermute | solution.py:16
  61.1 1.5 %collective-permute-start.27 = (bf16[144,384]{1,0:T(8,128)(2,1)S(1)}, bf16[144,384]{1,0:T(8,128)(2,1)S(1)}, u32[]{:S(2)}, u32[]{:S(2)}) collective-permute-start(bf16[144,384]{1,0:T(8,128)(2,1)S(1)} %get-tuple-element.75), channel_id=1, source_target_pairs={{0,8},{8,0},{16,24},{24,16},{1,9},{9,1},{17,25},{25,17},{2,10},{10... | collective-permute-start | bytes 331784 | tf_op jit(solution)/shard_map/ppermute | solution.py:16
  63.5 1.7 %collective-permute-done.32 = bf16[160,384]{1,0:T(8,128)(2,1)S(1)} collective-permute-done((bf16[160,384]{1,0:T(8,128)(2,1)S(1)}, bf16[160,384]{1,0:T(8,128)(2,1)S(1)}, u32[]{:S(2)}, u32[]{:S(2)}) %collective-permute-start.32) | collective-permute-done | bytes 122912 | tf_op jit(solution)/shard_map/ppermute | solution.py:16
  67.7 1.6 %shard_map.90 = (f32[27,128,256]{2,1,0:T(8,128)}, f32[8,384]{1,0:T(8,128)}) custom-call(bf16[288,384]{1,0:T(8,128)(2,1)S(1)} %pad_maximum_fusion.refs_0_, bf16[288,384]{1,0:T(8,128)(2,1)S(1)} %collective-permute-done.33.refs_1_, f32[27,128,256]{2,1,0:T(8,128)} %get-tuple-element.84.refs_2_), custom_call_target="tpu_custom_call", output_to_operand_aliasing={{0}: (2, {})} | custom-call | flops 1 | bytes 1 | tf_op jit(solution)/shard_map/pallas_call | solution.py:258
  (87 shorter events, 25.7 us)
Async XLA Ops:
  1.8 6.4 %collective-permute-start.3 = (bf16[512,128]{1,0:T(8,128)(2,1)S(1)}, bf16[512,128]{1,0:T(8,128)(2,1)S(1)}, u32[]{:S(2)}, u32[]{:S(2)}) collective-permute-start(bf16[512,128]{1,0:T(8,128)(2,1)S(1)} %bitcast.22), channel_id=1, source_target_pairs={{0,4},{2,6},{4,0},{6,2},{1,5},{3,7},{5,1},{7,3},{8,12},{10,14},{12... | collective-permute-start | bytes 393224 | tf_op jit(solution)/shard_map/ppermute | solution.py:16
  9.0 5.1 %collective-permute-start.1 = (bf16[512,128]{1,0:T(8,128)(2,1)S(1)}, bf16[512,128]{1,0:T(8,128)(2,1)S(1)}, u32[]{:S(2)}, u32[]{:S(2)}) collective-permute-start(bf16[512,128]{1,0:T(8,128)(2,1)S(1)} %get-tuple-element.46), channel_id=1, source_target_pairs={{0,1},{1,0},{2,3},{3,2},{4,5},{5,4},{6,7},{7,6},{8,9},{9,8},{10,11... | collective-permute-start | bytes 393224 | tf_op jit(solution)/shard_map/ppermute | solution.py:16
  11.7 6.9 %collective-permute-start.5 = (bf16[512,128]{1,0:T(8,128)(2,1)S(1)}, bf16[512,128]{1,0:T(8,128)(2,1)S(1)}, u32[]{:S(2)}, u32[]{:S(2)}) collective-permute-start(bf16[512,128]{1,0:T(8,128)(2,1)S(1)} %get-tuple-element.52), channel_id=1, source_target_pairs={{0,1},{1,0},{2,3},{3,2},{4,5},{5,4},{6,7},{7,6},{8,9},{9,8},{10,11... | collective-permute-start | bytes 393224 | tf_op jit(solution)/shard_map/ppermute | solution.py:16
  14.2 4.7 %collective-permute-start.2 = (bf16[512,128]{1,0:T(8,128)(2,1)S(1)}, bf16[512,128]{1,0:T(8,128)(2,1)S(1)}, u32[]{:S(2)}, u32[]{:S(2)}) collective-permute-start(bf16[512,128]{1,0:T(8,128)(2,1)S(1)} %get-tuple-element.47.refs_4_), channel_id=1, source_target_pairs={{0,1},{1,0},{2,3},{3,2},{4,5},{5,4},{6,7},{7,6},{8,9},{9,8},{10,11... | collective-permute-start | bytes 393224 | tf_op jit(solution)/shard_map/ppermute | solution.py:16
  15.8 9.0 %collective-permute-start.9 = (bf16[512,128]{1,0:T(8,128)(2,1)S(1)}, bf16[512,128]{1,0:T(8,128)(2,1)S(1)}, u32[]{:S(2)}, u32[]{:S(2)}) collective-permute-start(bf16[512,128]{1,0:T(8,128)(2,1)S(1)} %bitcast.24), channel_id=1, source_target_pairs={{0,2},{2,0},{4,6},{6,4},{1,3},{3,1},{5,7},{7,5},{8,10},{10,8},{12,... | collective-permute-start | bytes 393224 | tf_op jit(solution)/shard_map/ppermute | solution.py:16
  17.3 5.1 %collective-permute-start.10 = (bf16[512,128]{1,0:T(8,128)(2,1)S(1)}, bf16[512,128]{1,0:T(8,128)(2,1)S(1)}, u32[]{:S(2)}, u32[]{:S(2)}) collective-permute-start(bf16[512,128]{1,0:T(8,128)(2,1)S(1)} %get-tuple-element.56), channel_id=1, source_target_pairs={{0,4},{2,6},{4,0},{6,2},{1,5},{3,7},{5,1},{7,3},{8,12},{10,14},{12... | collective-permute-start | bytes 393224 | tf_op jit(solution)/shard_map/ppermute | solution.py:16
  18.7 4.9 %collective-permute-start.6 = (bf16[512,128]{1,0:T(8,128)(2,1)S(1)}, bf16[512,128]{1,0:T(8,128)(2,1)S(1)}, u32[]{:S(2)}, u32[]{:S(2)}) collective-permute-start(bf16[512,128]{1,0:T(8,128)(2,1)S(1)} %get-tuple-element.53), channel_id=1, source_target_pairs={{0,1},{1,0},{2,3},{3,2},{4,5},{5,4},{6,7},{7,6},{8,9},{9,8},{10,11... | collective-permute-start | bytes 393224 | tf_op jit(solution)/shard_map/ppermute | solution.py:16
  18.9 6.1 %collective-permute-start.12 = (bf16[512,128]{1,0:T(8,128)(2,1)S(1)}, bf16[512,128]{1,0:T(8,128)(2,1)S(1)}, u32[]{:S(2)}, u32[]{:S(2)}) collective-permute-start(bf16[512,128]{1,0:T(8,128)(2,1)S(1)} %get-tuple-element.88.refs_1_), channel_id=1, source_target_pairs={{0,4},{2,6},{4,0},{6,2},{1,5},{3,7},{5,1},{7,3},{8,12},{10,14},{12... | collective-permute-start | bytes 393224 | tf_op jit(solution)/shard_map/ppermute | solution.py:16
  20.4 6.1 %collective-permute-start.7 = (bf16[512,128]{1,0:T(8,128)(2,1)S(1)}, bf16[512,128]{1,0:T(8,128)(2,1)S(1)}, u32[]{:S(2)}, u32[]{:S(2)}) collective-permute-start(bf16[512,128]{1,0:T(8,128)(2,1)S(1)} %get-tuple-element.89.refs_1_.refs_0_), channel_id=1, source_target_pairs={{0,2},{2,0},{4,6},{6,4},{1,3},{3,1},{5,7},{7,5},{8,10},{10,8},{12,... | collective-permute-start | bytes 393224 | tf_op jit(solution)/shard_map/ppermute | solution.py:16
  24.8 5.1 %collective-permute-start.15 = (bf16[512,128]{1,0:T(8,128)(2,1)S(1)}, bf16[512,128]{1,0:T(8,128)(2,1)S(1)}, u32[]{:S(2)}, u32[]{:S(2)}) collective-permute-start(bf16[512,128]{1,0:T(8,128)(2,1)S(1)} %get-tuple-element.86.refs_3_), channel_id=1, source_target_pairs={{0,4},{2,6},{4,0},{6,2},{1,5},{3,7},{5,1},{7,3},{8,12},{10,14},{12... | collective-permute-start | bytes 393224 | tf_op jit(solution)/shard_map/ppermute | solution.py:16
  32.4 4.7 %collective-permute-start.17 = (bf16[144,384]{1,0:T(8,128)(2,1)S(1)}, bf16[144,384]{1,0:T(8,128)(2,1)S(1)}, u32[]{:S(2)}, u32[]{:S(2)}) collective-permute-start(bf16[144,384]{1,0:T(8,128)(2,1)S(1)} %get-tuple-element.64), channel_id=1, source_target_pairs={{0,8},{8,0},{16,24},{24,16},{1,9},{9,1},{17,25},{25,17},{2,10},{10... | collective-permute-start | bytes 331784 | tf_op jit(solution)/shard_map/ppermute | solution.py:16
  33.7 9.0 %collective-permute-start.8 = (bf16[512,128]{1,0:T(8,128)(2,1)S(1)}, bf16[512,128]{1,0:T(8,128)(2,1)S(1)}, u32[]{:S(2)}, u32[]{:S(2)}) collective-permute-start(bf16[512,128]{1,0:T(8,128)(2,1)S(1)} %get-tuple-element.88.refs_1_), channel_id=1, source_target_pairs={{0,2},{2,0},{4,6},{6,4},{1,3},{3,1},{5,7},{7,5},{8,10},{10,8},{12,... | collective-permute-start | bytes 393224 | tf_op jit(solution)/shard_map/ppermute | solution.py:16
  34.4 11.1 %collective-permute-start.20 = (f32[8,384]{1,0:T(8,128)S(1)}, f32[8,384]{1,0:T(8,128)S(1)}, u32[]{:S(2)}, u32[]{:S(2)}) collective-permute-start(f32[8,384]{1,0:T(8,128)S(1)} %get-tuple-element.71), channel_id=1, source_target_pairs={{0,16},{8,24},{16,0},{24,8},{1,17},{9,25},{17,1},{25,9},{2,18},{10... | collective-permute-start | bytes 36872 | tf_op jit(solution)/shard_map/ppermute | solution.py:16
  36.7 8.8 %collective-permute-start.21 = (bf16[144,384]{1,0:T(8,128)(2,1)S(1)}, bf16[144,384]{1,0:T(8,128)(2,1)S(1)}, u32[]{:S(2)}, u32[]{:S(2)}) collective-permute-start(bf16[144,384]{1,0:T(8,128)(2,1)S(1)} %get-tuple-element.73), channel_id=1, source_target_pairs={{0,8},{8,0},{16,24},{24,16},{1,9},{9,1},{17,25},{25,17},{2,10},{10... | collective-permute-start | bytes 331784 | tf_op jit(solution)/shard_map/ppermute | solution.py:16
  36.9 4.5 %collective-permute-start.18 = (bf16[512,128]{1,0:T(8,128)(2,1)S(1)}, bf16[512,128]{1,0:T(8,128)(2,1)S(1)}, u32[]{:S(2)}, u32[]{:S(2)}) collective-permute-start(bf16[512,128]{1,0:T(8,128)(2,1)S(1)} %get-tuple-element.65), channel_id=1, source_target_pairs={{0,4},{2,6},{4,0},{6,2},{1,5},{3,7},{5,1},{7,3},{8,12},{10,14},{12... | collective-permute-start | bytes 393224 | tf_op jit(solution)/shard_map/ppermute | solution.py:16
  37.2 8.4 %collective-permute-start.22 = (bf16[144,384]{1,0:T(8,128)(2,1)S(1)}, bf16[144,384]{1,0:T(8,128)(2,1)S(1)}, u32[]{:S(2)}, u32[]{:S(2)}) collective-permute-start(bf16[144,384]{1,0:T(8,128)(2,1)S(1)} %add_convert_fusion.refs_9_), channel_id=1, source_target_pairs={{0,16},{8,24},{16,0},{24,8},{1,17},{9,25},{17,1},{25,9},{2,18},{10... | collective-permute-start | bytes 331784 | tf_op jit(solution)/shard_map/ppermute | solution.py:16
  41.4 6.6 %collective-permute-start.19 = (bf16[512,128]{1,0:T(8,128)(2,1)S(1)}, bf16[512,128]{1,0:T(8,128)(2,1)S(1)}, u32[]{:S(2)}, u32[]{:S(2)}) collective-permute-start(bf16[512,128]{1,0:T(8,128)(2,1)S(1)} %collective-permute-done.18.refs_10_), channel_id=1, source_target_pairs={{0,2},{2,0},{4,6},{6,4},{1,3},{3,1},{5,7},{7,5},{8,10},{10,8},{12,... | collective-permute-start | bytes 393224 | tf_op jit(solution)/shard_map/ppermute | solution.py:16
  45.6 7.5 %collective-permute-start.25 = (bf16[144,384]{1,0:T(8,128)(2,1)S(1)}, bf16[144,384]{1,0:T(8,128)(2,1)S(1)}, u32[]{:S(2)}, u32[]{:S(2)}) collective-permute-start(bf16[144,384]{1,0:T(8,128)(2,1)S(1)} %bitcast_select_fusion.2.refs_0_), channel_id=1, source_target_pairs={{0,16},{8,24},{16,0},{24,8},{1,17},{9,25},{17,1},{25,9},{2,18},{10... | collective-permute-start | bytes 331784 | tf_op jit(solution)/shard_map/ppermute | solution.py:16
  45.7 7.4 %collective-permute-start.24 = (bf16[144,384]{1,0:T(8,128)(2,1)S(1)}, bf16[144,384]{1,0:T(8,128)(2,1)S(1)}, u32[]{:S(2)}, u32[]{:S(2)}) collective-permute-start(bf16[144,384]{1,0:T(8,128)(2,1)S(1)} %bitcast_select_fusion.2.refs_0_), channel_id=1, source_target_pairs={{0,8},{8,0},{16,24},{24,16},{1,9},{9,1},{17,25},{25,17},{2,10},{10... | collective-permute-start | bytes 331784 | tf_op jit(solution)/shard_map/ppermute | solution.py:16
  47.7 5.3 %collective-permute-start.23 = (bf16[144,384]{1,0:T(8,128)(2,1)S(1)}, bf16[144,384]{1,0:T(8,128)(2,1)S(1)}, u32[]{:S(2)}, u32[]{:S(2)}) collective-permute-start(bf16[144,384]{1,0:T(8,128)(2,1)S(1)} %bitcast_select_fusion.2.refs_0_), channel_id=1, source_target_pairs={{0,4},{2,6},{4,0},{6,2},{1,5},{3,7},{5,1},{7,3},{8,12},{10,14},{12... | collective-permute-start | bytes 331784 | tf_op jit(solution)/shard_map/ppermute | solution.py:16
  54.7 4.6 %collective-permute-start.28 = (bf16[144,384]{1,0:T(8,128)(2,1)S(1)}, bf16[144,384]{1,0:T(8,128)(2,1)S(1)}, u32[]{:S(2)}, u32[]{:S(2)}) collective-permute-start(bf16[144,384]{1,0:T(8,128)(2,1)S(1)} %get-tuple-element.76), channel_id=1, source_target_pairs={{0,8},{8,0},{16,24},{24,16},{1,9},{9,1},{17,25},{25,17},{2,10},{10... | collective-permute-start | bytes 331784 | tf_op jit(solution)/shard_map/ppermute | solution.py:16
  54.7 4.6 %collective-permute-start.29 = (bf16[144,384]{1,0:T(8,128)(2,1)S(1)}, bf16[144,384]{1,0:T(8,128)(2,1)S(1)}, u32[]{:S(2)}, u32[]{:S(2)}) collective-permute-start(bf16[144,384]{1,0:T(8,128)(2,1)S(1)} %get-tuple-element.77), channel_id=1, source_target_pairs={{0,4},{2,6},{4,0},{6,2},{1,5},{3,7},{5,1},{7,3},{8,12},{10,14},{12... | collective-permute-start | bytes 331784 | tf_op jit(solution)/shard_map/ppermute | solution.py:16
  60.3 4.9 %collective-permute-start.32 = (bf16[160,384]{1,0:T(8,128)(2,1)S(1)}, bf16[160,384]{1,0:T(8,128)(2,1)S(1)}, u32[]{:S(2)}, u32[]{:S(2)}) collective-permute-start(bf16[160,384]{1,0:T(8,128)(2,1)S(1)} %get-tuple-element.83), channel_id=1, source_target_pairs={{0,4},{2,6},{4,0},{6,2},{1,5},{3,7},{5,1},{7,3},{8,12},{10,14},{12... | collective-permute-start | bytes 368648 | tf_op jit(solution)/shard_map/ppermute | solution.py:16
  61.1 4.3 %collective-permute-start.27 = (bf16[144,384]{1,0:T(8,128)(2,1)S(1)}, bf16[144,384]{1,0:T(8,128)(2,1)S(1)}, u32[]{:S(2)}, u32[]{:S(2)}) collective-permute-start(bf16[144,384]{1,0:T(8,128)(2,1)S(1)} %get-tuple-element.75), channel_id=1, source_target_pairs={{0,8},{8,0},{16,24},{24,16},{1,9},{9,1},{17,25},{25,17},{2,10},{10... | collective-permute-start | bytes 331784 | tf_op jit(solution)/shard_map/ppermute | solution.py:16
  (14 other events, 48.4 us)

commit v6 on v5

--- a/solution.py
+++ b/solution.py
@@ -216,36 +216,34 @@
     four_c[0], four_c[1], four_c[2], four_c[3] = q[...], q1[...], q2[...], x0[...]
 
 
-def next_round_body(pos, q3, x2, total, last_x, two_c):
+def next_round_body(pos, core, q3, x2, total, last_x, two_c):
+    del core
     rows = q3.shape[0]
     last_x[0:rows, :] = q3[...]
     last_x[rows : rows + 16, :] = split_rows(total[:, : total.shape[1] // 3])
     two_c[0], two_c[1] = q3[...], x2[...]
 
 
-def both_cores(kinds, own, core):
-    pieces = [(who, j, own.at[n]) for n, (who, j) in enumerate(kinds)]
-    return pieces + [(who + 2, j, core.at[n]) for n, (who, j) in enumerate(kinds)]
-
-
-def first_spread_body(pos, own, core, out, done, wide, sems):
-    place(pos, both_cores(((0, 0), (0, 1), (0, 2), (1, 0)), own, core), out, wide, sems)
+FIRST, NEXT, LAST = ((0, 0), (0, 1), (0, 2), (1, 0)), ((0, 3), (1, 2)), ((1, 1), (1, 3))
+
+
+def stacked(kinds, own, core):
+    pieces = [(who, j, own.at[n]) for n, (who, j) in enumerate(kinds)] if own is not None else []
+    return pieces + ([(who + 2, j, core.at[n]) for n, (who, j) in enumerate(kinds)] if core is not None else [])
+
+
+def first_spread_body(pos, own, core, own_b, out, done, wide, sems):
+    place(pos, stacked(FIRST, own, core) + stacked(NEXT, own_b, None), out, wide, sems)
     done[...] = jnp.zeros_like(done)
 
 
-def next_spread_body(pos, own, core, before, out, done, wide, sems):
-    place(pos, both_cores(((0, 3), (1, 2)), own, core), out, wide, sems)
-    done[...] = jnp.zeros_like(done)
-
-
-def last_spread_body(pos, own, core, before, out, done, wide, sems):
+def last_spread_body(pos, own, core, core_b, before, out, wide, sems):
     rows = own.shape[0] // 2
     pieces = []
-    for n, (who, j) in enumerate(((1, 1), (1, 3))):
+    for n, (who, j) in enumerate(LAST):
         pieces.append((who, j, own.at[n * rows : (n + 1) * rows]))
         pieces.append((who + 2, j, core.at[n * rows : (n + 1) * rows]))
-    place(pos, pieces, out, wide, sems)
-    done[...] = jnp.zeros_like(done)
+    place(pos, pieces + stacked(NEXT, None, core_b), out, wide, sems)
 
 
 def spread(body, shape, small, *arrays, alias=False):
@@ -257,10 +255,10 @@
 
     return pl.pallas_call(
         inner,
-        out_shape=[jax.ShapeDtypeStruct(shape, F32), jax.ShapeDtypeStruct(*small)],
+        out_shape=[jax.ShapeDtypeStruct(shape, F32)] + [jax.ShapeDtypeStruct(*one) for one in small],
         in_specs=[whole] * (len(arrays) - alias) + [anywhere] * alias,
-        out_specs=[anywhere, whole],
-        scratch_shapes=[pltpu.VMEM((8, shape[0], 16, shape[2] // 2), F32), pltpu.SemaphoreType.DMA((8,))],
+        out_specs=[anywhere] + [whole] * len(small),
+        scratch_shapes=[pltpu.VMEM((10, shape[0], 16, shape[2] // 2), F32), pltpu.SemaphoreType.DMA((10,))],
         input_output_aliases={len(arrays) - 1: 0} if alias else {},
         compiler_params=pltpu.CompilerParams(vmem_limit_bytes=20 * MIB),
         cost_estimate=pl.CostEstimate(flops=1, bytes_accessed=1, transcendentals=0),
@@ -443,7 +441,7 @@
     q1, q2, x0 = swap(quarter, "dp", 1), swap(quarter, "dp", 2), swap(quarter, "slab", 2)
     total_b = total_a + total_z1
     out_shape = (27, local_in, outputs)
-    token = (8, lanes), F32
+    token = (((8, lanes), F32),)
     one_z, one_x, x0_z, four_c = vmem_call(
         round_body,
         [(quarter.shape, BF)] * 3 + [((4,) + quarter.shape, BF)],
@@ -453,21 +451,19 @@
         after=(total_z1, ig_done),
     )
     q3, x2, x1, core = swap(one_z, "dp", 1), swap(one_x, "slab", 2), swap(x0_z, "dp", 1), swap(four_c, "slab", 1)
-    out, done = spread(first_spread_body, out_shape, token, four_c, core)
     last_x, two_c = vmem_call(
         next_round_body,
         [((rows + 16, lanes), BF), ((2,) + quarter.shape, BF)],
         [],
         0,
-        q3, x2, total_b,
-        after=(done,),
+        core, q3, x2, total_b,
     )
     x3, core_b = swap(last_x, "slab", 2), swap(two_c, "slab", 1)
-    out, done = spread(next_spread_body, out_shape, token, two_c, core_b, out, alias=True)
+    out, done = spread(first_spread_body, out_shape, token, four_c, core, two_c)
     x3 = held_back(x3, done)
     pair_x = jnp.concatenate([x1, x3[:rows]], axis=0)
     core_x = swap(pair_x, "slab", 1)
-    weight_grad, _ = spread(last_spread_body, out_shape, token, pair_x, core_x, out, alias=True)
+    weight_grad = spread(last_spread_body, out_shape, (), pair_x, core_x, core_b, out, alias=True)[0]
     tail = x3[rows : rows + 1].astype(F32).reshape(3, local_out)
     bias_grad = jnp.where(x == y, total_b[0, :local_out], tail[0] + tail[1] + tail[2]) * factor
     shape = (samples, planes, nx, ny)

time: 69.8 us -> 68.5 us (0.981)
  waiting for transfers between devices: 14.3 us -> 12.3 us
  starting transfers between devices: 35.6 us -> 37.5 us
  Pallas kernels: 15.3 us -> 14.1 us
    ppermute x34, waiting for transfers between devices: 14.3 us -> 12.3 us  [swap(): lax.ppermute(value, axis, [(i, i ^ bit) for i in range(lax.axis_size(axis...]
    ppermute x34, starting transfers between devices: 35.6 us -> 37.5 us  [swap(): lax.ppermute(value, axis, [(i, i ^ bit) for i in range(lax.axis_size(axis...]
    pallas_call x3 -> x2, Pallas kernels: 3.86 us -> 2.59 us  [spread(): pl.pallas_call(inner, out_shape=[jax.ShapeDtypeStruct(shape, F32)] + [jax...]
  transfers between devices with their start and end apart: 34 -> 34, of which waited for: 14 -> 11; matrix products, arithmetic and copies ran while one was open for 1% -> 1% of each run, Pallas kernels for 19% -> 18%
where the time goes in v6:
time: 68.5 us; the launch traced here: 68.1 us
  starting transfers between devices  37.5 us (55%)
  Pallas kernels  14.1 us (21%)
  waiting for transfers between devices  12.3 us (18%)
  other arithmetic  1.76 us (3%)
  local copies, waits for them, and re-layouts  1.54 us (2%)
  between operations  0.89 us (1%)
    ppermute x34, starting transfers between devices, swap(): lax.ppermute(value, axis, [(i, i ^ bit) for i in range(lax.axis_size(axis...  37.5 us
    ppermute x34, waiting for transfers between devices, swap(): lax.ppermute(value, axis, [(i, i ^ bit) for i in range(lax.axis_size(axis...  12.3 us
    pallas_call x13, Pallas kernels, vmem_call(): pl.pallas_call(inner, out_shape=shapes, in_specs=[pl.BlockSpec(memory_spa...  11.5 us
    pallas_call x2, Pallas kernels, spread(): pl.pallas_call(inner, out_shape=[jax.ShapeDtypeStruct(shape, F32)] + [jax...  2.59 us
    unnamed x8, local copies, waits for them, and re-layouts  1.49 us
  transfers between devices with their start and end apart: 34, of which 11 were waited for; matrix products, arithmetic and copies ran while one was open for 1% of the time, Pallas kernels for 18%

profile of v6, /device:TPU:1, one launch (start us, length us, event | category | flops | bytes accessed | tf_op | source)
XLA Modules:
  0.0 68.1 jit_solution(6756236588971523648)
XLA Ops:
  1.8 2.7 %collective-permute-start.3 = (bf16[512,128]{1,0:T(8,128)(2,1)S(1)}, bf16[512,128]{1,0:T(8,128)(2,1)S(1)}, u32[]{:S(2)}, u32[]{:S(2)}) collective-permute-start(bf16[512,128]{1,0:T(8,128)(2,1)S(1)} %bitcast.22), channel_id=1, source_target_pairs={{0,4},{2,6},{4,0},{6,2},{1,5},{3,7},{5,1},{7,3},{8,12},{10,14},{12... | collective-permute-start | bytes 393224 | tf_op jit(solution)/shard_map/ppermute | solution.py:16
  4.4 1.5 %copy-done = bf16[3,3,3,128,256]{4,3,2,1,0:T(8,128)(2,1)S(1)} copy-done((bf16[3,3,3,128,256]{4,3,2,1,0:T(8,128)(2,1)S(1)}, bf16[3,3,3,128,256]{4,3,2,1,0:T(8,128)(2,1)}, u32[]{:S(2)}) %copy-start) | copy-done | bytes 1769496
  5.9 1.5 %shard_map.75 = (f32[512,128]{1,0:T(8,128)S(1)}, bf16[512,128]{1,0:T(8,128)(2,1)S(1)}, bf16[2,544,384]{2,1,0:T(8,128)(2,1)S(1)}, bf16[3,1152,256]{2,1,0:T(8,128)(2,1)S(1)}, f32[8,128]{1,0:T(8,128)S(1)}) custom-call(bf16[512,128]{1,0:T(8,128)(2,1)S(1)} %bitcast.27, bf16[512,128]{1,0:T(8,128)(2,1)S(1)} %bitcast.23, ...), custom_call_target="tpu_custom_call" | custom-call | flops 2811939328 | bytes 1048576 | tf_op jit(solution)/shard_map/pallas_call | solution.py:33
  9.0 1.5 %collective-permute-start.1 = (bf16[512,128]{1,0:T(8,128)(2,1)S(1)}, bf16[512,128]{1,0:T(8,128)(2,1)S(1)}, u32[]{:S(2)}, u32[]{:S(2)}) collective-permute-start(bf16[512,128]{1,0:T(8,128)(2,1)S(1)} %get-tuple-element.43), channel_id=1, source_target_pairs={{0,1},{1,0},{2,3},{3,2},{4,5},{5,4},{6,7},{7,6},{8,9},{9,8},{10,11... | collective-permute-start | bytes 393224 | tf_op jit(solution)/shard_map/ppermute | solution.py:16
  12.7 1.4 %collective-permute-done.1.refs_1_ = bf16[512,128]{1,0:T(8,128)(2,1)S(1)} collective-permute-done((bf16[512,128]{1,0:T(8,128)(2,1)S(1)}, bf16[512,128]{1,0:T(8,128)(2,1)S(1)}, u32[]{:S(2)}, u32[]{:S(2)}) %collective-permute-start.1) | collective-permute-done | bytes 131104 | tf_op jit(solution)/shard_map/ppermute | solution.py:16
  14.2 1.5 %collective-permute-start.2 = (bf16[512,128]{1,0:T(8,128)(2,1)S(1)}, bf16[512,128]{1,0:T(8,128)(2,1)S(1)}, u32[]{:S(2)}, u32[]{:S(2)}) collective-permute-start(bf16[512,128]{1,0:T(8,128)(2,1)S(1)} %get-tuple-element.44.refs_4_), channel_id=1, source_target_pairs={{0,1},{1,0},{2,3},{3,2},{4,5},{5,4},{6,7},{7,6},{8,9},{9,8},{10,11... | collective-permute-start | bytes 393224 | tf_op jit(solution)/shard_map/ppermute | solution.py:16
  15.8 1.6 %collective-permute-start.9 = (bf16[512,128]{1,0:T(8,128)(2,1)S(1)}, bf16[512,128]{1,0:T(8,128)(2,1)S(1)}, u32[]{:S(2)}, u32[]{:S(2)}) collective-permute-start(bf16[512,128]{1,0:T(8,128)(2,1)S(1)} %bitcast.24), channel_id=1, source_target_pairs={{0,2},{2,0},{4,6},{6,4},{1,3},{3,1},{5,7},{7,5},{8,10},{10,8},{12,... | collective-permute-start | bytes 393224 | tf_op jit(solution)/shard_map/ppermute | solution.py:16
  18.9 1.5 %collective-permute-start.12 = (bf16[512,128]{1,0:T(8,128)(2,1)S(1)}, bf16[512,128]{1,0:T(8,128)(2,1)S(1)}, u32[]{:S(2)}, u32[]{:S(2)}) collective-permute-start(bf16[512,128]{1,0:T(8,128)(2,1)S(1)} %get-tuple-element.82.refs_1_), channel_id=1, source_target_pairs={{0,4},{2,6},{4,0},{6,2},{1,5},{3,7},{5,1},{7,3},{8,12},{10,14},{12... | collective-permute-start | bytes 393224 | tf_op jit(solution)/shard_map/ppermute | solution.py:16
  20.4 2.0 %collective-permute-start.7 = (bf16[512,128]{1,0:T(8,128)(2,1)S(1)}, bf16[512,128]{1,0:T(8,128)(2,1)S(1)}, u32[]{:S(2)}, u32[]{:S(2)}) collective-permute-start(bf16[512,128]{1,0:T(8,128)(2,1)S(1)} %get-tuple-element.83.refs_1_.refs_0_), channel_id=1, source_target_pairs={{0,2},{2,0},{4,6},{6,4},{1,3},{3,1},{5,7},{7,5},{8,10},{10,8},{12,... | collective-permute-start | bytes 393224 | tf_op jit(solution)/shard_map/ppermute | solution.py:16
  26.5 1.6 %shard_map.80 = (f32[3,192,384]{2,1,0:T(8,128)S(1)}, f32[8,384]{1,0:T(8,128)S(1)}) custom-call(bf16[12,192,512]{2,1,0:T(8,128)(2,1)S(1)} %shard_map.79.refs_0_, bf16[512,128]{1,0:T(8,128)(2,1)S(1)} %get-tuple-element.83.refs_1_.refs_0_, bf16[512,128]{1,0:T(8,128)(2,1)S(1)} %collective-permute-done.7.refs_2_.refs_4_, ...), custom_call_target="tpu_custom_call" | custom-call | flops 4623878656 | bytes 1048576 | tf_op jit(solution)/shard_map/pallas_call | solution.py:33
  34.4 2.3 %collective-permute-start.20 = (f32[8,384]{1,0:T(8,128)S(1)}, f32[8,384]{1,0:T(8,128)S(1)}, u32[]{:S(2)}, u32[]{:S(2)}) collective-permute-start(f32[8,384]{1,0:T(8,128)S(1)} %get-tuple-element.68), channel_id=1, source_target_pairs={{0,16},{8,24},{16,0},{24,8},{1,17},{9,25},{17,1},{25,9},{2,18},{10... | collective-permute-start | bytes 36872 | tf_op jit(solution)/shard_map/ppermute | solution.py:16
  37.2 2.0 %collective-permute-start.22 = (bf16[144,384]{1,0:T(8,128)(2,1)S(1)}, bf16[144,384]{1,0:T(8,128)(2,1)S(1)}, u32[]{:S(2)}, u32[]{:S(2)}) collective-permute-start(bf16[144,384]{1,0:T(8,128)(2,1)S(1)} %add_convert_fusion.refs_9_), channel_id=1, source_target_pairs={{0,16},{8,24},{16,0},{24,8},{1,17},{9,25},{17,1},{25,9},{2,18},{10... | collective-permute-start | bytes 331784 | tf_op jit(solution)/shard_map/ppermute | solution.py:16
  39.1 2.2 %collective-permute-done.18.refs_10_ = bf16[512,128]{1,0:T(8,128)(2,1)S(1)} collective-permute-done((bf16[512,128]{1,0:T(8,128)(2,1)S(1)}, bf16[512,128]{1,0:T(8,128)(2,1)S(1)}, u32[]{:S(2)}, u32[]{:S(2)}) %collective-permute-start.18) | collective-permute-done | bytes 131104 | tf_op jit(solution)/shard_map/ppermute | solution.py:16
  41.4 1.4 %collective-permute-start.19 = (bf16[512,128]{1,0:T(8,128)(2,1)S(1)}, bf16[512,128]{1,0:T(8,128)(2,1)S(1)}, u32[]{:S(2)}, u32[]{:S(2)}) collective-permute-start(bf16[512,128]{1,0:T(8,128)(2,1)S(1)} %collective-permute-done.18.refs_10_), channel_id=1, source_target_pairs={{0,2},{2,0},{4,6},{6,4},{1,3},{3,1},{5,7},{7,5},{8,10},{10,8},{12,... | collective-permute-start | bytes 393224 | tf_op jit(solution)/shard_map/ppermute | solution.py:16
  42.8 2.7 %shard_map.84 = (bf16[512,128]{1,0:T(8,128)(2,1)S(1)}, f32[512,128]{1,0:T(8,128)S(1)}, bf16[2,512,128]{2,1,0:T(8,128)(2,1)}, f32[8,384]{1,0:T(8,128)S(1)}) custom-call(bf16[512,128]{1,0:T(8,128)(2,1)S(1)} %get-tuple-element.83.refs_1_.refs_0_, bf16[512,128]{1,0:T(8,128)(2,1)S(1)} %get-tuple-element.82.refs_1_, ...), custom_call_target="tpu_custom_call" | custom-call | flops 4623878656 | bytes 1048576 | tf_op jit(solution)/shard_map/pallas_call | solution.py:33
  45.7 2.0 %collective-permute-start.24 = (bf16[144,384]{1,0:T(8,128)(2,1)S(1)}, bf16[144,384]{1,0:T(8,128)(2,1)S(1)}, u32[]{:S(2)}, u32[]{:S(2)}) collective-permute-start(bf16[144,384]{1,0:T(8,128)(2,1)S(1)} %bitcast_select_fusion.2.refs_0_), channel_id=1, source_target_pairs={{0,8},{8,0},{16,24},{24,16},{1,9},{9,1},{17,25},{25,17},{2,10},{10... | collective-permute-start | bytes 331784 | tf_op jit(solution)/shard_map/ppermute | solution.py:16
  48.0 1.6 %shard_map.85 = (bf16[2,512,128]{2,1,0:T(8,128)(2,1)}, f32[8,384]{1,0:T(8,128)S(1)}) custom-call(bf16[512,128]{1,0:T(8,128)(2,1)S(1)} %collective-permute-done.16.refs_1_.refs_0_, bf16[512,128]{1,0:T(8,128)(2,1)S(1)} %collective-permute-done.19.refs_1_, bf16[27,128,256]{2,1,0:T(8,128)(2,1)S(1)} %bitcast.32, f32[512,128]{1,0:T(8,128)S(1)} %get-tuple-element.64.refs_3_, ...), custom_call_target="tpu_custom_call" | custom-call | flops 1000000000 | bytes 1048576 | tf_op jit(solution)/shard_map/pallas_call | solution.py:33
  49.6 2.1 %collective-permute-done.26.refs_4_ = f32[8,384]{1,0:T(8,128)S(1)} collective-permute-done((f32[8,384]{1,0:T(8,128)S(1)}, f32[8,384]{1,0:T(8,128)S(1)}, u32[]{:S(2)}, u32[]{:S(2)}) %collective-permute-start.26) | collective-permute-done | bytes 12320 | tf_op jit(solution)/shard_map/ppermute | solution.py:16
  53.1 1.6 %collective-permute-start.28 = (bf16[4,144,384]{2,1,0:T(8,128)(2,1)S(1)}, bf16[4,144,384]{2,1,0:T(8,128)(2,1)S(1)}, u32[]{:S(2)}, u32[]{:S(2)}) collective-permute-start(bf16[4,144,384]{2,1,0:T(8,128)(2,1)S(1)} %get-tuple-element.73.refs_0_), channel_id=1, source_target_pairs={{0,2},{2,0},{4,6},{6,4},{1,3},{3,1},{5,7},{7,5},{8,10},{10,8},{12,... | collective-permute-start | bytes 1327112 | tf_op jit(solution)/shard_map/ppermute | solution.py:16
  55.5 1.5 %collective-permute-start.27 = (bf16[144,384]{1,0:T(8,128)(2,1)S(1)}, bf16[144,384]{1,0:T(8,128)(2,1)S(1)}, u32[]{:S(2)}, u32[]{:S(2)}) collective-permute-start(bf16[144,384]{1,0:T(8,128)(2,1)S(1)} %get-tuple-element.72), channel_id=1, source_target_pairs={{0,8},{8,0},{16,24},{24,16},{1,9},{9,1},{17,25},{25,17},{2,10},{10... | collective-permute-start | bytes 331784 | tf_op jit(solution)/shard_map/ppermute | solution.py:16
  56.9 2.4 %collective-permute-done.29.refs_1_ = bf16[144,384]{1,0:T(8,128)(2,1)S(1)} collective-permute-done((bf16[144,384]{1,0:T(8,128)(2,1)S(1)}, bf16[144,384]{1,0:T(8,128)(2,1)S(1)}, u32[]{:S(2)}, u32[]{:S(2)}) %collective-permute-start.29) | collective-permute-done | bytes 110624 | tf_op jit(solution)/shard_map/ppermute | solution.py:16
  60.2 1.6 %collective-permute-start.33 = (bf16[2,144,384]{2,1,0:T(8,128)(2,1)S(1)}, bf16[2,144,384]{2,1,0:T(8,128)(2,1)S(1)}, u32[]{:S(2)}, u32[]{:S(2)}) collective-permute-start(bf16[2,144,384]{2,1,0:T(8,128)(2,1)S(1)} %get-tuple-element.76.refs_2_), channel_id=1, source_target_pairs={{0,2},{2,0},{4,6},{6,4},{1,3},{3,1},{5,7},{7,5},{8,10},{10,8},{12,... | collective-permute-start | bytes 663560 | tf_op jit(solution)/shard_map/ppermute | solution.py:16
  61.8 1.4 %shard_map.88 = (f32[27,128,256]{2,1,0:T(8,128)}, f32[8,384]{1,0:T(8,128)S(1)}) custom-call(bf16[4,144,384]{2,1,0:T(8,128)(2,1)S(1)} %get-tuple-element.73.refs_0_, bf16[4,144,384]{2,1,0:T(8,128)(2,1)S(1)} %collective-permute-done.28.refs_0_.refs_1_, bf16[2,144,384]{2,1,0:T(8,128)(2,1)S(1)} %get-tuple-element.76.refs_2_), custom_call_target="tpu_custom_call" | custom-call | flops 1 | bytes 1 | tf_op jit(solution)/shard_map/pallas_call | solution.py:256
  63.4 2.4 %collective-permute-start.32 = (bf16[288,384]{1,0:T(8,128)(2,1)S(1)}, bf16[288,384]{1,0:T(8,128)(2,1)S(1)}, u32[]{:S(2)}, u32[]{:S(2)}) collective-permute-start(bf16[288,384]{1,0:T(8,128)(2,1)S(1)} %pad_maximum_fusion.refs_0_), channel_id=1, source_target_pairs={{0,2},{2,0},{4,6},{6,4},{1,3},{3,1},{5,7},{7,5},{8,10},{10,8},{12,... | collective-permute-start | bytes 663560 | tf_op jit(solution)/shard_map/ppermute | solution.py:16
  (86 shorter events, 23.1 us)
Async XLA Ops:
  1.8 6.4 %collective-permute-start.3 = (bf16[512,128]{1,0:T(8,128)(2,1)S(1)}, bf16[512,128]{1,0:T(8,128)(2,1)S(1)}, u32[]{:S(2)}, u32[]{:S(2)}) collective-permute-start(bf16[512,128]{1,0:T(8,128)(2,1)S(1)} %bitcast.22), channel_id=1, source_target_pairs={{0,4},{2,6},{4,0},{6,2},{1,5},{3,7},{5,1},{7,3},{8,12},{10,14},{12... | collective-permute-start | bytes 393224 | tf_op jit(solution)/shard_map/ppermute | solution.py:16
  9.0 5.1 %collective-permute-start.1 = (bf16[512,128]{1,0:T(8,128)(2,1)S(1)}, bf16[512,128]{1,0:T(8,128)(2,1)S(1)}, u32[]{:S(2)}, u32[]{:S(2)}) collective-permute-start(bf16[512,128]{1,0:T(8,128)(2,1)S(1)} %get-tuple-element.43), channel_id=1, source_target_pairs={{0,1},{1,0},{2,3},{3,2},{4,5},{5,4},{6,7},{7,6},{8,9},{9,8},{10,11... | collective-permute-start | bytes 393224 | tf_op jit(solution)/shard_map/ppermute | solution.py:16
  11.7 6.9 %collective-permute-start.5 = (bf16[512,128]{1,0:T(8,128)(2,1)S(1)}, bf16[512,128]{1,0:T(8,128)(2,1)S(1)}, u32[]{:S(2)}, u32[]{:S(2)}) collective-permute-start(bf16[512,128]{1,0:T(8,128)(2,1)S(1)} %get-tuple-element.49), channel_id=1, source_target_pairs={{0,1},{1,0},{2,3},{3,2},{4,5},{5,4},{6,7},{7,6},{8,9},{9,8},{10,11... | collective-permute-start | bytes 393224 | tf_op jit(solution)/shard_map/ppermute | solution.py:16
  14.2 4.7 %collective-permute-start.2 = (bf16[512,128]{1,0:T(8,128)(2,1)S(1)}, bf16[512,128]{1,0:T(8,128)(2,1)S(1)}, u32[]{:S(2)}, u32[]{:S(2)}) collective-permute-start(bf16[512,128]{1,0:T(8,128)(2,1)S(1)} %get-tuple-element.44.refs_4_), channel_id=1, source_target_pairs={{0,1},{1,0},{2,3},{3,2},{4,5},{5,4},{6,7},{7,6},{8,9},{9,8},{10,11... | collective-permute-start | bytes 393224 | tf_op jit(solution)/shard_map/ppermute | solution.py:16
  15.8 9.0 %collective-permute-start.9 = (bf16[512,128]{1,0:T(8,128)(2,1)S(1)}, bf16[512,128]{1,0:T(8,128)(2,1)S(1)}, u32[]{:S(2)}, u32[]{:S(2)}) collective-permute-start(bf16[512,128]{1,0:T(8,128)(2,1)S(1)} %bitcast.24), channel_id=1, source_target_pairs={{0,2},{2,0},{4,6},{6,4},{1,3},{3,1},{5,7},{7,5},{8,10},{10,8},{12,... | collective-permute-start | bytes 393224 | tf_op jit(solution)/shard_map/ppermute | solution.py:16
  17.3 5.1 %collective-permute-start.10 = (bf16[512,128]{1,0:T(8,128)(2,1)S(1)}, bf16[512,128]{1,0:T(8,128)(2,1)S(1)}, u32[]{:S(2)}, u32[]{:S(2)}) collective-permute-start(bf16[512,128]{1,0:T(8,128)(2,1)S(1)} %get-tuple-element.53), channel_id=1, source_target_pairs={{0,4},{2,6},{4,0},{6,2},{1,5},{3,7},{5,1},{7,3},{8,12},{10,14},{12... | collective-permute-start | bytes 393224 | tf_op jit(solution)/shard_map/ppermute | solution.py:16
  18.7 4.9 %collective-permute-start.6 = (bf16[512,128]{1,0:T(8,128)(2,1)S(1)}, bf16[512,128]{1,0:T(8,128)(2,1)S(1)}, u32[]{:S(2)}, u32[]{:S(2)}) collective-permute-start(bf16[512,128]{1,0:T(8,128)(2,1)S(1)} %get-tuple-element.50), channel_id=1, source_target_pairs={{0,1},{1,0},{2,3},{3,2},{4,5},{5,4},{6,7},{7,6},{8,9},{9,8},{10,11... | collective-permute-start | bytes 393224 | tf_op jit(solution)/shard_map/ppermute | solution.py:16
  18.9 6.1 %collective-permute-start.12 = (bf16[512,128]{1,0:T(8,128)(2,1)S(1)}, bf16[512,128]{1,0:T(8,128)(2,1)S(1)}, u32[]{:S(2)}, u32[]{:S(2)}) collective-permute-start(bf16[512,128]{1,0:T(8,128)(2,1)S(1)} %get-tuple-element.82.refs_1_), channel_id=1, source_target_pairs={{0,4},{2,6},{4,0},{6,2},{1,5},{3,7},{5,1},{7,3},{8,12},{10,14},{12... | collective-permute-start | bytes 393224 | tf_op jit(solution)/shard_map/ppermute | solution.py:16
  20.4 6.1 %collective-permute-start.7 = (bf16[512,128]{1,0:T(8,128)(2,1)S(1)}, bf16[512,128]{1,0:T(8,128)(2,1)S(1)}, u32[]{:S(2)}, u32[]{:S(2)}) collective-permute-start(bf16[512,128]{1,0:T(8,128)(2,1)S(1)} %get-tuple-element.83.refs_1_.refs_0_), channel_id=1, source_target_pairs={{0,2},{2,0},{4,6},{6,4},{1,3},{3,1},{5,7},{7,5},{8,10},{10,8},{12,... | collective-permute-start | bytes 393224 | tf_op jit(solution)/shard_map/ppermute | solution.py:16
  24.8 5.1 %collective-permute-start.15 = (bf16[512,128]{1,0:T(8,128)(2,1)S(1)}, bf16[512,128]{1,0:T(8,128)(2,1)S(1)}, u32[]{:S(2)}, u32[]{:S(2)}) collective-permute-start(bf16[512,128]{1,0:T(8,128)(2,1)S(1)} %get-tuple-element.80.refs_3_), channel_id=1, source_target_pairs={{0,4},{2,6},{4,0},{6,2},{1,5},{3,7},{5,1},{7,3},{8,12},{10,14},{12... | collective-permute-start | bytes 393224 | tf_op jit(solution)/shard_map/ppermute | solution.py:16
  32.4 4.7 %collective-permute-start.17 = (bf16[144,384]{1,0:T(8,128)(2,1)S(1)}, bf16[144,384]{1,0:T(8,128)(2,1)S(1)}, u32[]{:S(2)}, u32[]{:S(2)}) collective-permute-start(bf16[144,384]{1,0:T(8,128)(2,1)S(1)} %get-tuple-element.61), channel_id=1, source_target_pairs={{0,8},{8,0},{16,24},{24,16},{1,9},{9,1},{17,25},{25,17},{2,10},{10... | collective-permute-start | bytes 331784 | tf_op jit(solution)/shard_map/ppermute | solution.py:16
  33.7 9.0 %collective-permute-start.8 = (bf16[512,128]{1,0:T(8,128)(2,1)S(1)}, bf16[512,128]{1,0:T(8,128)(2,1)S(1)}, u32[]{:S(2)}, u32[]{:S(2)}) collective-permute-start(bf16[512,128]{1,0:T(8,128)(2,1)S(1)} %get-tuple-element.82.refs_1_), channel_id=1, source_target_pairs={{0,2},{2,0},{4,6},{6,4},{1,3},{3,1},{5,7},{7,5},{8,10},{10,8},{12,... | collective-permute-start | bytes 393224 | tf_op jit(solution)/shard_map/ppermute | solution.py:16
  34.4 11.1 %collective-permute-start.20 = (f32[8,384]{1,0:T(8,128)S(1)}, f32[8,384]{1,0:T(8,128)S(1)}, u32[]{:S(2)}, u32[]{:S(2)}) collective-permute-start(f32[8,384]{1,0:T(8,128)S(1)} %get-tuple-element.68), channel_id=1, source_target_pairs={{0,16},{8,24},{16,0},{24,8},{1,17},{9,25},{17,1},{25,9},{2,18},{10... | collective-permute-start | bytes 36872 | tf_op jit(solution)/shard_map/ppermute | solution.py:16
  36.7 8.8 %collective-permute-start.21 = (bf16[144,384]{1,0:T(8,128)(2,1)S(1)}, bf16[144,384]{1,0:T(8,128)(2,1)S(1)}, u32[]{:S(2)}, u32[]{:S(2)}) collective-permute-start(bf16[144,384]{1,0:T(8,128)(2,1)S(1)} %get-tuple-element.70), channel_id=1, source_target_pairs={{0,8},{8,0},{16,24},{24,16},{1,9},{9,1},{17,25},{25,17},{2,10},{10... | collective-permute-start | bytes 331784 | tf_op jit(solution)/shard_map/ppermute | solution.py:16
  37.2 8.4 %collective-permute-start.22 = (bf16[144,384]{1,0:T(8,128)(2,1)S(1)}, bf16[144,384]{1,0:T(8,128)(2,1)S(1)}, u32[]{:S(2)}, u32[]{:S(2)}) collective-permute-start(bf16[144,384]{1,0:T(8,128)(2,1)S(1)} %add_convert_fusion.refs_9_), channel_id=1, source_target_pairs={{0,16},{8,24},{16,0},{24,8},{1,17},{9,25},{17,1},{25,9},{2,18},{10... | collective-permute-start | bytes 331784 | tf_op jit(solution)/shard_map/ppermute | solution.py:16
  41.4 6.6 %collective-permute-start.19 = (bf16[512,128]{1,0:T(8,128)(2,1)S(1)}, bf16[512,128]{1,0:T(8,128)(2,1)S(1)}, u32[]{:S(2)}, u32[]{:S(2)}) collective-permute-start(bf16[512,128]{1,0:T(8,128)(2,1)S(1)} %collective-permute-done.18.refs_10_), channel_id=1, source_target_pairs={{0,2},{2,0},{4,6},{6,4},{1,3},{3,1},{5,7},{7,5},{8,10},{10,8},{12,... | collective-permute-start | bytes 393224 | tf_op jit(solution)/shard_map/ppermute | solution.py:16
  45.6 7.5 %collective-permute-start.25 = (bf16[144,384]{1,0:T(8,128)(2,1)S(1)}, bf16[144,384]{1,0:T(8,128)(2,1)S(1)}, u32[]{:S(2)}, u32[]{:S(2)}) collective-permute-start(bf16[144,384]{1,0:T(8,128)(2,1)S(1)} %bitcast_select_fusion.2.refs_0_), channel_id=1, source_target_pairs={{0,16},{8,24},{16,0},{24,8},{1,17},{9,25},{17,1},{25,9},{2,18},{10... | collective-permute-start | bytes 331784 | tf_op jit(solution)/shard_map/ppermute | solution.py:16
  45.7 7.4 %collective-permute-start.24 = (bf16[144,384]{1,0:T(8,128)(2,1)S(1)}, bf16[144,384]{1,0:T(8,128)(2,1)S(1)}, u32[]{:S(2)}, u32[]{:S(2)}) collective-permute-start(bf16[144,384]{1,0:T(8,128)(2,1)S(1)} %bitcast_select_fusion.2.refs_0_), channel_id=1, source_target_pairs={{0,8},{8,0},{16,24},{24,16},{1,9},{9,1},{17,25},{25,17},{2,10},{10... | collective-permute-start | bytes 331784 | tf_op jit(solution)/shard_map/ppermute | solution.py:16
  47.7 5.3 %collective-permute-start.23 = (bf16[144,384]{1,0:T(8,128)(2,1)S(1)}, bf16[144,384]{1,0:T(8,128)(2,1)S(1)}, u32[]{:S(2)}, u32[]{:S(2)}) collective-permute-start(bf16[144,384]{1,0:T(8,128)(2,1)S(1)} %bitcast_select_fusion.2.refs_0_), channel_id=1, source_target_pairs={{0,4},{2,6},{4,0},{6,2},{1,5},{3,7},{5,1},{7,3},{8,12},{10,14},{12... | collective-permute-start | bytes 331784 | tf_op jit(solution)/shard_map/ppermute | solution.py:16
  53.1 6.2 %collective-permute-start.28 = (bf16[4,144,384]{2,1,0:T(8,128)(2,1)S(1)}, bf16[4,144,384]{2,1,0:T(8,128)(2,1)S(1)}, u32[]{:S(2)}, u32[]{:S(2)}) collective-permute-start(bf16[4,144,384]{2,1,0:T(8,128)(2,1)S(1)} %get-tuple-element.73.refs_0_), channel_id=1, source_target_pairs={{0,2},{2,0},{4,6},{6,4},{1,3},{3,1},{5,7},{7,5},{8,10},{10,8},{12,... | collective-permute-start | bytes 1327112 | tf_op jit(solution)/shard_map/ppermute | solution.py:16
  54.7 4.6 %collective-permute-start.29 = (bf16[144,384]{1,0:T(8,128)(2,1)S(1)}, bf16[144,384]{1,0:T(8,128)(2,1)S(1)}, u32[]{:S(2)}, u32[]{:S(2)}) collective-permute-start(bf16[144,384]{1,0:T(8,128)(2,1)S(1)} %get-tuple-element.74), channel_id=1, source_target_pairs={{0,8},{8,0},{16,24},{24,16},{1,9},{9,1},{17,25},{25,17},{2,10},{10... | collective-permute-start | bytes 331784 | tf_op jit(solution)/shard_map/ppermute | solution.py:16
  54.7 4.6 %collective-permute-start.30 = (bf16[144,384]{1,0:T(8,128)(2,1)S(1)}, bf16[144,384]{1,0:T(8,128)(2,1)S(1)}, u32[]{:S(2)}, u32[]{:S(2)}) collective-permute-start(bf16[144,384]{1,0:T(8,128)(2,1)S(1)} %get-tuple-element.75), channel_id=1, source_target_pairs={{0,4},{2,6},{4,0},{6,2},{1,5},{3,7},{5,1},{7,3},{8,12},{10,14},{12... | collective-permute-start | bytes 331784 | tf_op jit(solution)/shard_map/ppermute | solution.py:16
  55.5 7.8 %collective-permute-start.27 = (bf16[144,384]{1,0:T(8,128)(2,1)S(1)}, bf16[144,384]{1,0:T(8,128)(2,1)S(1)}, u32[]{:S(2)}, u32[]{:S(2)}) collective-permute-start(bf16[144,384]{1,0:T(8,128)(2,1)S(1)} %get-tuple-element.72), channel_id=1, source_target_pairs={{0,8},{8,0},{16,24},{24,16},{1,9},{9,1},{17,25},{25,17},{2,10},{10... | collective-permute-start | bytes 331784 | tf_op jit(solution)/shard_map/ppermute | solution.py:16
  60.2 6.1 %collective-permute-start.33 = (bf16[2,144,384]{2,1,0:T(8,128)(2,1)S(1)}, bf16[2,144,384]{2,1,0:T(8,128)(2,1)S(1)}, u32[]{:S(2)}, u32[]{:S(2)}) collective-permute-start(bf16[2,144,384]{2,1,0:T(8,128)(2,1)S(1)} %get-tuple-element.76.refs_2_), channel_id=1, source_target_pairs={{0,2},{2,0},{4,6},{6,4},{1,3},{3,1},{5,7},{7,5},{8,10},{10,8},{12,... | collective-permute-start | bytes 663560 | tf_op jit(solution)/shard_map/ppermute | solution.py:16
  (14 other events, 51.9 us)

commit v7 on v6

--- a/solution.py
+++ b/solution.py
@@ -359,7 +359,7 @@
         volume_body,
         [((4 * planes + 4, 3 * local_in // 2, plane), BF)],
         [],
-        0,
+        macs // 2,
         vol_n, vol_f, near, core_vf, x_n, x_f, cx_n, cx_f, ends,
     )[0]
     act_f, g_f = vmem_call(far_gate_body, [thin, thin], [], 0, own_f, recv_f, bias_row, cot, after=(g_n,))

time: 68.5 us -> 68 us (level)
  waiting for transfers between devices: 12.3 us -> 10.3 us
  starting transfers between devices: 37.5 us -> 38.8 us
    ppermute x34, waiting for transfers between devices: 12.3 us -> 10.3 us  [swap(): lax.ppermute(value, axis, [(i, i ^ bit) for i in range(lax.axis_size(axis...]
    ppermute x34, starting transfers between devices: 37.5 us -> 38.8 us  [swap(): lax.ppermute(value, axis, [(i, i ^ bit) for i in range(lax.axis_size(axis...]
  transfers between devices with their start and end apart: 34 -> 34, of which waited for: 11 -> 10; matrix products, arithmetic and copies ran while one was open for 1% -> 1% of each run, Pallas kernels for 18% -> 18%
where the time goes in v7:
time: 68 us; the launch traced here: 67.5 us
  starting transfers between devices  38.8 us (57%)
  Pallas kernels  14.1 us (21%)
  waiting for transfers between devices  10.3 us (15%)
  other arithmetic  1.76 us (3%)
  local copies, waits for them, and re-layouts  1.54 us (2%)
  between operations  0.9 us (1%)
    ppermute x34, starting transfers between devices, swap(): lax.ppermute(value, axis, [(i, i ^ bit) for i in range(lax.axis_size(axis...  38.8 us
    pallas_call x13, Pallas kernels, vmem_call(): pl.pallas_call(inner, out_shape=shapes, in_specs=[pl.BlockSpec(memory_spa...  11.5 us
    ppermute x34, waiting for transfers between devices, swap(): lax.ppermute(value, axis, [(i, i ^ bit) for i in range(lax.axis_size(axis...  10.3 us
    pallas_call x2, Pallas kernels, spread(): pl.pallas_call(inner, out_shape=[jax.ShapeDtypeStruct(shape, F32)] + [jax...  2.59 us
    unnamed x8, local copies, waits for them, and re-layouts  1.49 us
  transfers between devices with their start and end apart: 34, of which 10 were waited for; matrix products, arithmetic and copies ran while one was open for 1% of the time, Pallas kernels for 18%

profile of v7, /device:TPU:1, one launch (start us, length us, event | category | flops | bytes accessed | tf_op | source)
XLA Modules:
  0.0 67.5 jit_solution(11182122034371662454)
XLA Ops:
  1.8 2.7 %collective-permute-start.3 = (bf16[512,128]{1,0:T(8,128)(2,1)S(1)}, bf16[512,128]{1,0:T(8,128)(2,1)S(1)}, u32[]{:S(2)}, u32[]{:S(2)}) collective-permute-start(bf16[512,128]{1,0:T(8,128)(2,1)S(1)} %bitcast.22), channel_id=1, source_target_pairs={{0,4},{2,6},{4,0},{6,2},{1,5},{3,7},{5,1},{7,3},{8,12},{10,14},{12... | collective-permute-start | bytes 393224 | tf_op jit(solution)/shard_map/ppermute | solution.py:16
  4.4 1.5 %copy-done = bf16[3,3,3,128,256]{4,3,2,1,0:T(8,128)(2,1)S(1)} copy-done((bf16[3,3,3,128,256]{4,3,2,1,0:T(8,128)(2,1)S(1)}, bf16[3,3,3,128,256]{4,3,2,1,0:T(8,128)(2,1)}, u32[]{:S(2)}) %copy-start) | copy-done | bytes 1769496
  5.9 1.5 %shard_map.75 = (f32[512,128]{1,0:T(8,128)S(1)}, bf16[512,128]{1,0:T(8,128)(2,1)S(1)}, bf16[2,544,384]{2,1,0:T(8,128)(2,1)S(1)}, bf16[3,1152,256]{2,1,0:T(8,128)(2,1)S(1)}, f32[8,128]{1,0:T(8,128)S(1)}) custom-call(bf16[512,128]{1,0:T(8,128)(2,1)S(1)} %bitcast.27, bf16[512,128]{1,0:T(8,128)(2,1)S(1)} %bitcast.23, ...), custom_call_target="tpu_custom_call" | custom-call | flops 2811939328 | bytes 1048576 | tf_op jit(solution)/shard_map/pallas_call | solution.py:33
  9.0 1.5 %collective-permute-start.1 = (bf16[512,128]{1,0:T(8,128)(2,1)S(1)}, bf16[512,128]{1,0:T(8,128)(2,1)S(1)}, u32[]{:S(2)}, u32[]{:S(2)}) collective-permute-start(bf16[512,128]{1,0:T(8,128)(2,1)S(1)} %get-tuple-element.43), channel_id=1, source_target_pairs={{0,1},{1,0},{2,3},{3,2},{4,5},{5,4},{6,7},{7,6},{8,9},{9,8},{10,11... | collective-permute-start | bytes 393224 | tf_op jit(solution)/shard_map/ppermute | solution.py:16
  12.7 1.4 %collective-permute-done.1.refs_1_ = bf16[512,128]{1,0:T(8,128)(2,1)S(1)} collective-permute-done((bf16[512,128]{1,0:T(8,128)(2,1)S(1)}, bf16[512,128]{1,0:T(8,128)(2,1)S(1)}, u32[]{:S(2)}, u32[]{:S(2)}) %collective-permute-start.1) | collective-permute-done | bytes 131104 | tf_op jit(solution)/shard_map/ppermute | solution.py:16
  14.2 1.5 %collective-permute-start.2 = (bf16[512,128]{1,0:T(8,128)(2,1)S(1)}, bf16[512,128]{1,0:T(8,128)(2,1)S(1)}, u32[]{:S(2)}, u32[]{:S(2)}) collective-permute-start(bf16[512,128]{1,0:T(8,128)(2,1)S(1)} %get-tuple-element.44.refs_4_), channel_id=1, source_target_pairs={{0,1},{1,0},{2,3},{3,2},{4,5},{5,4},{6,7},{7,6},{8,9},{9,8},{10,11... | collective-permute-start | bytes 393224 | tf_op jit(solution)/shard_map/ppermute | solution.py:16
  15.8 1.6 %collective-permute-start.9 = (bf16[512,128]{1,0:T(8,128)(2,1)S(1)}, bf16[512,128]{1,0:T(8,128)(2,1)S(1)}, u32[]{:S(2)}, u32[]{:S(2)}) collective-permute-start(bf16[512,128]{1,0:T(8,128)(2,1)S(1)} %bitcast.24), channel_id=1, source_target_pairs={{0,2},{2,0},{4,6},{6,4},{1,3},{3,1},{5,7},{7,5},{8,10},{10,8},{12,... | collective-permute-start | bytes 393224 | tf_op jit(solution)/shard_map/ppermute | solution.py:16
  18.9 1.5 %collective-permute-start.12 = (bf16[512,128]{1,0:T(8,128)(2,1)S(1)}, bf16[512,128]{1,0:T(8,128)(2,1)S(1)}, u32[]{:S(2)}, u32[]{:S(2)}) collective-permute-start(bf16[512,128]{1,0:T(8,128)(2,1)S(1)} %get-tuple-element.82.refs_1_), channel_id=1, source_target_pairs={{0,4},{2,6},{4,0},{6,2},{1,5},{3,7},{5,1},{7,3},{8,12},{10,14},{12... | collective-permute-start | bytes 393224 | tf_op jit(solution)/shard_map/ppermute | solution.py:16
  20.4 2.0 %collective-permute-start.7 = (bf16[512,128]{1,0:T(8,128)(2,1)S(1)}, bf16[512,128]{1,0:T(8,128)(2,1)S(1)}, u32[]{:S(2)}, u32[]{:S(2)}) collective-permute-start(bf16[512,128]{1,0:T(8,128)(2,1)S(1)} %get-tuple-element.83.refs_1_.refs_0_), channel_id=1, source_target_pairs={{0,2},{2,0},{4,6},{6,4},{1,3},{3,1},{5,7},{7,5},{8,10},{10,8},{12,... | collective-permute-start | bytes 393224 | tf_op jit(solution)/shard_map/ppermute | solution.py:16
  26.5 1.6 %shard_map.80 = (f32[3,192,384]{2,1,0:T(8,128)S(1)}, f32[8,384]{1,0:T(8,128)S(1)}) custom-call(bf16[12,192,512]{2,1,0:T(8,128)(2,1)S(1)} %shard_map.79.refs_0_, bf16[512,128]{1,0:T(8,128)(2,1)S(1)} %get-tuple-element.83.refs_1_.refs_0_, bf16[512,128]{1,0:T(8,128)(2,1)S(1)} %collective-permute-done.7.refs_2_.refs_4_, ...), custom_call_target="tpu_custom_call" | custom-call | flops 4623878656 | bytes 1048576 | tf_op jit(solution)/shard_map/pallas_call | solution.py:33
  31.4 1.4 %collective-permute-start.17 = (bf16[144,384]{1,0:T(8,128)(2,1)S(1)}, bf16[144,384]{1,0:T(8,128)(2,1)S(1)}, u32[]{:S(2)}, u32[]{:S(2)}) collective-permute-start(bf16[144,384]{1,0:T(8,128)(2,1)S(1)} %get-tuple-element.61), channel_id=1, source_target_pairs={{0,8},{8,0},{16,24},{24,16},{1,9},{9,1},{17,25},{25,17},{2,10},{10... | collective-permute-start | bytes 331784 | tf_op jit(solution)/shard_map/ppermute | solution.py:16
  33.4 2.3 %collective-permute-start.20 = (f32[8,384]{1,0:T(8,128)S(1)}, f32[8,384]{1,0:T(8,128)S(1)}, u32[]{:S(2)}, u32[]{:S(2)}) collective-permute-start(f32[8,384]{1,0:T(8,128)S(1)} %get-tuple-element.68), channel_id=1, source_target_pairs={{0,16},{8,24},{16,0},{24,8},{1,17},{9,25},{17,1},{25,9},{2,18},{10... | collective-permute-start | bytes 36872 | tf_op jit(solution)/shard_map/ppermute | solution.py:16
  38.2 2.2 %collective-permute-done.18.refs_10_ = bf16[512,128]{1,0:T(8,128)(2,1)S(1)} collective-permute-done((bf16[512,128]{1,0:T(8,128)(2,1)S(1)}, bf16[512,128]{1,0:T(8,128)(2,1)S(1)}, u32[]{:S(2)}, u32[]{:S(2)}) %collective-permute-start.18) | collective-permute-done | bytes 131104 | tf_op jit(solution)/shard_map/ppermute | solution.py:16
  40.4 1.4 %collective-permute-start.19 = (bf16[512,128]{1,0:T(8,128)(2,1)S(1)}, bf16[512,128]{1,0:T(8,128)(2,1)S(1)}, u32[]{:S(2)}, u32[]{:S(2)}) collective-permute-start(bf16[512,128]{1,0:T(8,128)(2,1)S(1)} %collective-permute-done.18.refs_10_), channel_id=1, source_target_pairs={{0,2},{2,0},{4,6},{6,4},{1,3},{3,1},{5,7},{7,5},{8,10},{10,8},{12,... | collective-permute-start | bytes 393224 | tf_op jit(solution)/shard_map/ppermute | solution.py:16
  41.8 2.7 %shard_map.84 = (bf16[512,128]{1,0:T(8,128)(2,1)S(1)}, f32[512,128]{1,0:T(8,128)S(1)}, bf16[2,512,128]{2,1,0:T(8,128)(2,1)}, f32[8,384]{1,0:T(8,128)S(1)}) custom-call(bf16[512,128]{1,0:T(8,128)(2,1)S(1)} %get-tuple-element.83.refs_1_.refs_0_, bf16[512,128]{1,0:T(8,128)(2,1)S(1)} %get-tuple-element.82.refs_1_, ...), custom_call_target="tpu_custom_call" | custom-call | flops 4623878656 | bytes 1048576 | tf_op jit(solution)/shard_map/pallas_call | solution.py:33
  44.8 2.0 %collective-permute-start.24 = (bf16[144,384]{1,0:T(8,128)(2,1)S(1)}, bf16[144,384]{1,0:T(8,128)(2,1)S(1)}, u32[]{:S(2)}, u32[]{:S(2)}) collective-permute-start(bf16[144,384]{1,0:T(8,128)(2,1)S(1)} %bitcast_select_fusion.2.refs_0_), channel_id=1, source_target_pairs={{0,8},{8,0},{16,24},{24,16},{1,9},{9,1},{17,25},{25,17},{2,10},{10... | collective-permute-start | bytes 331784 | tf_op jit(solution)/shard_map/ppermute | solution.py:16
  47.9 1.6 %shard_map.85 = (bf16[2,512,128]{2,1,0:T(8,128)(2,1)}, f32[8,384]{1,0:T(8,128)S(1)}) custom-call(bf16[512,128]{1,0:T(8,128)(2,1)S(1)} %collective-permute-done.16.refs_1_.refs_0_, bf16[512,128]{1,0:T(8,128)(2,1)S(1)} %collective-permute-done.19.refs_1_, bf16[27,128,256]{2,1,0:T(8,128)(2,1)S(1)} %bitcast.32, f32[512,128]{1,0:T(8,128)S(1)} %get-tuple-element.64.refs_3_, ...), custom_call_target="tpu_custom_call" | custom-call | flops 1000000000 | bytes 1048576 | tf_op jit(solution)/shard_map/pallas_call | solution.py:33
  49.5 1.4 %collective-permute-done.26.refs_4_ = f32[8,384]{1,0:T(8,128)S(1)} collective-permute-done((f32[8,384]{1,0:T(8,128)S(1)}, f32[8,384]{1,0:T(8,128)S(1)}, u32[]{:S(2)}, u32[]{:S(2)}) %collective-permute-start.26) | collective-permute-done | bytes 12320 | tf_op jit(solution)/shard_map/ppermute | solution.py:16
  51.9 2.3 %collective-permute-start.28 = (bf16[4,144,384]{2,1,0:T(8,128)(2,1)S(1)}, bf16[4,144,384]{2,1,0:T(8,128)(2,1)S(1)}, u32[]{:S(2)}, u32[]{:S(2)}) collective-permute-start(bf16[4,144,384]{2,1,0:T(8,128)(2,1)S(1)} %get-tuple-element.73.refs_0_), channel_id=1, source_target_pairs={{0,2},{2,0},{4,6},{6,4},{1,3},{3,1},{5,7},{7,5},{8,10},{10,8},{12,... | collective-permute-start | bytes 1327112 | tf_op jit(solution)/shard_map/ppermute | solution.py:16
  54.9 1.5 %collective-permute-start.27 = (bf16[144,384]{1,0:T(8,128)(2,1)S(1)}, bf16[144,384]{1,0:T(8,128)(2,1)S(1)}, u32[]{:S(2)}, u32[]{:S(2)}) collective-permute-start(bf16[144,384]{1,0:T(8,128)(2,1)S(1)} %get-tuple-element.72), channel_id=1, source_target_pairs={{0,8},{8,0},{16,24},{24,16},{1,9},{9,1},{17,25},{25,17},{2,10},{10... | collective-permute-start | bytes 331784 | tf_op jit(solution)/shard_map/ppermute | solution.py:16
  56.4 2.4 %collective-permute-done.29.refs_1_ = bf16[144,384]{1,0:T(8,128)(2,1)S(1)} collective-permute-done((bf16[144,384]{1,0:T(8,128)(2,1)S(1)}, bf16[144,384]{1,0:T(8,128)(2,1)S(1)}, u32[]{:S(2)}, u32[]{:S(2)}) %collective-permute-start.29) | collective-permute-done | bytes 110624 | tf_op jit(solution)/shard_map/ppermute | solution.py:16
  59.7 1.6 %collective-permute-start.33 = (bf16[2,144,384]{2,1,0:T(8,128)(2,1)S(1)}, bf16[2,144,384]{2,1,0:T(8,128)(2,1)S(1)}, u32[]{:S(2)}, u32[]{:S(2)}) collective-permute-start(bf16[2,144,384]{2,1,0:T(8,128)(2,1)S(1)} %get-tuple-element.76.refs_2_), channel_id=1, source_target_pairs={{0,2},{2,0},{4,6},{6,4},{1,3},{3,1},{5,7},{7,5},{8,10},{10,8},{12,... | collective-permute-start | bytes 663560 | tf_op jit(solution)/shard_map/ppermute | solution.py:16
  61.2 1.4 %shard_map.88 = (f32[27,128,256]{2,1,0:T(8,128)}, f32[8,384]{1,0:T(8,128)S(1)}) custom-call(bf16[4,144,384]{2,1,0:T(8,128)(2,1)S(1)} %get-tuple-element.73.refs_0_, bf16[4,144,384]{2,1,0:T(8,128)(2,1)S(1)} %collective-permute-done.28.refs_0_.refs_1_, bf16[2,144,384]{2,1,0:T(8,128)(2,1)S(1)} %get-tuple-element.76.refs_2_), custom_call_target="tpu_custom_call" | custom-call | flops 1 | bytes 1 | tf_op jit(solution)/shard_map/pallas_call | solution.py:256
  62.8 2.4 %collective-permute-start.32 = (bf16[288,384]{1,0:T(8,128)(2,1)S(1)}, bf16[288,384]{1,0:T(8,128)(2,1)S(1)}, u32[]{:S(2)}, u32[]{:S(2)}) collective-permute-start(bf16[288,384]{1,0:T(8,128)(2,1)S(1)} %pad_maximum_fusion.refs_0_), channel_id=1, source_target_pairs={{0,2},{2,0},{4,6},{6,4},{1,3},{3,1},{5,7},{7,5},{8,10},{10,8},{12,... | collective-permute-start | bytes 663560 | tf_op jit(solution)/shard_map/ppermute | solution.py:16
  (86 shorter events, 23.2 us)
Async XLA Ops:
  1.8 6.4 %collective-permute-start.3 = (bf16[512,128]{1,0:T(8,128)(2,1)S(1)}, bf16[512,128]{1,0:T(8,128)(2,1)S(1)}, u32[]{:S(2)}, u32[]{:S(2)}) collective-permute-start(bf16[512,128]{1,0:T(8,128)(2,1)S(1)} %bitcast.22), channel_id=1, source_target_pairs={{0,4},{2,6},{4,0},{6,2},{1,5},{3,7},{5,1},{7,3},{8,12},{10,14},{12... | collective-permute-start | bytes 393224 | tf_op jit(solution)/shard_map/ppermute | solution.py:16
  9.0 5.1 %collective-permute-start.1 = (bf16[512,128]{1,0:T(8,128)(2,1)S(1)}, bf16[512,128]{1,0:T(8,128)(2,1)S(1)}, u32[]{:S(2)}, u32[]{:S(2)}) collective-permute-start(bf16[512,128]{1,0:T(8,128)(2,1)S(1)} %get-tuple-element.43), channel_id=1, source_target_pairs={{0,1},{1,0},{2,3},{3,2},{4,5},{5,4},{6,7},{7,6},{8,9},{9,8},{10,11... | collective-permute-start | bytes 393224 | tf_op jit(solution)/shard_map/ppermute | solution.py:16
  11.7 6.9 %collective-permute-start.5 = (bf16[512,128]{1,0:T(8,128)(2,1)S(1)}, bf16[512,128]{1,0:T(8,128)(2,1)S(1)}, u32[]{:S(2)}, u32[]{:S(2)}) collective-permute-start(bf16[512,128]{1,0:T(8,128)(2,1)S(1)} %get-tuple-element.49), channel_id=1, source_target_pairs={{0,1},{1,0},{2,3},{3,2},{4,5},{5,4},{6,7},{7,6},{8,9},{9,8},{10,11... | collective-permute-start | bytes 393224 | tf_op jit(solution)/shard_map/ppermute | solution.py:16
  14.2 4.7 %collective-permute-start.2 = (bf16[512,128]{1,0:T(8,128)(2,1)S(1)}, bf16[512,128]{1,0:T(8,128)(2,1)S(1)}, u32[]{:S(2)}, u32[]{:S(2)}) collective-permute-start(bf16[512,128]{1,0:T(8,128)(2,1)S(1)} %get-tuple-element.44.refs_4_), channel_id=1, source_target_pairs={{0,1},{1,0},{2,3},{3,2},{4,5},{5,4},{6,7},{7,6},{8,9},{9,8},{10,11... | collective-permute-start | bytes 393224 | tf_op jit(solution)/shard_map/ppermute | solution.py:16
  15.8 9.2 %collective-permute-start.9 = (bf16[512,128]{1,0:T(8,128)(2,1)S(1)}, bf16[512,128]{1,0:T(8,128)(2,1)S(1)}, u32[]{:S(2)}, u32[]{:S(2)}) collective-permute-start(bf16[512,128]{1,0:T(8,128)(2,1)S(1)} %bitcast.24), channel_id=1, source_target_pairs={{0,2},{2,0},{4,6},{6,4},{1,3},{3,1},{5,7},{7,5},{8,10},{10,8},{12,... | collective-permute-start | bytes 393224 | tf_op jit(solution)/shard_map/ppermute | solution.py:16
  17.3 5.1 %collective-permute-start.10 = (bf16[512,128]{1,0:T(8,128)(2,1)S(1)}, bf16[512,128]{1,0:T(8,128)(2,1)S(1)}, u32[]{:S(2)}, u32[]{:S(2)}) collective-permute-start(bf16[512,128]{1,0:T(8,128)(2,1)S(1)} %get-tuple-element.53), channel_id=1, source_target_pairs={{0,4},{2,6},{4,0},{6,2},{1,5},{3,7},{5,1},{7,3},{8,12},{10,14},{12... | collective-permute-start | bytes 393224 | tf_op jit(solution)/shard_map/ppermute | solution.py:16
  18.7 4.9 %collective-permute-start.6 = (bf16[512,128]{1,0:T(8,128)(2,1)S(1)}, bf16[512,128]{1,0:T(8,128)(2,1)S(1)}, u32[]{:S(2)}, u32[]{:S(2)}) collective-permute-start(bf16[512,128]{1,0:T(8,128)(2,1)S(1)} %get-tuple-element.50), channel_id=1, source_target_pairs={{0,1},{1,0},{2,3},{3,2},{4,5},{5,4},{6,7},{7,6},{8,9},{9,8},{10,11... | collective-permute-start | bytes 393224 | tf_op jit(solution)/shard_map/ppermute | solution.py:16
  18.9 6.4 %collective-permute-start.12 = (bf16[512,128]{1,0:T(8,128)(2,1)S(1)}, bf16[512,128]{1,0:T(8,128)(2,1)S(1)}, u32[]{:S(2)}, u32[]{:S(2)}) collective-permute-start(bf16[512,128]{1,0:T(8,128)(2,1)S(1)} %get-tuple-element.82.refs_1_), channel_id=1, source_target_pairs={{0,4},{2,6},{4,0},{6,2},{1,5},{3,7},{5,1},{7,3},{8,12},{10,14},{12... | collective-permute-start | bytes 393224 | tf_op jit(solution)/shard_map/ppermute | solution.py:16
  20.4 6.1 %collective-permute-start.7 = (bf16[512,128]{1,0:T(8,128)(2,1)S(1)}, bf16[512,128]{1,0:T(8,128)(2,1)S(1)}, u32[]{:S(2)}, u32[]{:S(2)}) collective-permute-start(bf16[512,128]{1,0:T(8,128)(2,1)S(1)} %get-tuple-element.83.refs_1_.refs_0_), channel_id=1, source_target_pairs={{0,2},{2,0},{4,6},{6,4},{1,3},{3,1},{5,7},{7,5},{8,10},{10,8},{12,... | collective-permute-start | bytes 393224 | tf_op jit(solution)/shard_map/ppermute | solution.py:16
  23.7 5.5 %collective-permute-start.15 = (bf16[512,128]{1,0:T(8,128)(2,1)S(1)}, bf16[512,128]{1,0:T(8,128)(2,1)S(1)}, u32[]{:S(2)}, u32[]{:S(2)}) collective-permute-start(bf16[512,128]{1,0:T(8,128)(2,1)S(1)} %get-tuple-element.80.refs_3_), channel_id=1, source_target_pairs={{0,4},{2,6},{4,0},{6,2},{1,5},{3,7},{5,1},{7,3},{8,12},{10,14},{12... | collective-permute-start | bytes 393224 | tf_op jit(solution)/shard_map/ppermute | solution.py:16
  31.4 5.6 %collective-permute-start.17 = (bf16[144,384]{1,0:T(8,128)(2,1)S(1)}, bf16[144,384]{1,0:T(8,128)(2,1)S(1)}, u32[]{:S(2)}, u32[]{:S(2)}) collective-permute-start(bf16[144,384]{1,0:T(8,128)(2,1)S(1)} %get-tuple-element.61), channel_id=1, source_target_pairs={{0,8},{8,0},{16,24},{24,16},{1,9},{9,1},{17,25},{25,17},{2,10},{10... | collective-permute-start | bytes 331784 | tf_op jit(solution)/shard_map/ppermute | solution.py:16
  32.8 9.0 %collective-permute-start.8 = (bf16[512,128]{1,0:T(8,128)(2,1)S(1)}, bf16[512,128]{1,0:T(8,128)(2,1)S(1)}, u32[]{:S(2)}, u32[]{:S(2)}) collective-permute-start(bf16[512,128]{1,0:T(8,128)(2,1)S(1)} %get-tuple-element.82.refs_1_), channel_id=1, source_target_pairs={{0,2},{2,0},{4,6},{6,4},{1,3},{3,1},{5,7},{7,5},{8,10},{10,8},{12,... | collective-permute-start | bytes 393224 | tf_op jit(solution)/shard_map/ppermute | solution.py:16
  33.4 11.1 %collective-permute-start.20 = (f32[8,384]{1,0:T(8,128)S(1)}, f32[8,384]{1,0:T(8,128)S(1)}, u32[]{:S(2)}, u32[]{:S(2)}) collective-permute-start(f32[8,384]{1,0:T(8,128)S(1)} %get-tuple-element.68), channel_id=1, source_target_pairs={{0,16},{8,24},{16,0},{24,8},{1,17},{9,25},{17,1},{25,9},{2,18},{10... | collective-permute-start | bytes 36872 | tf_op jit(solution)/shard_map/ppermute | solution.py:16
  35.7 8.8 %collective-permute-start.21 = (bf16[144,384]{1,0:T(8,128)(2,1)S(1)}, bf16[144,384]{1,0:T(8,128)(2,1)S(1)}, u32[]{:S(2)}, u32[]{:S(2)}) collective-permute-start(bf16[144,384]{1,0:T(8,128)(2,1)S(1)} %get-tuple-element.70), channel_id=1, source_target_pairs={{0,8},{8,0},{16,24},{24,16},{1,9},{9,1},{17,25},{25,17},{2,10},{10... | collective-permute-start | bytes 331784 | tf_op jit(solution)/shard_map/ppermute | solution.py:16
  37.1 7.5 %collective-permute-start.22 = (bf16[144,384]{1,0:T(8,128)(2,1)S(1)}, bf16[144,384]{1,0:T(8,128)(2,1)S(1)}, u32[]{:S(2)}, u32[]{:S(2)}) collective-permute-start(bf16[144,384]{1,0:T(8,128)(2,1)S(1)} %add_convert_fusion.refs_9_), channel_id=1, source_target_pairs={{0,16},{8,24},{16,0},{24,8},{1,17},{9,25},{17,1},{25,9},{2,18},{10... | collective-permute-start | bytes 331784 | tf_op jit(solution)/shard_map/ppermute | solution.py:16
  40.4 7.5 %collective-permute-start.19 = (bf16[512,128]{1,0:T(8,128)(2,1)S(1)}, bf16[512,128]{1,0:T(8,128)(2,1)S(1)}, u32[]{:S(2)}, u32[]{:S(2)}) collective-permute-start(bf16[512,128]{1,0:T(8,128)(2,1)S(1)} %collective-permute-done.18.refs_10_), channel_id=1, source_target_pairs={{0,2},{2,0},{4,6},{6,4},{1,3},{3,1},{5,7},{7,5},{8,10},{10,8},{12,... | collective-permute-start | bytes 393224 | tf_op jit(solution)/shard_map/ppermute | solution.py:16
  44.6 7.1 %collective-permute-start.25 = (bf16[144,384]{1,0:T(8,128)(2,1)S(1)}, bf16[144,384]{1,0:T(8,128)(2,1)S(1)}, u32[]{:S(2)}, u32[]{:S(2)}) collective-permute-start(bf16[144,384]{1,0:T(8,128)(2,1)S(1)} %bitcast_select_fusion.2.refs_0_), channel_id=1, source_target_pairs={{0,16},{8,24},{16,0},{24,8},{1,17},{9,25},{17,1},{25,9},{2,18},{10... | collective-permute-start | bytes 331784 | tf_op jit(solution)/shard_map/ppermute | solution.py:16
  44.8 7.0 %collective-permute-start.24 = (bf16[144,384]{1,0:T(8,128)(2,1)S(1)}, bf16[144,384]{1,0:T(8,128)(2,1)S(1)}, u32[]{:S(2)}, u32[]{:S(2)}) collective-permute-start(bf16[144,384]{1,0:T(8,128)(2,1)S(1)} %bitcast_select_fusion.2.refs_0_), channel_id=1, source_target_pairs={{0,8},{8,0},{16,24},{24,16},{1,9},{9,1},{17,25},{25,17},{2,10},{10... | collective-permute-start | bytes 331784 | tf_op jit(solution)/shard_map/ppermute | solution.py:16
  46.8 5.0 %collective-permute-start.23 = (bf16[144,384]{1,0:T(8,128)(2,1)S(1)}, bf16[144,384]{1,0:T(8,128)(2,1)S(1)}, u32[]{:S(2)}, u32[]{:S(2)}) collective-permute-start(bf16[144,384]{1,0:T(8,128)(2,1)S(1)} %bitcast_select_fusion.2.refs_0_), channel_id=1, source_target_pairs={{0,4},{2,6},{4,0},{6,2},{1,5},{3,7},{5,1},{7,3},{8,12},{10,14},{12... | collective-permute-start | bytes 331784 | tf_op jit(solution)/shard_map/ppermute | solution.py:16
  51.9 6.9 %collective-permute-start.28 = (bf16[4,144,384]{2,1,0:T(8,128)(2,1)S(1)}, bf16[4,144,384]{2,1,0:T(8,128)(2,1)S(1)}, u32[]{:S(2)}, u32[]{:S(2)}) collective-permute-start(bf16[4,144,384]{2,1,0:T(8,128)(2,1)S(1)} %get-tuple-element.73.refs_0_), channel_id=1, source_target_pairs={{0,2},{2,0},{4,6},{6,4},{1,3},{3,1},{5,7},{7,5},{8,10},{10,8},{12,... | collective-permute-start | bytes 1327112 | tf_op jit(solution)/shard_map/ppermute | solution.py:16
  54.2 4.6 %collective-permute-start.29 = (bf16[144,384]{1,0:T(8,128)(2,1)S(1)}, bf16[144,384]{1,0:T(8,128)(2,1)S(1)}, u32[]{:S(2)}, u32[]{:S(2)}) collective-permute-start(bf16[144,384]{1,0:T(8,128)(2,1)S(1)} %get-tuple-element.74), channel_id=1, source_target_pairs={{0,8},{8,0},{16,24},{24,16},{1,9},{9,1},{17,25},{25,17},{2,10},{10... | collective-permute-start | bytes 331784 | tf_op jit(solution)/shard_map/ppermute | solution.py:16
  54.2 4.6 %collective-permute-start.30 = (bf16[144,384]{1,0:T(8,128)(2,1)S(1)}, bf16[144,384]{1,0:T(8,128)(2,1)S(1)}, u32[]{:S(2)}, u32[]{:S(2)}) collective-permute-start(bf16[144,384]{1,0:T(8,128)(2,1)S(1)} %get-tuple-element.75), channel_id=1, source_target_pairs={{0,4},{2,6},{4,0},{6,2},{1,5},{3,7},{5,1},{7,3},{8,12},{10,14},{12... | collective-permute-start | bytes 331784 | tf_op jit(solution)/shard_map/ppermute | solution.py:16
  54.9 7.8 %collective-permute-start.27 = (bf16[144,384]{1,0:T(8,128)(2,1)S(1)}, bf16[144,384]{1,0:T(8,128)(2,1)S(1)}, u32[]{:S(2)}, u32[]{:S(2)}) collective-permute-start(bf16[144,384]{1,0:T(8,128)(2,1)S(1)} %get-tuple-element.72), channel_id=1, source_target_pairs={{0,8},{8,0},{16,24},{24,16},{1,9},{9,1},{17,25},{25,17},{2,10},{10... | collective-permute-start | bytes 331784 | tf_op jit(solution)/shard_map/ppermute | solution.py:16
  59.7 6.1 %collective-permute-start.33 = (bf16[2,144,384]{2,1,0:T(8,128)(2,1)S(1)}, bf16[2,144,384]{2,1,0:T(8,128)(2,1)S(1)}, u32[]{:S(2)}, u32[]{:S(2)}) collective-permute-start(bf16[2,144,384]{2,1,0:T(8,128)(2,1)S(1)} %get-tuple-element.76.refs_2_), channel_id=1, source_target_pairs={{0,2},{2,0},{4,6},{6,4},{1,3},{3,1},{5,7},{7,5},{8,10},{10,8},{12,... | collective-permute-start | bytes 663560 | tf_op jit(solution)/shard_map/ppermute | solution.py:16
  (14 other events, 49.3 us)
